TPU v7x, 128 devices: a whole 4x4x4 slice. The times are simulated.
128 devices in a mesh: dp: 16 (over y_hi, z, core), tensor: 8 (over y_lo, x).
Axes of the slice: x: 4, y: 4 (y_hi: 2, y_lo: 2; y = y_hi * 2 + y_lo), z: 4, core: 2. Of those that a mesh axis runs over, the one named last changes fastest.
Arguments:
- weight: float32 [1024, 15872], P(None, 'tensor'), may hold values from -3 to 3
- grad_parts: float32 [16, 1024, 15872], P('dp', None, 'tensor'), may hold values from -6 to 6
- m_codes: int32 [7936, 2048], P(('dp', 'tensor')), may hold values from 0 to 255
- v_codes: int32 [7936, 2048], P(('dp', 'tensor')), may hold values from 0 to 255
- m_absmax: float32 [7936], P(('dp', 'tensor')), may hold values from 0.1 to 1
- v_absmax: float32 [7936], P(('dp', 'tensor')), may hold values from 0.001 to 0.01
- code_m: float32 [256], replicated, may hold values from -1 to 1
- code_v: float32 [256], replicated, may hold values from 0.05 to 1
- step: int32 [1], replicated, may hold values from 1 to 64
Outputs:
- new_weight: float32 [1024, 15872], P(None, 'tensor')
- m_scaled: bfloat16 [7936, 2048], P(('dp', 'tensor'))
- v_scaled: bfloat16 [7936, 2048], P(('dp', 'tensor'))
- m_absmax_new: float32 [7936], P(('dp', 'tensor'))
- v_absmax_new: float32 [7936], P(('dp', 'tensor'))
All inputs are finite; a program needn't handle non-finite values. Where the computation divides by a largest or mean magnitude, that divisor is 1e-20 or more.
Results may differ from a plain program's by a relative error of at most 0.001.
Values sent between devices are 32-bit elements; how exact they have to be, the bound alone decides.
No kernel may reach another device: no remote copies, remote signals or barrier semaphores. Data moves between devices by JAX's collectives and lax.ppermute only.
A program may use at most 128 MiB of HBM per device.

v0:
```python
import jax
import jax.numpy as jnp
from jax import lax
from jax.sharding import PartitionSpec as P

QKV = 15872
BLOCK = 2048
ROWS_DEV = 8


beta_one = 0.9
beta_two = 0.999
adam_eps = 1e-08
learn_rate = 0.02
decay_rate = 0.1
scale_eps = 1e-06


def lookup(codes, table):
    high = codes // 16
    low = codes - high * 16
    digits = lax.broadcasted_iota(jnp.int32, (16, 1, 1), 0)
    low_hits = (low[None, :, :] == digits).astype(jnp.float32)
    grid = table.reshape(16, 16)
    picked = jnp.einsum("jk,krb->jrb", grid, low_hits, precision=lax.Precision.HIGHEST)
    high_hits = high[None, :, :] == digits
    return jnp.sum(jnp.where(high_hits, picked, jnp.float32(0.0)), axis=0)


def shards(weight, grad_parts, m_codes, v_codes, m_absmax, v_absmax, code_m, code_v, step):
    partial_value = grad_parts[0]
    summed = lax.psum_scatter(partial_value, "dp", scatter_dimension=0, tiled=True)
    rows = lax.all_to_all(summed, "tensor", split_axis=0, concat_axis=1, tiled=True)
    grad = rows.reshape(-1, BLOCK)
    m_old = lookup(m_codes, code_m) * m_absmax[:, None]
    v_old = lookup(v_codes, code_v) * v_absmax[:, None]
    m_new = beta_one * m_old + (1.0 - beta_one) * grad
    v_new = beta_two * v_old + (1.0 - beta_two) * grad * grad
    count = step[0].astype(jnp.float32)
    fix_one = 1.0 - jnp.power(jnp.float32(beta_one), count)
    fix_two = 1.0 - jnp.power(jnp.float32(beta_two), count)
    update = (m_new / fix_one / (jnp.sqrt(v_new / fix_two) + adam_eps)).reshape(ROWS_DEV, QKV)
    columns = lax.all_to_all(update, "tensor", split_axis=1, concat_axis=0, tiled=True)
    mine = lax.all_gather(columns, "dp", axis=0, tiled=True)
    new_weight = weight - learn_rate * (mine + decay_rate * weight)
    m_absmax_new = jnp.max(jnp.abs(m_new), axis=1)
    v_absmax_new = jnp.max(v_new, axis=1)
    m_scaled = (m_new / (m_absmax_new[:, None] + scale_eps)).astype(jnp.bfloat16)
    v_scaled = (v_new / (v_absmax_new[:, None] + scale_eps)).astype(jnp.bfloat16)
    return (new_weight, m_scaled, v_scaled, m_absmax_new, v_absmax_new)


def solution(mesh):
    in_specs = (
        P(None, "tensor"),
        P("dp", None, "tensor"),
        P(("dp", "tensor"), None),
        P(("dp", "tensor"), None),
        P(("dp", "tensor")),
        P(("dp", "tensor")),
        P(),
        P(),
        P(),
    )
    out_specs = (
        P(None, "tensor"),
        P(("dp", "tensor"), None),
        P(("dp", "tensor"), None),
        P(("dp", "tensor")),
        P(("dp", "tensor")),
    )
    return jax.shard_map(shards, mesh=mesh, in_specs=in_specs, out_specs=out_specs, check_vma=False)
```

profile of v0, /device:TPU:1, one launch (start us, length us, event | category | flops | bytes accessed | tf_op | source)
XLA Modules:
  0.0 254.9 jit_solution(13629513754558413037)
XLA Ops:
  7.2 0.0 reduce-scatter.2.cloned.1.call-start
  7.2 9.1 %copy.26 = f32[1,1024,1984]{2,1,0:T(8,128)} copy(f32[1,1024,1984]{1,2,0:T(8,128)} %param.10) | data formatting | bytes 16252928 | tf_op args[1]
  16.4 0.0 copy-start.5
  16.4 0.0 copy-start
  16.4 0.0 copy-start.1
  16.4 0.0 reduce-scatter.2.cloned.1.call-update
  16.4 0.6 copy-done.5
  17.0 0.0 copy-start.6
  17.0 0.1 reshape.69
  17.1 0.3 copy-done
  17.4 0.3 multiply_subtract_fusion.1
  17.7 0.0 copy-done.1
  17.8 0.3 multiply_subtract_fusion.2
  18.1 103.2 %reduce-scatter.2.cloned.1.call-done = f32[64,1984]{1,0:T(8,128)} async-done(((f32[1024,1984]{1,0:T(8,128)}), f32[64,1984]{1,0:T(8,128)}) %reduce-scatter.2.cloned.1.call-update) | async-done | bytes 507920 | tf_op jit(solution)/shard_map/reduce_scatter | solution.py:32
  121.3 4.0 %all-to-all-start = ((f32[8,8,1984]{2,1,0:T(8,128)}), f32[8,8,1984]{2,1,0:T(8,128)S(1)}, u32[]{:S(2)}, u32[]{:S(2)}) async-start(f32[8,8,1984]{2,1,0:T(8,128)} %bitcast.25), calls=%async_computation.1 | async-start | bytes 1048576 | tf_op jit(solution)/shard_map/all_to_all | solution.py:33
  125.3 0.0 all-gather.2.cloned.1.call-start
  125.4 5.8 %fusion = f32[62,2048]{1,0:T(8,128)} fusion(s32[62,2048]{1,0:T(8,128)S(1)} %get-tuple-element.27, f32[16,16,1]{1,0,2:T(8,128)S(1)} %reshape.69, s32[62,2048]{1,0:T(8,128)S(1)} %get-tuple-element.26), kind=kOutput, calls=%fused_computation.2 | convolution fusion | flops 398069760 | bytes 1524736 | tf_op jit(solution)/shard_map/jk,krb->jrb/dot_general | solution.py:25
  131.2 0.0 copy-done.6
  131.2 0.0 copy-start.2
  131.2 0.0 copy-start.7
  131.2 0.0 copy-start.8
  131.2 0.1 reshape.68
  132.1 5.3 %fusion.1 = f32[62,2048]{1,0:T(8,128)S(1)} fusion(s32[62,2048]{1,0:T(8,128)S(1)} %get-tuple-element.29, f32[16,16,1]{1,0,2:T(8,128)S(1)} %reshape.68, s32[62,2048]{1,0:T(8,128)S(1)} %get-tuple-element.28), kind=kOutput, calls=%fused_computation.4 | convolution fusion | flops 398069760 | bytes 1524736 | tf_op jit(solution)/shard_map/jk,krb->jrb/dot_general | solution.py:25
  137.4 0.0 all-to-all-done
  137.4 0.3 copy.35
  137.7 0.4 reshape.67
  138.1 0.0 copy-done.2
  138.1 0.0 copy-done.7
  138.1 0.0 copy-done.8
  138.1 0.4 fusion.17
  138.5 0.0 copy-start.3
  138.5 0.0 copy-start.4
  138.5 0.3 mul.106
  138.8 0.3 mul.98
  139.1 0.5 fusion.13
  139.6 0.3 copy.28
  139.9 12.9 %all_to_all.32 = f32[8,8,1984]{2,0,1:T(8,128)} all-to-all(f32[8,8,1984]{2,0,1:T(8,128)S(1)} %copy.28), channel_id=1, replica_groups=mesh['dp'=16,'tensor'=8] {'tensor'}, dimensions={1} | all-to-all | bytes 1015808 | tf_op jit(solution)/shard_map/all_to_all | solution.py:43
  152.8 0.0 all-gather.2.cloned.1.call-update
  152.8 9.1 %copy.30 = f32[1024,1984]{1,0:T(8,128)} copy(f32[1024,1984]{0,1:T(8,128)} %param.9) | data formatting | bytes 16252928 | tf_op args[0]
  161.9 0.0 copy-done.3
  161.9 0.0 copy-done.4
  161.9 1.0 divide_convert_fusion
  162.9 63.9 %all-gather.2.cloned.1.call-done = f32[1024,1984]{1,0:T(8,128)} async-done(((f32[64,1984]{1,0:T(8,128)}), f32[1024,1984]{1,0:T(8,128)}) %all-gather.2.cloned.1.call-update) | async-done | bytes 8126480 | tf_op jit(solution)/shard_map/all_gather | solution.py:44
  226.8 12.0 %multiply_subtract_fusion = f32[1024,1984]{1,0:T(8,128)} fusion(f32[1024,1984]{1,0:T(8,128)} %copy.30, f32[1024,1984]{1,0:T(8,128)} %all-gather.2.cloned.1.call-done), kind=kLoop, calls=%fused_computation | loop fusion | flops 8126464 | bytes 24379392 | tf_op jit(solution)/shard_map/sub | solution.py:45
  238.9 9.1 %copy.31 = f32[1024,1984]{0,1:T(8,128)} copy(f32[1024,1984]{1,0:T(8,128)} %multiply_subtract_fusion) | data formatting | bytes 16252928
  (1 shorter events, 0.0 us)
Async XLA Ops:
  7.2 114.1 %reduce-scatter.2.cloned.1.call-start = ((), (), s32[]{:S(2)}) async-start(), calls=%async_computation.3 | async-start | bytes 8912896 | tf_op jit(solution)/shard_map/reduce_scatter | solution.py:32
  16.4 0.7 copy-start.5
  16.4 1.1 copy-start
  16.4 1.4 copy-start.1
  17.0 114.2 %copy-start.6 = (f32[256]{0:T(256)S(1)}, f32[256]{0:T(256)}, u32[]{:S(2)}) copy-start(f32[256]{0:T(256)} %param.15) | copy-start | bytes 3076
  121.3 16.1 %all-to-all-start = ((f32[8,8,1984]{2,1,0:T(8,128)}), f32[8,8,1984]{2,1,0:T(8,128)S(1)}, u32[]{:S(2)}, u32[]{:S(2)}) async-start(f32[8,8,1984]{2,1,0:T(8,128)} %bitcast.25), calls=%async_computation.1 | async-start | bytes 1048576 | tf_op jit(solution)/shard_map/all_to_all | solution.py:33
  125.3 101.5 %all-gather.2.cloned.1.call-start = ((), (), s32[]{:S(2)}) async-start(), calls=%async_computation.4 | async-start | bytes 8912896 | tf_op jit(solution)/shard_map/all_gather | solution.py:44
  131.2 6.9 %copy-start.2 = (f32[62,2048]{1,0:T(8,128)S(1)}, f32[62,2048]{1,0:T(8,128)}, u32[]{:S(2)}) copy-start(f32[62,2048]{1,0:T(8,128)} %fusion) | copy-start | bytes 1523716
  131.2 6.9 %copy-start.7 = (f32[62]{0:T(128)S(1)}, f32[62]{0:T(128)}, u32[]{:S(2)}) copy-start(f32[62]{0:T(128)} %param.13) | copy-start | bytes 748
  131.2 6.9 %copy-start.8 = (f32[62]{0:T(128)S(1)}, f32[62]{0:T(128)}, u32[]{:S(2)}) copy-start(f32[62]{0:T(128)} %param.14) | copy-start | bytes 748
  138.5 23.4 %copy-start.3 = (f32[62]{0:T(128)}, f32[62]{0:T(128)S(1)}, u32[]{:S(2)}) copy-start(f32[62]{0:T(128)S(1)} %get-tuple-element.20) | copy-start | bytes 748
  138.5 23.4 %copy-start.4 = (f32[62]{0:T(128)}, f32[62]{0:T(128)S(1)}, u32[]{:S(2)}) copy-start(f32[62]{0:T(128)S(1)} %get-tuple-element.21) | copy-start | bytes 748
Sparse Core Ops, SparseCore 0:
  16.5 104.7 reduce-scatter.1
  152.9 73.8 all-gather.1
where the time goes:
time: 256 us; the launch traced here: 255 us
  waiting for transfers between devices  167 us (65%)
  local copies, waits for them, and re-layouts  30.2 us (12%)
  between operations  14.9 us (6%)
  other arithmetic  14.5 us (6%)
  blocking collectives  12.9 us (5%)
  matrix products  11.1 us (4%)
  starting transfers between devices  4.09 us (2%)
    reduce_scatter x1, waiting for transfers between devices, shards(): lax.psum_scatter(partial_value, 'dp', scatter_dimension=0, tiled=True)  103 us
    all_gather x1, waiting for transfers between devices, shards(): mine = lax.all_gather(columns, 'dp', axis=0, tiled=True)  63.9 us
    unnamed x21, local copies, waits for them, and re-layouts  28.4 us
    all_to_all x1, blocking collectives, shards(): lax.all_to_all(update, 'tensor', split_axis=1, concat_axis=0, tiled=True)  12.9 us
    sub x1, other arithmetic, shards(): new_weight = weight - learn_rate * (mine + decay_rate * weight)  12 us
    dot_general x2, matrix products, lookup(): jnp.einsum('jk,krb->jrb', grid, low_hits, precision=lax.Precision.HIGHEST)  11.1 us
  transfers between devices with their start and end apart: 3, of which 2 were waited for; matrix products, arithmetic and copies ran while one was open for 9% of the time, Pallas kernels for 0%

commit v1 on v0

v1 whole, which is shorter than its diff:
```python
import jax
import jax.numpy as jnp
from jax import lax
from jax.sharding import Mesh, PartitionSpec as P

BLOCK = 2048
N_YH, N_Z, N_CORE, N_YL, N_X = 2, 4, 2, 2, 4
AXES = ("yh", "z", "core", "yl", "x")
DP = ("yh", "z", "core")
TENSOR = ("yl", "x")
ROW_OWNERS = ("core", "yl", "x")
PARTS = 2

beta_one = 0.9
beta_two = 0.999
adam_eps = 1e-08
learn_rate = 0.02
decay_rate = 0.1
scale_eps = 1e-06

SWAP = [(0, 1), (1, 0)]
UP = [(i, (i + 1) % N_Z) for i in range(N_Z)]
DOWN = [(i, (i - 1) % N_Z) for i in range(N_Z)]


def lookup(codes, table):
    high = codes // 16
    low = codes - high * 16
    digits = lax.broadcasted_iota(jnp.int32, (16, 1, 1), 0)
    low_hits = (low[None, :, :] == digits).astype(jnp.float32)
    grid = table.reshape(16, 16)
    picked = jnp.einsum("jk,krb->jrb", grid, low_hits, precision=lax.Precision.HIGHEST)
    high_hits = high[None, :, :] == digits
    return jnp.sum(jnp.where(high_hits, picked, jnp.float32(0.0)), axis=0)


def tile(array, yh, z):
    where = (yh * N_Z + z % N_Z) * 128
    return lax.dynamic_slice_in_dim(array, where, 128, axis=1)


def reduce_part(grad_t, part, width, half, c, z, h):
    send = lax.dynamic_slice_in_dim(grad_t, (1 - c) * half + part * width, width, axis=0)
    other = lax.ppermute(send, "core", SWAP)
    own = lax.dynamic_slice_in_dim(grad_t, c * half + part * width, width, axis=0) + other
    up = lax.ppermute(jnp.stack([tile(own, 0, z + 2), tile(own, 1, z + 1)]), "z", UP)
    down = lax.ppermute(jnp.stack([tile(own, 1, z + 2), tile(own, 0, z + 3)]), "z", DOWN)
    up2 = lax.ppermute(tile(own, 0, z + 1) + up[0], "z", UP)
    down2 = lax.ppermute(tile(own, 1, z + 3) + down[0], "z", DOWN)
    low = tile(own, 0, z) + down[1] + up2
    high = tile(own, 1, z) + up[1] + down2
    far = lax.ppermute(jnp.where(h == 0, high, low), "yh", SWAP)
    return jnp.where(h == 0, low, high) + far


def gather_part(mine, h):
    far = lax.ppermute(mine, "yh", SWAP)
    low = jnp.where(h == 0, mine, far)
    high = jnp.where(h == 0, far, mine)
    both = jnp.stack([low, high])
    up = lax.ppermute(both, "z", UP)
    down = lax.ppermute(both, "z", DOWN)
    up2 = lax.ppermute(up[0], "z", UP)
    down2 = lax.ppermute(down[1], "z", DOWN)
    return both, up, down, jnp.stack([up2, down2])


def shards(weight, grad_parts, m_codes, v_codes, m_absmax, v_absmax, code_m, code_v, step):
    rows, columns = weight.shape
    half = columns // N_CORE
    width = half // PARTS
    owners = N_CORE * N_YL * N_X
    c = lax.axis_index("core")
    z = lax.axis_index("z")
    h = lax.axis_index("yh")
    grad_t = grad_parts[0].T
    weight_t = weight.T
    row_tile = rows // (N_YH * N_Z)
    dev_rows = row_tile // owners
    count = step[0].astype(jnp.float32)
    fix_one = 1.0 - jnp.power(jnp.float32(beta_one), count)
    fix_two = 1.0 - jnp.power(jnp.float32(beta_two), count)

    def spread(state):
        wide = state.reshape(dev_rows, N_YL * N_X, N_CORE, PARTS, width)
        return wide.transpose(3, 2, 1, 0, 4).reshape(PARTS, owners, dev_rows, width)

    def collect(parts):
        whole = jnp.stack(parts).reshape(PARTS, N_CORE, N_YL * N_X, dev_rows, width)
        return whole.transpose(3, 2, 1, 0, 4).reshape(-1, BLOCK)

    m_old = spread(lookup(m_codes, code_m) * m_absmax[:, None])
    v_old = spread(lookup(v_codes, code_v) * v_absmax[:, None])

    m_parts, v_parts, pieces = [], [], []
    for part in range(PARTS):
        mine = reduce_part(grad_t, part, width, half, c, z, h)
        sent = mine.T.reshape(owners, dev_rows, width)
        grad = lax.all_to_all(sent, ROW_OWNERS, split_axis=0, concat_axis=0, tiled=True)
        m_new = beta_one * m_old[part] + (1.0 - beta_one) * grad
        v_new = beta_two * v_old[part] + (1.0 - beta_two) * grad * grad
        m_parts.append(m_new)
        v_parts.append(v_new)
        update = m_new / fix_one / (jnp.sqrt(v_new / fix_two) + adam_eps)
        back = lax.all_to_all(update, ROW_OWNERS, split_axis=0, concat_axis=0, tiled=True)
        got = gather_part(back.reshape(row_tile, width).T, h)
        pieces.append([(g, lax.ppermute(g, "core", SWAP)) for g in got])

    halves = []
    for core in range(N_CORE):
        for part in range(PARTS):
            near, up, down, far = [jnp.where(c == core, g, o) for g, o in pieces[part]]
            ring = jnp.stack([near, down, far, up])
            tiles = [lax.dynamic_index_in_dim(ring, (k - z) % N_Z, 0, keepdims=False) for k in range(N_Z)]
            halves.append(jnp.concatenate([t[yh] for yh in range(N_YH) for t in tiles], axis=1))
    mine_t = jnp.concatenate(halves, axis=0)
    new_weight = (weight_t - learn_rate * (mine_t + decay_rate * weight_t)).T

    m_new = collect(m_parts)
    v_new = collect(v_parts)
    m_absmax_new = jnp.max(jnp.abs(m_new), axis=1)
    v_absmax_new = jnp.max(v_new, axis=1)
    m_scaled = (m_new / (m_absmax_new[:, None] + scale_eps)).astype(jnp.bfloat16)
    v_scaled = (v_new / (v_absmax_new[:, None] + scale_eps)).astype(jnp.bfloat16)
    return (new_weight, m_scaled, v_scaled, m_absmax_new, v_absmax_new)


def solution(mesh):
    fine = Mesh(mesh.devices.reshape(N_YH, N_Z, N_CORE, N_YL, N_X), AXES)
    blocks = P(DP + TENSOR)
    in_specs = (P(None, TENSOR), P(DP, None, TENSOR), blocks, blocks, blocks, blocks, P(), P(), P())
    out_specs = (P(None, TENSOR), blocks, blocks, blocks, blocks)
    return jax.shard_map(shards, mesh=fine, in_specs=in_specs, out_specs=out_specs, check_vma=False)
```

time: 256 us -> 243 us (0.949)
  waiting for transfers between devices: 167 us -> 57 us
  starting transfers between devices: 4.09 us -> 63.4 us
  local copies, waits for them, and re-layouts: 30.2 us -> 64.4 us
  other arithmetic: 14.5 us -> 43.1 us
  blocking collectives: 12.9 us -> 0 us
  between operations: 14.9 us -> 2.14 us
    reduce_scatter x1 -> x0, waiting for transfers between devices: 103 us -> none  [shards(): lax.psum_scatter(partial_value, 'dp', scatter_dimension=0, tiled=True)]
    all_gather x1 -> x0, waiting for transfers between devices: 63.9 us -> none  [shards(): mine = lax.all_gather(columns, 'dp', axis=0, tiled=True)]
    ppermute x0 -> x30, starting transfers between devices: none -> 45.7 us  [the longest x8 16.3 us: shards(): pieces.append([(g, lax.ppermute(g, 'core', SWAP)) for g in got])]
    ppermute x0 -> x30, waiting for transfers between devices: none -> 34.1 us  [the longest x2 12.1 us: reduce_part(): lax.ppermute(jnp.stack([tile(own, 1, z + 2), tile(own, 0, z + 3)]), 'z',...]
    all_to_all x1 -> x4, waiting for transfers between devices: 0.01 us -> 22.9 us  [the longest x2 13.9 us: shards(): lax.all_to_all(sent, ROW_OWNERS, split_axis=0, concat_axis=0, tiled=True)]
    all_to_all x1 -> x4, starting transfers between devices: 4.01 us -> 17.7 us  [the longest x2 10.5 us: shards(): lax.all_to_all(sent, ROW_OWNERS, split_axis=0, concat_axis=0, tiled=True)]
    another operation x0 -> x4, local copies, waits for them, and re-layouts: none -> 13.4 us
    all_to_all x1 -> x0, blocking collectives: 12.9 us -> none  [shards(): lax.all_to_all(update, 'tensor', split_axis=1, concat_axis=0, tiled=True)]
  transfers between devices with their start and end apart: 3 -> 34, of which waited for: 2 -> 14; matrix products, arithmetic and copies ran while one was open for 9% -> 26% of each run, Pallas kernels for 0% -> 0%
where the time goes in v1:
time: 243 us; the launch traced here: 241 us
  local copies, waits for them, and re-layouts  64.4 us (27%)
  starting transfers between devices  63.4 us (26%)
  waiting for transfers between devices  57 us (23%)
  other arithmetic  43.1 us (18%)
  matrix products  11.4 us (5%)
    unnamed x64, local copies, waits for them, and re-layouts  27.4 us
    ppermute x8, starting transfers between devices, shards(): pieces.append([(g, lax.ppermute(g, 'core', SWAP)) for g in got])  16.3 us
    all_to_all x2, waiting for transfers between devices, shards(): lax.all_to_all(sent, ROW_OWNERS, split_axis=0, concat_axis=0, tiled=True)  13.9 us
    another operation x3, local copies, waits for them, and re-layouts  12.3 us
    ppermute x2, waiting for transfers between devices, reduce_part(): lax.ppermute(jnp.stack([tile(own, 1, z + 2), tile(own, 0, z + 3)]), 'z',...  12.1 us
    transpose x1, other arithmetic, shards(): new_weight = (weight_t - learn_rate * (mine_t + decay_rate * weight_t)).T  12.1 us
    dot_general x2, matrix products, lookup(): jnp.einsum('jk,krb->jrb', grid, low_hits, precision=lax.Precision.HIGHEST)  11.4 us
    all_to_all x2, starting transfers between devices, shards(): lax.all_to_all(sent, ROW_OWNERS, split_axis=0, concat_axis=0, tiled=True)  10.5 us
  transfers between devices with their start and end apart: 34, of which 14 were waited for; matrix products, arithmetic and copies ran while one was open for 26% of the time, Pallas kernels for 0%

profile of v1, /device:TPU:1, one launch (start us, length us, event | category | flops | bytes accessed | tf_op | source)
XLA Modules:
  0.0 241.5 jit_solution(14281394677672952701)
XLA Ops:
  0.7 7.4 %constant_dynamic-slice_fusion = (f32[1,1024,496]{1,2,0:T(8,128)}, f32[496,1024]{1,0:T(8,128)}, f32[1,1024,496]{1,2,0:T(8,128)}, f32[496,1024]{1,0:T(8,128)}) fusion(f32[1,1024,1984]{1,2,0:T(8,128)} %param.10, s32[]{:T(128)S(6)} %select_n.309, s32[]{:T(128)S(6)} %select_n.278, s32[]{:T(128)S(6)} %select_n.277, s32[]{:T(128)S(6)} %select_n.310), kind=kLoop, calls=%fused_computation.190 | loop fusion | bytes 16252944 | tf_op jit(solution)/shard_map/dynamic-slice.6
  9.7 1.9 copy.51
  11.6 3.0 %copy.48 = f32[1,1024,496]{2,1,0:T(8,128)} copy(f32[1,1024,496]{1,2,0:T(8,128)} %get-tuple-element.39) | data formatting | bytes 4063232 | tf_op jit(solution)/shard_map/dynamic-slice.4
  14.9 5.5 %fusion.4 = f32[62,2048]{1,0:T(8,128)S(1)} fusion(s32[62,2048]{1,0:T(8,128)S(1)} %get-tuple-element.76, f32[16,16,1]{1,0,2:T(8,128)S(1)} %reshape.181, s32[62,2048]{1,0:T(8,128)S(1)} %get-tuple-element.75), kind=kOutput, calls=%fused_computation.8 | convolution fusion | flops 398069760 | bytes 1524736 | tf_op jit(solution)/shard_map/jk,krb->jrb/dot_general | solution.py:32
  21.6 2.9 %copy.52 = f32[496,1024]{0,1:T(8,128)} copy(f32[496,1024]{1,0:T(8,128)} %collective-permute-done.15) | data formatting | bytes 4063232 | tf_op jit(solution)/shard_map/ppermute | solution.py:44
  24.5 3.4 %bitcast_add_fusion = f32[496,1024]{0,1:T(8,128)} fusion(f32[496,1024]{0,1:T(8,128)} %copy.52, f32[1,1024,496]{2,1,0:T(8,128)S(1)} %copy.51), kind=kLoop, calls=%fused_computation.21 | loop fusion | flops 507904 | bytes 6094848 | tf_op jit(solution)/shard_map/add | solution.py:45
  27.9 2.9 %copy.49 = f32[496,1024]{0,1:T(8,128)} copy(f32[496,1024]{1,0:T(8,128)} %collective-permute-done) | data formatting | bytes 4063232 | tf_op jit(solution)/shard_map/ppermute | solution.py:44
  30.8 2.7 %bitcast_add_fusion.1 = f32[496,1024]{0,1:T(8,128)S(1)} fusion(f32[496,1024]{0,1:T(8,128)} %copy.49, f32[1,1024,496]{2,1,0:T(8,128)} %copy.48), kind=kLoop, calls=%fused_computation.22 | loop fusion | flops 507904 | bytes 6094848 | tf_op jit(solution)/shard_map/add | solution.py:45
  35.5 3.8 %collective-permute-start.16 = (f32[2,496,128]{1,2,0:T(8,128)}, f32[2,496,128]{1,2,0:T(8,128)}, u32[]{:S(2)}, u32[]{:S(2)}) collective-permute-start(f32[2,496,128]{1,2,0:T(8,128)} %pad_maximum_fusion.8), channel_id=1, source_target_pairs={{0,48},{16,0},{32,16},{48,32},{1,49},{17,1},{33,17},{49,33},{2,50}... | collective-permute-start | bytes 1523720 | tf_op jit(solution)/shard_map/ppermute | solution.py:47
  40.3 5.9 %fusion.3 = f32[62,2048]{1,0:T(8,128)} fusion(s32[62,2048]{1,0:T(8,128)S(1)} %copy-done.8, f32[16,16,1]{1,0,2:T(8,128)S(1)} %reshape.182, s32[62,2048]{1,0:T(8,128)S(1)} %get-tuple-element.77), kind=kOutput, calls=%fused_computation.6 | convolution fusion | flops 398069760 | bytes 1524736 | tf_op jit(solution)/shard_map/jk,krb->jrb/dot_general | solution.py:32
  46.3 4.2 %collective-permute-done.16 = f32[2,496,128]{1,2,0:T(8,128)} collective-permute-done((f32[2,496,128]{1,2,0:T(8,128)}, f32[2,496,128]{1,2,0:T(8,128)}, u32[]{:S(2)}, u32[]{:S(2)}) %collective-permute-start.16) | collective-permute-done | bytes 507936 | tf_op jit(solution)/shard_map/ppermute | solution.py:47
  50.5 2.0 fusion.39
  53.8 7.9 %collective-permute-done.1 = f32[2,496,128]{1,2,0:T(8,128)} collective-permute-done((f32[2,496,128]{1,2,0:T(8,128)}, f32[2,496,128]{1,2,0:T(8,128)}, u32[]{:S(2)}, u32[]{:S(2)}) %collective-permute-start.1) | collective-permute-done | bytes 507936 | tf_op jit(solution)/shard_map/ppermute | solution.py:47
  61.7 1.7 fusion.53
  66.4 2.2 copy.59
  70.3 3.0 %collective-permute-start.19 = (f32[496,128]{0,1:T(8,128)}, f32[496,128]{0,1:T(8,128)S(1)}, u32[]{:S(2)}, u32[]{:S(2)}) collective-permute-start(f32[496,128]{0,1:T(8,128)} %get-tuple-element.41), channel_id=1, source_target_pairs={{0,48},{16,0},{32,16},{48,32},{1,49},{17,1},{33,17},{49,33},{2,50}... | collective-permute-start | bytes 761864 | tf_op jit(solution)/shard_map/ppermute | solution.py:49
  74.5 1.9 slice_multiply_fusion
  76.4 2.7 %collective-permute-start.4 = (f32[496,128]{0,1:T(8,128)}, f32[496,128]{0,1:T(8,128)S(1)}, u32[]{:S(2)}, u32[]{:S(2)}) collective-permute-start(f32[496,128]{0,1:T(8,128)} %get-tuple-element.46), channel_id=1, source_target_pairs={{0,48},{16,0},{32,16},{48,32},{1,49},{17,1},{33,17},{49,33},{2,50}... | collective-permute-start | bytes 761864 | tf_op jit(solution)/shard_map/ppermute | solution.py:49
  81.2 3.8 %collective-permute-done.18 = f32[496,128]{0,1:T(8,128)} collective-permute-done((f32[496,128]{0,1:T(8,128)S(1)}, f32[496,128]{0,1:T(8,128)}, u32[]{:S(2)}, u32[]{:S(2)}) %collective-permute-start.18) | collective-permute-done | bytes 253984 | tf_op jit(solution)/shard_map/ppermute | solution.py:48
  85.1 2.2 broadcast_select_fusion
  87.3 2.9 %collective-permute-start.20 = (f32[496,128]{0,1:T(8,128)}, f32[496,128]{0,1:T(8,128)}, u32[]{:S(2)}, u32[]{:S(2)}) collective-permute-start(f32[496,128]{0,1:T(8,128)} %get-tuple-element.28), channel_id=1, source_target_pairs={{0,64},{64,0},{1,65},{65,1},{2,66},{66,2},{3,67},{67,3},{4,68},{68... | collective-permute-start | bytes 761864 | tf_op jit(solution)/shard_map/ppermute | solution.py:52
  90.2 1.9 broadcast_select_fusion.1
  92.1 2.9 %collective-permute-start.5 = (f32[496,128]{0,1:T(8,128)}, f32[496,128]{0,1:T(8,128)S(1)}, u32[]{:S(2)}, u32[]{:S(2)}) collective-permute-start(f32[496,128]{0,1:T(8,128)} %get-tuple-element.34), channel_id=1, source_target_pairs={{0,64},{64,0},{1,65},{65,1},{2,66},{66,2},{3,67},{67,3},{4,68},{68... | collective-permute-start | bytes 761864 | tf_op jit(solution)/shard_map/ppermute | solution.py:52
  95.7 9.2 %copy.46 = f32[1024,1984]{1,0:T(8,128)} copy(f32[1024,1984]{0,1:T(8,128)} %param.9) | data formatting | bytes 16252928 | tf_op args[0]
  104.9 1.8 add_bitcast_fusion
  106.7 6.9 %all-to-all-start.2 = ((f32[16,8,496]{2,1,0:T(8,128)}), f32[16,8,496]{2,1,0:T(8,128)S(1)}, u32[]{:S(2)}, u32[]{:S(2)}) async-start(f32[16,8,496]{2,1,0:T(8,128)} %add_bitcast_fusion), calls=%async_computation.2 | async-start | bytes 524288 | tf_op jit(solution)/shard_map/all_to_all | solution.py:99
  114.4 7.0 %all-to-all-done.2 = f32[16,8,496]{2,1,0:T(8,128)S(1)} async-done(((f32[16,8,496]{2,1,0:T(8,128)}), f32[16,8,496]{2,1,0:T(8,128)S(1)}, u32[]{:S(2)}, u32[]{:S(2)}) %all-to-all-start.2) | async-done | bytes 253984 | tf_op jit(solution)/shard_map/all_to_all | solution.py:99
  121.4 3.6 %all-to-all-start = ((f32[16,8,496]{2,1,0:T(8,128)}), f32[16,8,496]{2,1,0:T(8,128)S(1)}, u32[]{:S(2)}, u32[]{:S(2)}) async-start(f32[16,8,496]{2,1,0:T(8,128)} %add_bitcast_fusion.1), calls=%async_computation | async-start | bytes 524288 | tf_op jit(solution)/shard_map/all_to_all | solution.py:99
  125.9 6.9 %all-to-all-done = f32[16,8,496]{2,1,0:T(8,128)S(1)} async-done(((f32[16,8,496]{2,1,0:T(8,128)}), f32[16,8,496]{2,1,0:T(8,128)S(1)}, u32[]{:S(2)}, u32[]{:S(2)}) %all-to-all-start) | async-done | bytes 253984 | tf_op jit(solution)/shard_map/all_to_all | solution.py:99
  132.7 3.6 %all-to-all-start.3 = ((f32[16,8,496]{2,1,0:T(8,128)}), f32[16,8,496]{2,1,0:T(8,128)S(1)}, u32[]{:S(2)}, u32[]{:S(2)}) async-start(f32[16,8,496]{2,1,0:T(8,128)} %get-tuple-element.25), calls=%async_computation.3 | async-start | bytes 524288 | tf_op jit(solution)/shard_map/all_to_all | solution.py:105
  140.8 3.4 %all-to-all-done.3 = f32[16,8,496]{2,1,0:T(8,128)S(1)} async-done(((f32[16,8,496]{2,1,0:T(8,128)}), f32[16,8,496]{2,1,0:T(8,128)S(1)}, u32[]{:S(2)}, u32[]{:S(2)}) %all-to-all-start.3) | async-done | bytes 253984 | tf_op jit(solution)/shard_map/all_to_all | solution.py:105
  144.1 3.6 %all-to-all-start.1 = ((f32[16,8,496]{2,1,0:T(8,128)}), f32[16,8,496]{2,1,0:T(8,128)S(1)}, u32[]{:S(2)}, u32[]{:S(2)}) async-start(f32[16,8,496]{2,1,0:T(8,128)} %get-tuple-element.31), calls=%async_computation.1 | async-start | bytes 524288 | tf_op jit(solution)/shard_map/all_to_all | solution.py:105
  147.7 1.9 collective-permute-start.21
  149.8 5.7 %all-to-all-done.1 = f32[16,8,496]{2,1,0:T(8,128)S(1)} async-done(((f32[16,8,496]{2,1,0:T(8,128)}), f32[16,8,496]{2,1,0:T(8,128)S(1)}, u32[]{:S(2)}, u32[]{:S(2)}) %all-to-all-start.1) | async-done | bytes 253984 | tf_op jit(solution)/shard_map/all_to_all | solution.py:105
  155.5 1.9 collective-permute-start.6
  160.8 3.8 %collective-permute-done.6 = f32[496,128]{0,1:T(8,128)S(1)} collective-permute-done((f32[496,128]{0,1:T(8,128)S(1)}, f32[496,128]{0,1:T(8,128)S(1)}, u32[]{:S(2)}, u32[]{:S(2)}) %collective-permute-start.6) | collective-permute-done | bytes 253984 | tf_op jit(solution)/shard_map/ppermute | solution.py:57
  168.5 3.1 %collective-permute-done.23 = f32[2,496,128]{1,2,0:T(8,128)S(1)} collective-permute-done((f32[2,496,128]{1,2,0:T(8,128)S(1)}, f32[2,496,128]{1,2,0:T(8,128)S(1)}, u32[]{:S(2)}, u32[]{:S(2)}) %collective-permute-start.23) | collective-permute-done | bytes 507936 | tf_op jit(solution)/shard_map/ppermute | solution.py:62
  171.6 3.5 %collective-permute-start.7 = (f32[2,496,128]{1,2,0:T(8,128)S(1)}, f32[2,496,128]{1,2,0:T(8,128)S(1)}, u32[]{:S(2)}, u32[]{:S(2)}) collective-permute-start(f32[2,496,128]{1,2,0:T(8,128)S(1)} %pad_maximum_fusion.6), channel_id=1, source_target_pairs={{0,8},{8,0},{1,9},{9,1},{2,10},{10,2},{3,11},{11,3},{4,12},{12,4},... | collective-permute-start | bytes 1523720 | tf_op jit(solution)/shard_map/ppermute | solution.py:107
  175.1 2.8 %collective-permute-start.27 = (f32[496,128]{0,1:T(8,128)S(1)}, f32[496,128]{0,1:T(8,128)S(1)}, u32[]{:S(2)}, u32[]{:S(2)}) collective-permute-start(f32[496,128]{0,1:T(8,128)S(1)} %slice_bitcast_fusion), channel_id=1, source_target_pairs={{0,48},{16,0},{32,16},{48,32},{1,49},{17,1},{33,17},{49,33},{2,50}... | collective-permute-start | bytes 761864 | tf_op jit(solution)/shard_map/ppermute | solution.py:64
  178.0 4.9 %collective-permute-done.8 = f32[2,496,128]{1,2,0:T(8,128)S(1)} collective-permute-done((f32[2,496,128]{1,2,0:T(8,128)S(1)}, f32[2,496,128]{1,2,0:T(8,128)S(1)}, u32[]{:S(2)}, u32[]{:S(2)}) %collective-permute-start.8) | collective-permute-done | bytes 507936 | tf_op jit(solution)/shard_map/ppermute | solution.py:62
  182.9 2.6 %collective-permute-done.10 = f32[2,496,128]{1,2,0:T(8,128)S(1)} collective-permute-done((f32[2,496,128]{1,2,0:T(8,128)S(1)}, f32[2,496,128]{1,2,0:T(8,128)S(1)}, u32[]{:S(2)}, u32[]{:S(2)}) %collective-permute-start.10) | collective-permute-done | bytes 507936 | tf_op jit(solution)/shard_map/ppermute | solution.py:61
  187.1 3.0 %collective-permute-start.24 = (f32[2,496,128]{1,2,0:T(8,128)S(1)}, f32[2,496,128]{1,2,0:T(8,128)S(1)}, u32[]{:S(2)}, u32[]{:S(2)}) collective-permute-start(f32[2,496,128]{1,2,0:T(8,128)S(1)} %collective-permute-done.23), channel_id=1, source_target_pairs={{0,8},{8,0},{1,9},{9,1},{2,10},{10,2},{3,11},{11,3},{4,12},{12,4},... | collective-permute-start | bytes 1523720 | tf_op jit(solution)/shard_map/ppermute | solution.py:107
  190.2 1.7 collective-permute-start.29
  192.0 4.1 %collective-permute-start.9 = (f32[2,496,128]{1,2,0:T(8,128)S(1)}, f32[2,496,128]{1,2,0:T(8,128)S(1)}, u32[]{:S(2)}, u32[]{:S(2)}) collective-permute-start(f32[2,496,128]{1,2,0:T(8,128)S(1)} %collective-permute-done.8), channel_id=1, source_target_pairs={{0,8},{8,0},{1,9},{9,1},{2,10},{10,2},{3,11},{11,3},{4,12},{12,4},... | collective-permute-start | bytes 1523720 | tf_op jit(solution)/shard_map/ppermute | solution.py:107
  196.2 2.7 %collective-permute-start.28 = (f32[2,496,128]{1,2,0:T(8,128)S(1)}, f32[2,496,128]{1,2,0:T(8,128)S(1)}, u32[]{:S(2)}, u32[]{:S(2)}) collective-permute-start(f32[2,496,128]{1,2,0:T(8,128)S(1)} %pad_maximum_fusion.11), channel_id=1, source_target_pairs={{0,8},{8,0},{1,9},{9,1},{2,10},{10,2},{3,11},{11,3},{4,12},{12,4},... | collective-permute-start | bytes 1523720 | tf_op jit(solution)/shard_map/ppermute | solution.py:107
  211.5 8.8 %concatenate.21 = f32[1984,1024]{0,1:T(8,128)} concatenate(f32[496,1024]{0,1:T(8,128)S(1)} %fusion.45, f32[496,1024]{0,1:T(8,128)} %copy-done.1, f32[496,1024]{0,1:T(8,128)} %copy-done, f32[496,1024]{0,1:T(8,128)} %fusion.15), dimensions={0} | concatenate | bytes 16252928 | tf_op jit(solution)/shard_map/concatenate | solution.py:116
  220.2 12.1 %fusion.2 = f32[1024,1984]{1,0:T(8,128)} fusion(f32[1984,1024]{0,1:T(8,128)} %concatenate.21, f32[1024,1984]{1,0:T(8,128)} %copy.46), kind=kLoop, calls=%fused_computation.4 | loop fusion | flops 8126464 | bytes 24379392 | tf_op jit(solution)/shard_map/transpose | solution.py:117
  232.3 9.1 %copy.55 = f32[1024,1984]{0,1:T(8,128)} copy(f32[1024,1984]{1,0:T(8,128)} %fusion.2) | data formatting | bytes 16252928
  (159 shorter events, 43.1 us)
Async XLA Ops:
  0.6 8.9 %copy-start.11 = (f32[256]{0:T(256)S(1)}, f32[256]{0:T(256)}, u32[]{:S(2)}) copy-start(f32[256]{0:T(256)} %param.15) | copy-start | bytes 3076
  0.7 8.9 %copy-start.12 = (f32[256]{0:T(256)S(1)}, f32[256]{0:T(256)}, u32[]{:S(2)}) copy-start(f32[256]{0:T(256)} %param.16) | copy-start | bytes 3076
  8.1 13.6 %collective-permute-start.15 = (f32[496,1024]{1,0:T(8,128)}, f32[496,1024]{1,0:T(8,128)}, u32[]{:S(2)}, u32[]{:S(2)}) collective-permute-start(f32[496,1024]{1,0:T(8,128)} %get-tuple-element.40), channel_id=1, source_target_pairs={{0,8},{8,0},{1,9},{9,1},{2,10},{10,2},{3,11},{11,3},{4,12},{12,4},... | collective-permute-start | bytes 6094856 | tf_op jit(solution)/shard_map/ppermute | solution.py:44
  9.5 18.4 %collective-permute-start = (f32[496,1024]{1,0:T(8,128)}, f32[496,1024]{1,0:T(8,128)}, u32[]{:S(2)}, u32[]{:S(2)}) collective-permute-start(f32[496,1024]{1,0:T(8,128)} %get-tuple-element.38), channel_id=1, source_target_pairs={{0,8},{8,0},{1,9},{9,1},{2,10},{10,2},{3,11},{11,3},{4,12},{12,4},... | collective-permute-start | bytes 6094856 | tf_op jit(solution)/shard_map/ppermute | solution.py:44
  11.6 3.0 %copy-start.6 = (s32[62,2048]{1,0:T(8,128)S(1)}, s32[62,2048]{1,0:T(8,128)}, u32[]{:S(2)}) copy-start(s32[62,2048]{1,0:T(8,128)} %param.11) | copy-start | bytes 1523716
  14.9 5.5 %copy-start.13 = (f32[62]{0:T(128)S(1)}, f32[62]{0:T(128)}, u32[]{:S(2)}) copy-start(f32[62]{0:T(128)} %param.13) | copy-start | bytes 748
  14.9 5.6 %copy-start.7 = (s32[62,2048]{1,0:T(8,128)S(1)}, s32[62,2048]{1,0:T(8,128)}, u32[]{:S(2)}) copy-start(s32[62,2048]{1,0:T(8,128)} %param.12) | copy-start | bytes 1523716
  33.5 6.8 %copy-start.8 = (s32[62,2048]{1,0:T(8,128)S(1)}, s32[62,2048]{1,0:T(8,128)}, u32[]{:S(2)}) copy-start(s32[62,2048]{1,0:T(8,128)} %get-tuple-element.78) | copy-start | bytes 1523716
  35.5 14.9 %collective-permute-start.16 = (f32[2,496,128]{1,2,0:T(8,128)}, f32[2,496,128]{1,2,0:T(8,128)}, u32[]{:S(2)}, u32[]{:S(2)}) collective-permute-start(f32[2,496,128]{1,2,0:T(8,128)} %pad_maximum_fusion.8), channel_id=1, source_target_pairs={{0,48},{16,0},{32,16},{48,32},{1,49},{17,1},{33,17},{49,33},{2,50}... | collective-permute-start | bytes 1523720 | tf_op jit(solution)/shard_map/ppermute | solution.py:47
  40.2 21.5 %collective-permute-start.1 = (f32[2,496,128]{1,2,0:T(8,128)}, f32[2,496,128]{1,2,0:T(8,128)}, u32[]{:S(2)}, u32[]{:S(2)}) collective-permute-start(f32[2,496,128]{1,2,0:T(8,128)} %pad_maximum_fusion.4), channel_id=1, source_target_pairs={{0,48},{16,0},{32,16},{48,32},{1,49},{17,1},{33,17},{49,33},{2,50}... | collective-permute-start | bytes 1523720 | tf_op jit(solution)/shard_map/ppermute | solution.py:47
  52.5 12.3 %copy-start.9 = (f32[62,2048]{1,0:T(8,128)S(1)}, f32[62,2048]{1,0:T(8,128)}, u32[]{:S(2)}) copy-start(f32[62,2048]{1,0:T(8,128)} %fusion.3) | copy-start | bytes 1523716
  52.5 12.3 %copy-start.14 = (f32[62]{0:T(128)S(1)}, f32[62]{0:T(128)}, u32[]{:S(2)}) copy-start(f32[62]{0:T(128)} %param.14) | copy-start | bytes 748
  53.3 20.0 %collective-permute-start.17 = (f32[2,496,128]{1,2,0:T(8,128)}, f32[2,496,128]{1,2,0:T(8,128)}, u32[]{:S(2)}, u32[]{:S(2)}) collective-permute-start(f32[2,496,128]{1,2,0:T(8,128)} %pad_maximum_fusion.9), channel_id=1, source_target_pairs={{0,16},{16,32},{32,48},{48,0},{1,17},{17,33},{33,49},{49,1},{2,18}... | collective-permute-start | bytes 1523720 | tf_op jit(solution)/shard_map/ppermute | solution.py:46
  64.3 15.2 %collective-permute-start.2 = (f32[2,496,128]{1,2,0:T(8,128)}, f32[2,496,128]{1,2,0:T(8,128)}, u32[]{:S(2)}, u32[]{:S(2)}) collective-permute-start(f32[2,496,128]{1,2,0:T(8,128)} %pad_maximum_fusion.5), channel_id=1, source_target_pairs={{0,16},{16,32},{32,48},{48,0},{1,17},{17,33},{33,49},{49,1},{2,18}... | collective-permute-start | bytes 1523720 | tf_op jit(solution)/shard_map/ppermute | solution.py:46
  69.2 5.2 %copy-start.2 = (f32[8,8,2,2,496]{4,0,1,2,3:T(8,128)S(1)}, f32[8,8,2,2,496]{4,0,1,2,3:T(8,128)}, u32[]{:S(2)}) copy-start(f32[8,8,2,2,496]{4,0,1,2,3:T(8,128)} %copy.59) | copy-start | bytes 1523716
  70.3 10.2 %collective-permute-start.19 = (f32[496,128]{0,1:T(8,128)}, f32[496,128]{0,1:T(8,128)S(1)}, u32[]{:S(2)}, u32[]{:S(2)}) collective-permute-start(f32[496,128]{0,1:T(8,128)} %get-tuple-element.41), channel_id=1, source_target_pairs={{0,48},{16,0},{32,16},{48,32},{1,49},{17,1},{33,17},{49,33},{2,50}... | collective-permute-start | bytes 761864 | tf_op jit(solution)/shard_map/ppermute | solution.py:49
  74.4 10.7 %collective-permute-start.18 = (f32[496,128]{0,1:T(8,128)S(1)}, f32[496,128]{0,1:T(8,128)}, u32[]{:S(2)}, u32[]{:S(2)}) collective-permute-start(f32[496,128]{0,1:T(8,128)S(1)} %fusion.42), channel_id=1, source_target_pairs={{0,16},{16,32},{32,48},{48,0},{1,17},{17,33},{33,49},{49,1},{2,18}... | collective-permute-start | bytes 761864 | tf_op jit(solution)/shard_map/ppermute | solution.py:48
  76.4 13.8 %collective-permute-start.4 = (f32[496,128]{0,1:T(8,128)}, f32[496,128]{0,1:T(8,128)S(1)}, u32[]{:S(2)}, u32[]{:S(2)}) collective-permute-start(f32[496,128]{0,1:T(8,128)} %get-tuple-element.46), channel_id=1, source_target_pairs={{0,48},{16,0},{32,16},{48,32},{1,49},{17,1},{33,17},{49,33},{2,50}... | collective-permute-start | bytes 761864 | tf_op jit(solution)/shard_map/ppermute | solution.py:49
  80.4 9.8 %collective-permute-start.3 = (f32[496,128]{0,1:T(8,128)S(1)}, f32[496,128]{0,1:T(8,128)S(1)}, u32[]{:S(2)}, u32[]{:S(2)}) collective-permute-start(f32[496,128]{0,1:T(8,128)S(1)} %fusion.56), channel_id=1, source_target_pairs={{0,16},{16,32},{32,48},{48,0},{1,17},{17,33},{33,49},{49,1},{2,18}... | collective-permute-start | bytes 761864 | tf_op jit(solution)/shard_map/ppermute | solution.py:48
  87.3 17.7 %collective-permute-start.20 = (f32[496,128]{0,1:T(8,128)}, f32[496,128]{0,1:T(8,128)}, u32[]{:S(2)}, u32[]{:S(2)}) collective-permute-start(f32[496,128]{0,1:T(8,128)} %get-tuple-element.28), channel_id=1, source_target_pairs={{0,64},{64,0},{1,65},{65,1},{2,66},{66,2},{3,67},{67,3},{4,68},{68... | collective-permute-start | bytes 761864 | tf_op jit(solution)/shard_map/ppermute | solution.py:52
  92.1 21.6 %collective-permute-start.5 = (f32[496,128]{0,1:T(8,128)}, f32[496,128]{0,1:T(8,128)S(1)}, u32[]{:S(2)}, u32[]{:S(2)}) collective-permute-start(f32[496,128]{0,1:T(8,128)} %get-tuple-element.34), channel_id=1, source_target_pairs={{0,64},{64,0},{1,65},{65,1},{2,66},{66,2},{3,67},{67,3},{4,68},{68... | collective-permute-start | bytes 761864 | tf_op jit(solution)/shard_map/ppermute | solution.py:52
  104.9 20.1 %copy-start.4 = (f32[1,2,8,8,496]{4,3,2,1,0:T(8,128)S(1)}, f32[1,2,8,8,496]{4,3,2,1,0:T(8,128)}, u32[]{:S(2)}) copy-start(f32[1,2,8,8,496]{4,3,2,1,0:T(8,128)} %get-tuple-element.71) | copy-start | bytes 761860
  104.9 20.1 %copy-start.5 = (f32[1,2,8,8,496]{4,3,2,1,0:T(8,128)S(1)}, f32[1,2,8,8,496]{4,3,2,1,0:T(8,128)}, u32[]{:S(2)}) copy-start(f32[1,2,8,8,496]{4,3,2,1,0:T(8,128)} %get-tuple-element.82) | copy-start | bytes 761860
  106.7 29.6 %copy-start.3 = (f32[1,2,8,8,496]{4,3,2,1,0:T(8,128)S(1)}, f32[1,2,8,8,496]{4,3,2,1,0:T(8,128)}, u32[]{:S(2)}) copy-start(f32[1,2,8,8,496]{4,3,2,1,0:T(8,128)} %get-tuple-element.81) | copy-start | bytes 761860
  106.7 14.7 %all-to-all-start.2 = ((f32[16,8,496]{2,1,0:T(8,128)}), f32[16,8,496]{2,1,0:T(8,128)S(1)}, u32[]{:S(2)}, u32[]{:S(2)}) async-start(f32[16,8,496]{2,1,0:T(8,128)} %add_bitcast_fusion), calls=%async_computation.2 | async-start | bytes 524288 | tf_op jit(solution)/shard_map/all_to_all | solution.py:99
  121.4 11.3 %all-to-all-start = ((f32[16,8,496]{2,1,0:T(8,128)}), f32[16,8,496]{2,1,0:T(8,128)S(1)}, u32[]{:S(2)}, u32[]{:S(2)}) async-start(f32[16,8,496]{2,1,0:T(8,128)} %add_bitcast_fusion.1), calls=%async_computation | async-start | bytes 524288 | tf_op jit(solution)/shard_map/all_to_all | solution.py:99
  132.7 11.4 %all-to-all-start.3 = ((f32[16,8,496]{2,1,0:T(8,128)}), f32[16,8,496]{2,1,0:T(8,128)S(1)}, u32[]{:S(2)}, u32[]{:S(2)}) async-start(f32[16,8,496]{2,1,0:T(8,128)} %get-tuple-element.25), calls=%async_computation.3 | async-start | bytes 524288 | tf_op jit(solution)/shard_map/all_to_all | solution.py:105
  138.6 5.5 %copy-start.16 = (f32[62]{0:T(128)}, f32[62]{0:T(128)S(1)}, u32[]{:S(2)}) copy-start(f32[62]{0:T(128)S(1)} %reduce_max.19) | copy-start | bytes 748
  144.1 11.4 %all-to-all-start.1 = ((f32[16,8,496]{2,1,0:T(8,128)}), f32[16,8,496]{2,1,0:T(8,128)S(1)}, u32[]{:S(2)}, u32[]{:S(2)}) async-start(f32[16,8,496]{2,1,0:T(8,128)} %get-tuple-element.31), calls=%async_computation.1 | async-start | bytes 524288 | tf_op jit(solution)/shard_map/all_to_all | solution.py:105
  147.7 11.3 %collective-permute-start.21 = (f32[496,128]{0,1:T(8,128)S(1)}, f32[496,128]{0,1:T(8,128)S(1)}, u32[]{:S(2)}, u32[]{:S(2)}) collective-permute-start(f32[496,128]{0,1:T(8,128)S(1)} %bitcast.327), channel_id=1, source_target_pairs={{0,64},{64,0},{1,65},{65,1},{2,66},{66,2},{3,67},{67,3},{4,68},{68... | collective-permute-start | bytes 761864 | tf_op jit(solution)/shard_map/ppermute | solution.py:57
  149.8 15.0 %copy-start.15 = (f32[62]{0:T(128)}, f32[62]{0:T(128)S(1)}, u32[]{:S(2)}) copy-start(f32[62]{0:T(128)S(1)} %abs_reduce_fusion) | copy-start | bytes 748
  155.5 9.2 %collective-permute-start.6 = (f32[496,128]{0,1:T(8,128)S(1)}, f32[496,128]{0,1:T(8,128)S(1)}, u32[]{:S(2)}, u32[]{:S(2)}) collective-permute-start(f32[496,128]{0,1:T(8,128)S(1)} %bitcast.328), channel_id=1, source_target_pairs={{0,64},{64,0},{1,65},{65,1},{2,66},{66,2},{3,67},{67,3},{4,68},{68... | collective-permute-start | bytes 761864 | tf_op jit(solution)/shard_map/ppermute | solution.py:57
  159.2 12.5 %collective-permute-start.23 = (f32[2,496,128]{1,2,0:T(8,128)S(1)}, f32[2,496,128]{1,2,0:T(8,128)S(1)}, u32[]{:S(2)}, u32[]{:S(2)}) collective-permute-start(f32[2,496,128]{1,2,0:T(8,128)S(1)} %pad_maximum_fusion.10), channel_id=1, source_target_pairs={{0,48},{16,0},{32,16},{48,32},{1,49},{17,1},{33,17},{49,33},{2,50}... | collective-permute-start | bytes 1523720 | tf_op jit(solution)/shard_map/ppermute | solution.py:62
  160.8 14.3 %collective-permute-start.25 = (f32[2,496,128]{1,2,0:T(8,128)S(1)}, f32[2,496,128]{1,2,0:T(8,128)S(1)}, u32[]{:S(2)}, u32[]{:S(2)}) collective-permute-start(f32[2,496,128]{1,2,0:T(8,128)S(1)} %pad_maximum_fusion.10), channel_id=1, source_target_pairs={{0,16},{16,32},{32,48},{48,0},{1,17},{17,33},{33,49},{49,1},{2,18}... | collective-permute-start | bytes 1523720 | tf_op jit(solution)/shard_map/ppermute | solution.py:61
  164.8 18.1 %collective-permute-start.8 = (f32[2,496,128]{1,2,0:T(8,128)S(1)}, f32[2,496,128]{1,2,0:T(8,128)S(1)}, u32[]{:S(2)}, u32[]{:S(2)}) collective-permute-start(f32[2,496,128]{1,2,0:T(8,128)S(1)} %pad_maximum_fusion.6), channel_id=1, source_target_pairs={{0,48},{16,0},{32,16},{48,32},{1,49},{17,1},{33,17},{49,33},{2,50}... | collective-permute-start | bytes 1523720 | tf_op jit(solution)/shard_map/ppermute | solution.py:62
  167.2 18.6 %collective-permute-start.22 = (f32[2,496,128]{1,2,0:T(8,128)S(1)}, f32[2,496,128]{1,2,0:T(8,128)S(1)}, u32[]{:S(2)}, u32[]{:S(2)}) collective-permute-start(f32[2,496,128]{1,2,0:T(8,128)S(1)} %pad_maximum_fusion.10), channel_id=1, source_target_pairs={{0,8},{8,0},{1,9},{9,1},{2,10},{10,2},{3,11},{11,3},{4,12},{12,4},... | collective-permute-start | bytes 1523720 | tf_op jit(solution)/shard_map/ppermute | solution.py:107
  168.5 16.9 %collective-permute-start.10 = (f32[2,496,128]{1,2,0:T(8,128)S(1)}, f32[2,496,128]{1,2,0:T(8,128)S(1)}, u32[]{:S(2)}, u32[]{:S(2)}) collective-permute-start(f32[2,496,128]{1,2,0:T(8,128)S(1)} %pad_maximum_fusion.6), channel_id=1, source_target_pairs={{0,16},{16,32},{32,48},{48,0},{1,17},{17,33},{33,49},{49,1},{2,18}... | collective-permute-start | bytes 1523720 | tf_op jit(solution)/shard_map/ppermute | solution.py:61
  171.6 15.5 %collective-permute-start.7 = (f32[2,496,128]{1,2,0:T(8,128)S(1)}, f32[2,496,128]{1,2,0:T(8,128)S(1)}, u32[]{:S(2)}, u32[]{:S(2)}) collective-permute-start(f32[2,496,128]{1,2,0:T(8,128)S(1)} %pad_maximum_fusion.6), channel_id=1, source_target_pairs={{0,8},{8,0},{1,9},{9,1},{2,10},{10,2},{3,11},{11,3},{4,12},{12,4},... | collective-permute-start | bytes 1523720 | tf_op jit(solution)/shard_map/ppermute | solution.py:107
  175.1 15.1 %collective-permute-start.27 = (f32[496,128]{0,1:T(8,128)S(1)}, f32[496,128]{0,1:T(8,128)S(1)}, u32[]{:S(2)}, u32[]{:S(2)}) collective-permute-start(f32[496,128]{0,1:T(8,128)S(1)} %slice_bitcast_fusion), channel_id=1, source_target_pairs={{0,48},{16,0},{32,16},{48,32},{1,49},{17,1},{33,17},{49,33},{2,50}... | collective-permute-start | bytes 761864 | tf_op jit(solution)/shard_map/ppermute | solution.py:64
  182.9 9.1 %collective-permute-start.26 = (f32[496,128]{0,1:T(8,128)S(1)}, f32[496,128]{0,1:T(8,128)S(1)}, u32[]{:S(2)}, u32[]{:S(2)}) collective-permute-start(f32[496,128]{0,1:T(8,128)S(1)} %slice_bitcast_fusion.1), channel_id=1, source_target_pairs={{0,16},{16,32},{32,48},{48,0},{1,17},{17,33},{33,49},{49,1},{2,18}... | collective-permute-start | bytes 761864 | tf_op jit(solution)/shard_map/ppermute | solution.py:63
  185.4 10.6 %collective-permute-start.12 = (f32[496,128]{0,1:T(8,128)S(1)}, f32[496,128]{0,1:T(8,128)S(1)}, u32[]{:S(2)}, u32[]{:S(2)}) collective-permute-start(f32[496,128]{0,1:T(8,128)S(1)} %slice_bitcast_fusion.6), channel_id=1, source_target_pairs={{0,48},{16,0},{32,16},{48,32},{1,49},{17,1},{33,17},{49,33},{2,50}... | collective-permute-start | bytes 761864 | tf_op jit(solution)/shard_map/ppermute | solution.py:64
  185.9 10.3 %collective-permute-start.11 = (f32[496,128]{0,1:T(8,128)S(1)}, f32[496,128]{0,1:T(8,128)S(1)}, u32[]{:S(2)}, u32[]{:S(2)}) collective-permute-start(f32[496,128]{0,1:T(8,128)S(1)} %slice_bitcast_fusion.7), channel_id=1, source_target_pairs={{0,16},{16,32},{32,48},{48,0},{1,17},{17,33},{33,49},{49,1},{2,18}... | collective-permute-start | bytes 761864 | tf_op jit(solution)/shard_map/ppermute | solution.py:63
  187.1 11.7 %collective-permute-start.24 = (f32[2,496,128]{1,2,0:T(8,128)S(1)}, f32[2,496,128]{1,2,0:T(8,128)S(1)}, u32[]{:S(2)}, u32[]{:S(2)}) collective-permute-start(f32[2,496,128]{1,2,0:T(8,128)S(1)} %collective-permute-done.23), channel_id=1, source_target_pairs={{0,8},{8,0},{1,9},{9,1},{2,10},{10,2},{3,11},{11,3},{4,12},{12,4},... | collective-permute-start | bytes 1523720 | tf_op jit(solution)/shard_map/ppermute | solution.py:107
  190.2 8.9 %collective-permute-start.29 = (f32[2,496,128]{1,2,0:T(8,128)S(1)}, f32[2,496,128]{1,2,0:T(8,128)S(1)}, u32[]{:S(2)}, u32[]{:S(2)}) collective-permute-start(f32[2,496,128]{1,2,0:T(8,128)S(1)} %collective-permute-done.25), channel_id=1, source_target_pairs={{0,8},{8,0},{1,9},{9,1},{2,10},{10,2},{3,11},{11,3},{4,12},{12,4},... | collective-permute-start | bytes 1523720 | tf_op jit(solution)/shard_map/ppermute | solution.py:107
  192.0 7.2 %collective-permute-start.9 = (f32[2,496,128]{1,2,0:T(8,128)S(1)}, f32[2,496,128]{1,2,0:T(8,128)S(1)}, u32[]{:S(2)}, u32[]{:S(2)}) collective-permute-start(f32[2,496,128]{1,2,0:T(8,128)S(1)} %collective-permute-done.8), channel_id=1, source_target_pairs={{0,8},{8,0},{1,9},{9,1},{2,10},{10,2},{3,11},{11,3},{4,12},{12,4},... | collective-permute-start | bytes 1523720 | tf_op jit(solution)/shard_map/ppermute | solution.py:107
  196.1 3.2 %collective-permute-start.14 = (f32[2,496,128]{1,2,0:T(8,128)S(1)}, f32[2,496,128]{1,2,0:T(8,128)S(1)}, u32[]{:S(2)}, u32[]{:S(2)}) collective-permute-start(f32[2,496,128]{1,2,0:T(8,128)S(1)} %collective-permute-done.10), channel_id=1, source_target_pairs={{0,8},{8,0},{1,9},{9,1},{2,10},{10,2},{3,11},{11,3},{4,12},{12,4},... | collective-permute-start | bytes 1523720 | tf_op jit(solution)/shard_map/ppermute | solution.py:107
  196.2 7.4 %collective-permute-start.28 = (f32[2,496,128]{1,2,0:T(8,128)S(1)}, f32[2,496,128]{1,2,0:T(8,128)S(1)}, u32[]{:S(2)}, u32[]{:S(2)}) collective-permute-start(f32[2,496,128]{1,2,0:T(8,128)S(1)} %pad_maximum_fusion.11), channel_id=1, source_target_pairs={{0,8},{8,0},{1,9},{9,1},{2,10},{10,2},{3,11},{11,3},{4,12},{12,4},... | collective-permute-start | bytes 1523720 | tf_op jit(solution)/shard_map/ppermute | solution.py:107
  198.9 2.2 collective-permute-start.13
  (3 other events, 3.4 us)

commit v2 on v0

v2 whole, which is shorter than its diff:
```python
import functools

import jax
import jax.numpy as jnp
from jax import lax
from jax.experimental import pallas as pl
from jax.experimental.pallas import tpu as pltpu
from jax.sharding import Mesh, PartitionSpec as P

BLOCK = 2048
LANES = 128
N_YH, N_Z, N_CORE, N_YL, N_X = 2, 4, 2, 2, 4
N_TENSOR = N_YL * N_X
OWNERS = N_CORE * N_TENSOR
AXES = ("yh", "z", "core", "yl", "x")
DP = ("yh", "z", "core")
TENSOR = ("yl", "x")
ROW_OWNERS = ("yh", "core", "yl", "x")
PARTS = 2

beta_one = 0.9
beta_two = 0.999
adam_eps = 1e-08
learn_rate = 0.02
decay_rate = 0.1
scale_eps = 1e-06

SWAP = [(0, 1), (1, 0)]
UP = [(i, (i + 1) % N_Z) for i in range(N_Z)]
DOWN = [(i, (i - 1) % N_Z) for i in range(N_Z)]

ANY = pl.BlockSpec(memory_space=pl.ANY)
SMEM = pl.BlockSpec(memory_space=pltpu.SMEM)
VMEM = pl.BlockSpec(memory_space=pltpu.VMEM)
f32 = jnp.float32


def shape(*dims):
    return jax.ShapeDtypeStruct(dims, f32)


def params():
    return pltpu.CompilerParams(vmem_limit_bytes=40 * 2**20)


def lane_tile(yh, z):
    return pl.ds(pl.multiple_of((yh * N_Z + lax.rem(z, N_Z)) * LANES, LANES), LANES)


def lookup_kernel(m_codes, v_codes, m_scale, v_scale, code_m, code_v, m_out, v_out):
    rows = m_codes.shape[0]
    for codes, scale, table, out in ((m_codes, m_scale, code_m, m_out), (v_codes, v_scale, code_v, v_out)):
        for r in range(0, rows, 8):
            low = jnp.broadcast_to(table[0:1, :], (8, LANES))
            high = jnp.broadcast_to(table[1:2, :], (8, LANES))
            factor = scale[r : r + 8, :]
            for k in range(0, BLOCK, LANES):
                index = codes[r : r + 8, k : k + LANES]
                lane = index & (LANES - 1)
                a = jnp.take_along_axis(low, lane, axis=1)
                b = jnp.take_along_axis(high, lane, axis=1)
                out[r : r + 8, k : k + LANES] = jnp.where(index < LANES, a, b) * factor


def lookup(m_codes, v_codes, m_absmax, v_absmax, code_m, code_v):
    blocks = m_codes.shape[0]
    step = 32
    wide = pl.BlockSpec((step, BLOCK), lambda i: (i, 0))
    thin = pl.BlockSpec((step, 1), lambda i: (i, 0))
    table = pl.BlockSpec((2, LANES), lambda i: (0, 0))
    return pl.pallas_call(
        lookup_kernel,
        grid=(pl.cdiv(blocks, step),),
        in_specs=[wide, wide, thin, thin, table, table],
        out_specs=[wide, wide],
        out_shape=[shape(blocks, BLOCK)] * 2,
        compiler_params=params(),
        name="lookup",
    )(m_codes, v_codes, m_absmax[:, None], v_absmax[:, None], code_m.reshape(2, LANES), code_v.reshape(2, LANES))


def spread_kernel(half, width, m_in, v_in, m_out, v_out):
    for src, dst in ((m_in, m_out), (v_in, v_out)):
        for part in range(PARTS):
            for owner in range(OWNERS):
                c, j = divmod(owner, N_TENSOR)
                at = j * N_CORE * half + c * half + part * width
                dst[part, owner] = src[:, at : at + width]


def collect_kernel(half, width, *refs):
    ins, outs = refs[: 2 * PARTS], refs[2 * PARTS :]
    for which, dst in enumerate(outs):
        for part in range(PARTS):
            for owner in range(OWNERS):
                c, j = divmod(owner, N_TENSOR)
                at = j * N_CORE * half + c * half + part * width
                dst[:, at : at + width] = ins[which * PARTS + part][owner]


def slice_kernel(part, width, side, place, grad, out, sem):
    c = place[0] if side == 0 else 1 - place[0]
    at = pl.multiple_of(c * (width * PARTS) + part * width, 8)
    copy = pltpu.make_async_copy(grad.at[pl.ds(at, width)], out, sem)
    copy.start()
    copy.wait()


def take_slice(place, grad_t, part, width, side):
    return pl.pallas_call(
        functools.partial(slice_kernel, part, width, side),
        in_specs=[SMEM, ANY],
        out_specs=VMEM,
        out_shape=shape(width, grad_t.shape[1]),
        scratch_shapes=[pltpu.SemaphoreType.DMA],
        compiler_params=params(),
        name="take_slice",
    )(place, grad_t)


def pack_kernel(place, own, other, up, down, keep):
    z = place[1]
    picks = (
        (up, 0, 0, z + 2),
        (up, 1, 1, z + 1),
        (down, 0, 1, z + 2),
        (down, 1, 0, z + 3),
        (keep, 0, 0, z + 1),
        (keep, 1, 1, z + 3),
        (keep, 2, 0, z),
        (keep, 3, 1, z),
    )
    for dst, slot, yh, to in picks:
        lanes = lane_tile(yh, to)
        dst[slot] = own[:, lanes] + other[:, lanes]


def relay_kernel(keep, up, down, up2, down2, rest):
    up2[...] = keep[0] + up[0]
    down2[...] = keep[1] + down[0]
    rest[0] = keep[2] + down[1]
    rest[1] = keep[3] + up[1]


def turn_kernel(width, rest, up2, down2, out, held):
    for yh, last in enumerate((up2, down2)):
        held[0:width, :] = rest[yh] + last[...]
        out[yh * LANES : (yh + 1) * LANES, :] = held[...].T[:, :width]


def reduce_part(place, grad_t, part, width):
    rows = grad_t.shape[1]
    send = take_slice(place, grad_t, part, width, 1)
    other = lax.ppermute(send, "core", SWAP)
    own = take_slice(place, grad_t, part, width, 0)
    up, down, keep = pl.pallas_call(
        pack_kernel,
        in_specs=[SMEM, VMEM, VMEM],
        out_specs=[VMEM] * 3,
        out_shape=[shape(2, width, LANES), shape(2, width, LANES), shape(4, width, LANES)],
        compiler_params=params(),
        name="pack",
    )(place, own, other)
    up = lax.ppermute(up, "z", UP)
    down = lax.ppermute(down, "z", DOWN)
    up2, down2, rest = pl.pallas_call(
        relay_kernel,
        in_specs=[VMEM] * 3,
        out_specs=[VMEM] * 3,
        out_shape=[shape(width, LANES), shape(width, LANES), shape(2, width, LANES)],
        compiler_params=params(),
        name="relay",
    )(keep, up, down)
    up2 = lax.ppermute(up2, "z", UP)
    down2 = lax.ppermute(down2, "z", DOWN)
    turned = pl.pallas_call(
        functools.partial(turn_kernel, width),
        in_specs=[VMEM] * 3,
        out_specs=VMEM,
        out_shape=shape(N_YH * LANES, width),
        scratch_shapes=[pltpu.VMEM((pl.cdiv(width, LANES) * LANES, LANES), f32)],
        compiler_params=params(),
        name="turn",
    )(rest, up2, down2)
    sent = turned.reshape(N_YH * OWNERS, -1, width)
    return lax.all_to_all(sent, ROW_OWNERS, split_axis=0, concat_axis=0, tiled=True)


def adam_kernel(fixes, grads, m_old, v_old, m_out, v_out, update):
    grad = grads[:OWNERS] + grads[OWNERS:]
    m_new = beta_one * m_old[...] + (1.0 - beta_one) * grad
    v_new = beta_two * v_old[...] + (1.0 - beta_two) * grad * grad
    m_out[...] = m_new
    v_out[...] = v_new
    step = m_new / fixes[0] / (jnp.sqrt(v_new / fixes[1]) + adam_eps)
    update[:OWNERS] = step
    update[OWNERS:] = step


def adam(fixes, grads, m_old, v_old):
    return pl.pallas_call(
        adam_kernel,
        in_specs=[SMEM, VMEM, VMEM, VMEM],
        out_specs=[VMEM] * 3,
        out_shape=[shape(*m_old.shape), shape(*m_old.shape), shape(*grads.shape)],
        compiler_params=params(),
        name="adam",
    )(fixes, grads, m_old, v_old)


def unturn_kernel(width, rows, out, held):
    for yh in range(N_YH):
        held[:, 0:width] = rows[yh * LANES : (yh + 1) * LANES, :]
        out[yh] = held[...].T[:width, :]


def gather_part(update, width):
    back = lax.all_to_all(update, ROW_OWNERS, split_axis=0, concat_axis=0, tiled=True)
    near = pl.pallas_call(
        functools.partial(unturn_kernel, width),
        in_specs=[VMEM],
        out_specs=VMEM,
        out_shape=shape(N_YH, width, LANES),
        scratch_shapes=[pltpu.VMEM((LANES, pl.cdiv(width, LANES) * LANES), f32)],
        compiler_params=params(),
        name="unturn",
    )(back.reshape(N_YH * LANES, width))
    up = lax.ppermute(near, "z", UP)
    down = lax.ppermute(near, "z", DOWN)
    up2 = lax.ppermute(up[0], "z", UP)
    down2 = lax.ppermute(down[1], "z", DOWN)
    own = [near, up, down, up2, down2]
    return own + [lax.ppermute(g, "core", SWAP) for g in own]


def weight_kernel(part, width, place, weight, *refs):
    pieces, (out, held, in_sem, out_sem) = refs[:10], refs[-4:]
    c, z = place[0], place[1]

    def rows(side):
        core = c if side == 0 else 1 - c
        return pl.ds(pl.multiple_of(core * (width * PARTS) + part * width, 8), width)

    loads = [pltpu.make_async_copy(weight.at[rows(s)], held.at[s], in_sem.at[s]) for s in range(2)]
    stores = [pltpu.make_async_copy(held.at[s], out.at[rows(s)], out_sem.at[s]) for s in range(2)]
    for load in loads:
        load.start()
    for side in range(2):
        near, up, down, up2, down2 = pieces[5 * side : 5 * side + 5]
        loads[side].wait()
        for yh in range(N_YH):
            far = (up2, down2)[yh]
            for piece, at in ((near.at[yh], z), (up.at[yh], z + 3), (down.at[yh], z + 1), (far, z + 2)):
                lanes = lane_tile(yh, at)
                old = held[side, :, lanes]
                held[side, :, lanes] = old - learn_rate * (piece[...] + decay_rate * old)
        stores[side].start()
    for store in stores:
        store.wait()


def write_weight(place, weight_t, pieces, so_far, part, width):
    done = [] if so_far is None else [so_far]
    return pl.pallas_call(
        functools.partial(weight_kernel, part, width),
        in_specs=[SMEM, ANY] + [VMEM] * 10 + [ANY] * len(done),
        out_specs=ANY,
        out_shape=shape(*weight_t.shape),
        input_output_aliases={12: 0} if done else {},
        scratch_shapes=[
            pltpu.VMEM((2, width, weight_t.shape[1]), f32),
            pltpu.SemaphoreType.DMA((2,)),
            pltpu.SemaphoreType.DMA((2,)),
        ],
        compiler_params=params(),
        name="write_weight",
    )(place, weight_t, *pieces, *done)


def shards(weight, grad_parts, m_codes, v_codes, m_absmax, v_absmax, code_m, code_v, step):
    columns = weight.shape[1]
    half = columns // N_CORE
    width = half // PARTS
    dev_rows = LANES // OWNERS
    place = jnp.stack([lax.axis_index("core"), lax.axis_index("z")]).astype(jnp.int32)
    grad_t = grad_parts[0].T
    weight_t = weight.T
    count = step[0].astype(f32)
    fix_one = 1.0 - jnp.power(f32(beta_one), count)
    fix_two = 1.0 - jnp.power(f32(beta_two), count)
    fixes = jnp.stack([fix_one, fix_two])

    m_old, v_old = lookup(m_codes, v_codes, m_absmax, v_absmax, code_m, code_v)
    flat = (dev_rows, columns * N_TENSOR)
    m_old, v_old = pl.pallas_call(
        functools.partial(spread_kernel, half, width),
        in_specs=[VMEM] * 2,
        out_specs=[VMEM] * 2,
        out_shape=[shape(PARTS, OWNERS, dev_rows, width)] * 2,
        compiler_params=params(),
        name="spread",
    )(m_old.reshape(flat), v_old.reshape(flat))

    m_parts, v_parts, gathered = [], [], []
    for part in range(PARTS):
        grads = reduce_part(place, grad_t, part, width)
        m_new, v_new, update = adam(fixes, grads, m_old[part], v_old[part])
        m_parts.append(m_new)
        v_parts.append(v_new)
        gathered.append(gather_part(update, width))

    new_weight = None
    for part in range(PARTS):
        new_weight = write_weight(place, weight_t, gathered[part], new_weight, part, width)

    m_new, v_new = pl.pallas_call(
        functools.partial(collect_kernel, half, width),
        in_specs=[VMEM] * (2 * PARTS),
        out_specs=[VMEM] * 2,
        out_shape=[shape(*flat)] * 2,
        compiler_params=params(),
        name="collect",
    )(*m_parts, *v_parts)
    m_new = m_new.reshape(-1, BLOCK)
    v_new = v_new.reshape(-1, BLOCK)
    m_absmax_new = jnp.max(jnp.abs(m_new), axis=1)
    v_absmax_new = jnp.max(v_new, axis=1)
    m_scaled = (m_new / (m_absmax_new[:, None] + scale_eps)).astype(jnp.bfloat16)
    v_scaled = (v_new / (v_absmax_new[:, None] + scale_eps)).astype(jnp.bfloat16)
    return (new_weight.T, m_scaled, v_scaled, m_absmax_new, v_absmax_new)


def solution(mesh):
    fine = Mesh(mesh.devices.reshape(N_YH, N_Z, N_CORE, N_YL, N_X), AXES)
    blocks = P(DP + TENSOR)
    in_specs = (P(None, TENSOR), P(DP, None, TENSOR), blocks, blocks, blocks, blocks, P(), P(), P())
    out_specs = (P(None, TENSOR), blocks, blocks, blocks, blocks)
    return jax.shard_map(shards, mesh=fine, in_specs=in_specs, out_specs=out_specs, check_vma=False)
```

time: 256 us -> 180 us (0.70)
  waiting for transfers between devices: 167 us -> 66.6 us
  starting transfers between devices: 4.09 us -> 57.6 us
  Pallas kernels: 0 us -> 25.1 us
  between operations: 14.9 us -> 1.95 us
  blocking collectives: 12.9 us -> 0 us
  matrix products: 11.1 us -> 0 us
  other arithmetic: 14.5 us -> 5.22 us
  local copies, waits for them, and re-layouts: 30.2 us -> 22.6 us
    reduce_scatter x1 -> x0, waiting for transfers between devices: 103 us -> none  [shards(): lax.psum_scatter(partial_value, 'dp', scatter_dimension=0, tiled=True)]
    all_gather x1 -> x0, waiting for transfers between devices: 63.9 us -> none  [shards(): mine = lax.all_gather(columns, 'dp', axis=0, tiled=True)]
    ppermute x0 -> x28, waiting for transfers between devices: none -> 45.1 us  [the longest x2 19.5 us: reduce_part(): up2 = lax.ppermute(up2, 'z', UP)]
    ppermute x0 -> x28, starting transfers between devices: none -> 33.6 us  [the longest x10 7.48 us: gather_part(): return own + [lax.ppermute(g, 'core', SWAP) for g in own]]
    pallas_call x0 -> x19, Pallas kernels: none -> 25.1 us  [the longest x2 9.45 us: write_weight(): pl.pallas_call(functools.partial(weight_kernel, part, width), in_specs=[S...]
    all_to_all x1 -> x4, waiting for transfers between devices: 0.01 us -> 21.4 us  [the longest x2 17.4 us: gather_part(): lax.all_to_all(update, ROW_OWNERS, split_axis=0, concat_axis=0, tiled=True)]
    all_to_all x1 -> x4, starting transfers between devices: 4.01 us -> 23.9 us  [the longest x2 16 us: reduce_part(): lax.all_to_all(sent, ROW_OWNERS, split_axis=0, concat_axis=0, tiled=True)]
    all_to_all x1 -> x0, blocking collectives: 12.9 us -> none  [shards(): lax.all_to_all(update, 'tensor', split_axis=1, concat_axis=0, tiled=True)]
  transfers between devices with their start and end apart: 3 -> 32, of which waited for: 2 -> 12; matrix products, arithmetic and copies ran while one was open for 9% -> 6% of each run, Pallas kernels for 0% -> 11%
where the time goes in v2:
time: 180 us; the launch traced here: 179 us
  waiting for transfers between devices  66.6 us (37%)
  starting transfers between devices  57.6 us (32%)
  Pallas kernels  25.1 us (14%)
  local copies, waits for them, and re-layouts  22.6 us (13%)
  other arithmetic  5.22 us (3%)
  between operations  1.95 us (1%)
    ppermute x2, waiting for transfers between devices, reduce_part(): up2 = lax.ppermute(up2, 'z', UP)  19.5 us
    all_to_all x2, waiting for transfers between devices, gather_part(): lax.all_to_all(update, ROW_OWNERS, split_axis=0, concat_axis=0, tiled=True)  17.4 us
    unnamed x54, local copies, waits for them, and re-layouts  17 us
    all_to_all x2, starting transfers between devices, reduce_part(): lax.all_to_all(sent, ROW_OWNERS, split_axis=0, concat_axis=0, tiled=True)  16 us
    ppermute x2, waiting for transfers between devices, gather_part(): up = lax.ppermute(near, 'z', UP)  14.5 us
    pallas_call x2, Pallas kernels, write_weight(): pl.pallas_call(functools.partial(weight_kernel, part, width), in_specs=[S...  9.45 us
    all_to_all x2, starting transfers between devices, gather_part(): lax.all_to_all(update, ROW_OWNERS, split_axis=0, concat_axis=0, tiled=True)  7.97 us
    ppermute x10, starting transfers between devices, gather_part(): return own + [lax.ppermute(g, 'core', SWAP) for g in own]  7.48 us
  transfers between devices with their start and end apart: 32, of which 12 were waited for; matrix products, arithmetic and copies ran while one was open for 6% of the time, Pallas kernels for 11%

profile of v2, /device:TPU:1, one launch (start us, length us, event | category | flops | bytes accessed | tf_op | source)
XLA Modules:
  0.0 179.0 jit_solution(8962784633125481534)
XLA Ops:
  0.7 3.3 %copy-done = f32[1,1024,1984]{1,2,0:T(8,128)S(1)} copy-done((f32[1,1024,1984]{1,2,0:T(8,128)S(1)}, f32[1,1024,1984]{1,2,0:T(8,128)}, u32[]{:S(2)}) %copy-start) | copy-done | bytes 8126488
  5.0 1.5 collective-permute-start
  8.5 1.8 %collective-permute-done.other = f32[496,1024]{1,0:T(8,128)} collective-permute-done((f32[496,1024]{1,0:T(8,128)S(1)}, f32[496,1024]{1,0:T(8,128)}, u32[]{:S(2)}, u32[]{:S(2)}) %collective-permute-start) | collective-permute-done | bytes 2031648 | tf_op jit(solution)/shard_map/ppermute | solution.py:154
  10.3 2.1 %pack.2 = (f32[2,496,128]{2,1,0:T(8,128)S(1)}, f32[2,496,128]{2,1,0:T(8,128)S(1)}, f32[4,496,128]{2,1,0:T(8,128)S(1)}) custom-call(s32[2]{0:T(128)S(1)} %pad_add_fusion.place, f32[496,1024]{1,0:T(8,128)S(1)} %take_slice.4.own, f32[496,1024]{1,0:T(8,128)} %collective-permute-done.other), custom_call_target="tpu_custom_call" | custom-call | tf_op jit(solution)/shard_map/pack/pallas_call | solution.py:156
  12.4 1.8 collective-permute-start.1
  14.2 2.2 %collective-permute-start.2 = (f32[2,496,128]{2,1,0:T(8,128)S(1)}, f32[2,496,128]{2,1,0:T(8,128)S(1)}, u32[]{:S(2)}, u32[]{:S(2)}) collective-permute-start(f32[2,496,128]{2,1,0:T(8,128)S(1)} %get-tuple-element.31), channel_id=1, source_target_pairs={{0,48},{16,0},{32,16},{48,32},{1,49},{17,1},{33,17},{49,33},{2,50}... | collective-permute-start | bytes 1523720 | tf_op jit(solution)/shard_map/ppermute | solution.py:165
  17.4 2.0 %pack.3 = (f32[2,496,128]{2,1,0:T(8,128)}, f32[2,496,128]{2,1,0:T(8,128)}, f32[4,496,128]{2,1,0:T(8,128)S(1)}) custom-call(s32[2]{0:T(128)S(1)} %pad_add_fusion.place, f32[496,1024]{1,0:T(8,128)S(1)} %take_slice.6.own, f32[496,1024]{1,0:T(8,128)S(1)} %collective-permute-done.14.other), custom_call_target="tpu_custom_call" | custom-call | tf_op jit(solution)/shard_map/pack/pallas_call | solution.py:156
  19.4 1.0 copy-done.2
  20.4 2.7 %collective-permute-start.16 = (f32[2,496,128]{2,1,0:T(8,128)}, f32[2,496,128]{2,1,0:T(8,128)S(1)}, u32[]{:S(2)}, u32[]{:S(2)}) collective-permute-start(f32[2,496,128]{2,1,0:T(8,128)} %get-tuple-element.42), channel_id=1, source_target_pairs={{0,48},{16,0},{32,16},{48,32},{1,49},{17,1},{33,17},{49,33},{2,50}... | collective-permute-start | bytes 1523720 | tf_op jit(solution)/shard_map/ppermute | solution.py:165
  23.0 4.9 %collective-permute-done.1.up = f32[2,496,128]{2,1,0:T(8,128)S(1)} collective-permute-done((f32[2,496,128]{2,1,0:T(8,128)S(1)}, f32[2,496,128]{2,1,0:T(8,128)S(1)}, u32[]{:S(2)}, u32[]{:S(2)}) %collective-permute-start.1) | collective-permute-done | bytes 507936 | tf_op jit(solution)/shard_map/ppermute | solution.py:164
  28.5 2.3 %collective-permute-start.4 = (f32[496,128]{1,0:T(8,128)S(1)}, f32[496,128]{1,0:T(8,128)S(1)}, u32[]{:S(2)}, u32[]{:S(2)}) collective-permute-start(f32[496,128]{1,0:T(8,128)S(1)} %get-tuple-element.34), channel_id=1, source_target_pairs={{0,48},{16,0},{32,16},{48,32},{1,49},{17,1},{33,17},{49,33},{2,50}... | collective-permute-start | bytes 761864 | tf_op jit(solution)/shard_map/ppermute | solution.py:175
  30.8 13.5 %collective-permute-done.3.up2 = f32[496,128]{1,0:T(8,128)S(1)} collective-permute-done((f32[496,128]{1,0:T(8,128)S(1)}, f32[496,128]{1,0:T(8,128)S(1)}, u32[]{:S(2)}, u32[]{:S(2)}) %collective-permute-start.3) | collective-permute-done | bytes 253984 | tf_op jit(solution)/shard_map/ppermute | solution.py:174
  44.3 1.0 turn.2
  45.3 8.0 %all-to-all-start = ((f32[32,8,496]{2,1,0:T(8,128)}), f32[32,8,496]{2,1,0:T(8,128)S(1)}, u32[]{:S(2)}, u32[]{:S(2)}) async-start(f32[32,8,496]{2,1,0:T(8,128)} %bitcast.6), calls=%async_computation | async-start | bytes 1048576 | tf_op jit(solution)/shard_map/all_to_all | solution.py:186
  54.1 1.0 copy-done.11
  55.3 1.0 collective-permute-start.17
  56.3 1.9 %collective-permute-start.18 = (f32[496,128]{1,0:T(8,128)S(1)}, f32[496,128]{1,0:T(8,128)S(1)}, u32[]{:S(2)}, u32[]{:S(2)}) collective-permute-start(f32[496,128]{1,0:T(8,128)S(1)} %get-tuple-element.45), channel_id=1, source_target_pairs={{0,48},{16,0},{32,16},{48,32},{1,49},{17,1},{33,17},{49,33},{2,50}... | collective-permute-start | bytes 761864 | tf_op jit(solution)/shard_map/ppermute | solution.py:175
  58.2 6.0 %collective-permute-done.17.up2 = f32[496,128]{1,0:T(8,128)S(1)} collective-permute-done((f32[496,128]{1,0:T(8,128)S(1)}, f32[496,128]{1,0:T(8,128)S(1)}, u32[]{:S(2)}, u32[]{:S(2)}) %collective-permute-start.17) | collective-permute-done | bytes 253984 | tf_op jit(solution)/shard_map/ppermute | solution.py:174
  64.2 1.0 turn.3
  65.2 8.0 %all-to-all-start.2 = ((f32[32,8,496]{2,1,0:T(8,128)}), f32[32,8,496]{2,1,0:T(8,128)S(1)}, u32[]{:S(2)}, u32[]{:S(2)}) async-start(f32[32,8,496]{2,1,0:T(8,128)} %bitcast.16), calls=%async_computation.2 | async-start | bytes 1048576 | tf_op jit(solution)/shard_map/all_to_all | solution.py:186
  74.2 1.4 lookup.1
  76.4 1.3 reshape.62.m_in
  78.5 1.5 adam.2
  80.7 4.1 %all-to-all-done.2.grads = f32[32,8,496]{2,1,0:T(8,128)S(1)} async-done(((f32[32,8,496]{2,1,0:T(8,128)}), f32[32,8,496]{2,1,0:T(8,128)S(1)}, u32[]{:S(2)}, u32[]{:S(2)}) %all-to-all-start.2) | async-done | bytes 507936 | tf_op jit(solution)/shard_map/all_to_all | solution.py:186
  84.8 4.0 %all-to-all-start.1 = ((f32[32,8,496]{2,1,0:T(8,128)}), f32[32,8,496]{2,1,0:T(8,128)S(1)}, u32[]{:S(2)}, u32[]{:S(2)}) async-start(f32[32,8,496]{2,1,0:T(8,128)} %get-tuple-element.39), calls=%async_computation.1 | async-start | bytes 1048576 | tf_op jit(solution)/shard_map/all_to_all | solution.py:218
  88.8 1.5 adam.3
  91.7 8.7 %all-to-all-done.1 = f32[32,8,496]{2,1,0:T(8,128)S(1)} async-done(((f32[32,8,496]{2,1,0:T(8,128)}), f32[32,8,496]{2,1,0:T(8,128)S(1)}, u32[]{:S(2)}, u32[]{:S(2)}) %all-to-all-start.1) | async-done | bytes 507936 | tf_op jit(solution)/shard_map/all_to_all | solution.py:218
  100.4 4.0 %all-to-all-start.3 = ((f32[32,8,496]{2,1,0:T(8,128)}), f32[32,8,496]{2,1,0:T(8,128)S(1)}, u32[]{:S(2)}, u32[]{:S(2)}) async-start(f32[32,8,496]{2,1,0:T(8,128)} %get-tuple-element.46), calls=%async_computation.3 | async-start | bytes 1048576 | tf_op jit(solution)/shard_map/all_to_all | solution.py:218
  104.6 2.8 %collective-permute-start.6 = (f32[2,496,128]{2,1,0:T(8,128)S(1)}, f32[2,496,128]{2,1,0:T(8,128)S(1)}, u32[]{:S(2)}, u32[]{:S(2)}) collective-permute-start(f32[2,496,128]{2,1,0:T(8,128)S(1)} %unturn.2.refs_0_), channel_id=1, source_target_pairs={{0,48},{16,0},{32,16},{48,32},{1,49},{17,1},{33,17},{49,33},{2,50}... | collective-permute-start | bytes 1523720 | tf_op jit(solution)/shard_map/ppermute | solution.py:229
  107.5 8.6 %all-to-all-done.3 = f32[32,8,496]{2,1,0:T(8,128)S(1)} async-done(((f32[32,8,496]{2,1,0:T(8,128)}), f32[32,8,496]{2,1,0:T(8,128)S(1)}, u32[]{:S(2)}, u32[]{:S(2)}) %all-to-all-start.3) | async-done | bytes 507936 | tf_op jit(solution)/shard_map/all_to_all | solution.py:218
  116.3 2.8 %collective-permute-start.20 = (f32[2,496,128]{2,1,0:T(8,128)S(1)}, f32[2,496,128]{2,1,0:T(8,128)S(1)}, u32[]{:S(2)}, u32[]{:S(2)}) collective-permute-start(f32[2,496,128]{2,1,0:T(8,128)S(1)} %unturn.3.refs_0_), channel_id=1, source_target_pairs={{0,48},{16,0},{32,16},{48,32},{1,49},{17,1},{33,17},{49,33},{2,50}... | collective-permute-start | bytes 1523720 | tf_op jit(solution)/shard_map/ppermute | solution.py:229
  122.3 1.0 reshape.67
  123.3 1.2 abs_reduce_fusion
  125.6 3.0 %collective-permute-start.8 = (f32[496,128]{1,0:T(8,128)S(1)}, f32[496,128]{1,0:T(8,128)}, u32[]{:S(2)}, u32[]{:S(2)}) collective-permute-start(f32[496,128]{1,0:T(8,128)S(1)} %slice_bitcast_fusion.6), channel_id=1, source_target_pairs={{0,48},{16,0},{32,16},{48,32},{1,49},{17,1},{33,17},{49,33},{2,50}... | collective-permute-start | bytes 761864 | tf_op jit(solution)/shard_map/ppermute | solution.py:231
  128.5 1.1 collective-permute-done.20.refs_2_
  129.7 3.5 %collective-permute-start.22 = (f32[496,128]{1,0:T(8,128)S(1)}, f32[496,128]{1,0:T(8,128)S(1)}, u32[]{:S(2)}, u32[]{:S(2)}) collective-permute-start(f32[496,128]{1,0:T(8,128)S(1)} %slice_bitcast_fusion.4), channel_id=1, source_target_pairs={{0,48},{16,0},{32,16},{48,32},{1,49},{17,1},{33,17},{49,33},{2,50}... | collective-permute-start | bytes 761864 | tf_op jit(solution)/shard_map/ppermute | solution.py:231
  133.2 3.8 %collective-permute-done.19.refs_1_ = f32[2,496,128]{2,1,0:T(8,128)S(1)} collective-permute-done((f32[2,496,128]{2,1,0:T(8,128)S(1)}, f32[2,496,128]{2,1,0:T(8,128)S(1)}, u32[]{:S(2)}, u32[]{:S(2)}) %collective-permute-start.19) | collective-permute-done | bytes 507936 | tf_op jit(solution)/shard_map/ppermute | solution.py:228
  137.1 10.8 %collective-permute-done.5.refs_1_ = f32[2,496,128]{2,1,0:T(8,128)S(1)} collective-permute-done((f32[2,496,128]{2,1,0:T(8,128)S(1)}, f32[2,496,128]{2,1,0:T(8,128)S(1)}, u32[]{:S(2)}, u32[]{:S(2)}) %collective-permute-start.5) | collective-permute-done | bytes 507936 | tf_op jit(solution)/shard_map/ppermute | solution.py:228
  147.8 2.7 %collective-permute-start.25 = (f32[2,496,128]{2,1,0:T(8,128)S(1)}, f32[2,496,128]{2,1,0:T(8,128)}, u32[]{:S(2)}, u32[]{:S(2)}) collective-permute-start(f32[2,496,128]{2,1,0:T(8,128)S(1)} %collective-permute-done.20.refs_2_), channel_id=1, source_target_pairs={{0,8},{8,0},{1,9},{9,1},{2,10},{10,2},{3,11},{11,3},{4,12},{12,4},... | collective-permute-start | bytes 1523720 | tf_op jit(solution)/shard_map/ppermute | solution.py:233
  153.4 1.5 collective-permute-start.26
  155.7 2.0 %reshape.68 = f32[62,2048]{1,0:T(8,128)} reshape(f32[8,15872]{1,0:T(8,128)} %copy-done.9) | data formatting | bytes 1015808 | tf_op jit(solution)/shard_map/reshape | solution.py:325
  157.8 1.2 reduce_max.19
  159.0 2.4 %collective-permute-done.7.refs_3_ = f32[496,128]{1,0:T(8,128)} collective-permute-done((f32[496,128]{1,0:T(8,128)}, f32[496,128]{1,0:T(8,128)}, u32[]{:S(2)}, u32[]{:S(2)}) %collective-permute-start.7) | collective-permute-done | bytes 253984 | tf_op jit(solution)/shard_map/ppermute | solution.py:230
  163.1 1.8 %divide_convert_fusion = bf16[62,2048]{1,0:T(8,128)(2,1)} fusion(f32[62,2048]{1,0:T(8,128)} %reshape.68, f32[62]{0:T(128)S(1)} %broadcast_add_fusion), kind=kLoop, calls=%fused_computation | loop fusion | flops 253952 | bytes 762104 | tf_op jit(solution)/shard_map/convert_element_type | solution.py:329
  165.0 3.3 %copy-done.1 = f32[1024,1984]{0,1:T(8,128)S(1)} copy-done((f32[1024,1984]{0,1:T(8,128)S(1)}, f32[1024,1984]{0,1:T(8,128)}, u32[]{:S(2)}) %copy-start.1) | copy-done | bytes 8126488
  168.3 1.0 copy-done.8
  169.3 4.9 %write_weight.2.refs_10_ = f32[1984,1024]{1,0:T(8,128)} custom-call(s32[2]{0:T(128)S(1)} %pad_add_fusion.place, f32[1984,1024]{1,0:T(8,128)S(1)} %bitcast.37, f32[2,496,128]{2,1,0:T(8,128)S(1)} %unturn.3.refs_0_, f32[2,496,128]{2,1,0:T(8,128)S(1)} %collective-permute-done.19.refs_1_, f32[2,496,128]{2,1,0:T(8,128)S(1)} %collective-permute-done.20.refs_2_, ...), custom_call_target="tpu_custom_call" | custom-call | tf_op jit(solution)/shard_map/write_weight/pallas_call | solution.py:264
  174.3 4.5 %write_weight.3 = f32[1984,1024]{1,0:T(8,128)} custom-call(s32[2]{0:T(128)S(1)} %pad_add_fusion.place, f32[1984,1024]{1,0:T(8,128)S(1)} %bitcast.38, f32[2,496,128]{2,1,0:T(8,128)S(1)} %unturn.2.refs_0_, f32[2,496,128]{2,1,0:T(8,128)S(1)} %collective-permute-done.5.refs_1_, ...), custom_call_target="tpu_custom_call", output_to_operand_aliasing={{}: (12, {})} | custom-call | tf_op jit(solution)/shard_map/write_weight/pallas_call | solution.py:264
  (109 shorter events, 19.4 us)
Async XLA Ops:
  0.7 3.3 %copy-start = (f32[1,1024,1984]{1,2,0:T(8,128)S(1)}, f32[1,1024,1984]{1,2,0:T(8,128)}, u32[]{:S(2)}) copy-start(f32[1,1024,1984]{1,2,0:T(8,128)} %param.10) | copy-start | bytes 24379396
  5.0 5.3 %collective-permute-start = (f32[496,1024]{1,0:T(8,128)S(1)}, f32[496,1024]{1,0:T(8,128)}, u32[]{:S(2)}, u32[]{:S(2)}) collective-permute-start(f32[496,1024]{1,0:T(8,128)S(1)} %take_slice.5), channel_id=1, source_target_pairs={{0,8},{8,0},{1,9},{9,1},{2,10},{10,2},{3,11},{11,3},{4,12},{12,4},... | collective-permute-start | bytes 6094856 | tf_op jit(solution)/shard_map/ppermute | solution.py:154
  6.5 9.9 %slice-start = ((s8[8126464]{0:T(1024)(128)(4,1)}), s8[4194304]{0:T(1024)(128)(4,1)S(1)}, s32[]{:S(2)}) async-start(s8[8126464]{0:T(1024)(128)(4,1)} %bitcast.34), calls=%async_computation.4 | async-start | bytes 8388608
  7.4 9.0 %slice-start.1 = ((s8[8126464]{0:T(1024)(128)(4,1)}), s8[3932160]{0:T(1024)(128)(4,1)S(1)}, s32[]{:S(2)}) async-start(s8[8126464]{0:T(1024)(128)(4,1)} %bitcast.34), calls=%async_computation.5 | async-start | bytes 7864320
  7.4 9.9 %collective-permute-start.14 = (f32[496,1024]{1,0:T(8,128)S(1)}, f32[496,1024]{1,0:T(8,128)S(1)}, u32[]{:S(2)}, u32[]{:S(2)}) collective-permute-start(f32[496,1024]{1,0:T(8,128)S(1)} %take_slice.7), channel_id=1, source_target_pairs={{0,8},{8,0},{1,9},{9,1},{2,10},{10,2},{3,11},{11,3},{4,12},{12,4},... | collective-permute-start | bytes 6094856 | tf_op jit(solution)/shard_map/ppermute | solution.py:154
  12.4 15.6 %collective-permute-start.1 = (f32[2,496,128]{2,1,0:T(8,128)S(1)}, f32[2,496,128]{2,1,0:T(8,128)S(1)}, u32[]{:S(2)}, u32[]{:S(2)}) collective-permute-start(f32[2,496,128]{2,1,0:T(8,128)S(1)} %get-tuple-element.30), channel_id=1, source_target_pairs={{0,16},{16,32},{32,48},{48,0},{1,17},{17,33},{33,49},{49,1},{2,18}... | collective-permute-start | bytes 1523720 | tf_op jit(solution)/shard_map/ppermute | solution.py:164
  14.2 13.8 %collective-permute-start.2 = (f32[2,496,128]{2,1,0:T(8,128)S(1)}, f32[2,496,128]{2,1,0:T(8,128)S(1)}, u32[]{:S(2)}, u32[]{:S(2)}) collective-permute-start(f32[2,496,128]{2,1,0:T(8,128)S(1)} %get-tuple-element.31), channel_id=1, source_target_pairs={{0,48},{16,0},{32,16},{48,32},{1,49},{17,1},{33,17},{49,33},{2,50}... | collective-permute-start | bytes 1523720 | tf_op jit(solution)/shard_map/ppermute | solution.py:165
  20.4 32.9 %collective-permute-start.15 = (f32[2,496,128]{2,1,0:T(8,128)}, f32[2,496,128]{2,1,0:T(8,128)S(1)}, u32[]{:S(2)}, u32[]{:S(2)}) collective-permute-start(f32[2,496,128]{2,1,0:T(8,128)} %get-tuple-element.41), channel_id=1, source_target_pairs={{0,16},{16,32},{32,48},{48,0},{1,17},{17,33},{33,49},{49,1},{2,18}... | collective-permute-start | bytes 1523720 | tf_op jit(solution)/shard_map/ppermute | solution.py:164
  20.4 32.9 %collective-permute-start.16 = (f32[2,496,128]{2,1,0:T(8,128)}, f32[2,496,128]{2,1,0:T(8,128)S(1)}, u32[]{:S(2)}, u32[]{:S(2)}) collective-permute-start(f32[2,496,128]{2,1,0:T(8,128)} %get-tuple-element.42), channel_id=1, source_target_pairs={{0,48},{16,0},{32,16},{48,32},{1,49},{17,1},{33,17},{49,33},{2,50}... | collective-permute-start | bytes 1523720 | tf_op jit(solution)/shard_map/ppermute | solution.py:165
  28.0 26.1 %copy-start.3 = (f32[4,496,128]{2,1,0:T(8,128)S(1)}, f32[4,496,128]{2,1,0:T(8,128)}, u32[]{:S(2)}) copy-start(f32[4,496,128]{2,1,0:T(8,128)} %copy-done.2) | copy-start | bytes 3047428
  28.1 16.2 %collective-permute-start.3 = (f32[496,128]{1,0:T(8,128)S(1)}, f32[496,128]{1,0:T(8,128)S(1)}, u32[]{:S(2)}, u32[]{:S(2)}) collective-permute-start(f32[496,128]{1,0:T(8,128)S(1)} %get-tuple-element.33), channel_id=1, source_target_pairs={{0,16},{16,32},{32,48},{48,0},{1,17},{17,33},{33,49},{49,1},{2,18}... | collective-permute-start | bytes 761864 | tf_op jit(solution)/shard_map/ppermute | solution.py:174
  28.5 15.8 %collective-permute-start.4 = (f32[496,128]{1,0:T(8,128)S(1)}, f32[496,128]{1,0:T(8,128)S(1)}, u32[]{:S(2)}, u32[]{:S(2)}) collective-permute-start(f32[496,128]{1,0:T(8,128)S(1)} %get-tuple-element.34), channel_id=1, source_target_pairs={{0,48},{16,0},{32,16},{48,32},{1,49},{17,1},{33,17},{49,33},{2,50}... | collective-permute-start | bytes 761864 | tf_op jit(solution)/shard_map/ppermute | solution.py:175
  45.3 19.9 %all-to-all-start = ((f32[32,8,496]{2,1,0:T(8,128)}), f32[32,8,496]{2,1,0:T(8,128)S(1)}, u32[]{:S(2)}, u32[]{:S(2)}) async-start(f32[32,8,496]{2,1,0:T(8,128)} %bitcast.6), calls=%async_computation | async-start | bytes 1048576 | tf_op jit(solution)/shard_map/all_to_all | solution.py:186
  54.1 1.0 copy-start.11
  55.1 18.8 %copy-start.21 = (f32[62]{0:T(128)S(1)}, f32[62]{0:T(128)}, u32[]{:S(2)}) copy-start(f32[62]{0:T(128)} %param.13) | copy-start | bytes 748
  55.1 18.9 %copy-start.22 = (f32[62]{0:T(128)S(1)}, f32[62]{0:T(128)}, u32[]{:S(2)}) copy-start(f32[62]{0:T(128)} %param.14) | copy-start | bytes 748
  55.1 19.0 %copy-start.4 = (s32[62,2048]{1,0:T(8,128)S(1)}, s32[62,2048]{1,0:T(8,128)}, u32[]{:S(2)}) copy-start(s32[62,2048]{1,0:T(8,128)} %m_codes.1) | copy-start | bytes 1523716
  55.1 19.0 %copy-start.5 = (s32[62,2048]{1,0:T(8,128)S(1)}, s32[62,2048]{1,0:T(8,128)}, u32[]{:S(2)}) copy-start(s32[62,2048]{1,0:T(8,128)} %v_codes.1) | copy-start | bytes 1523716
  55.1 19.0 %copy-start.18 = (f32[256]{0:T(256)S(1)}, f32[256]{0:T(256)}, u32[]{:S(2)}) copy-start(f32[256]{0:T(256)} %param.15) | copy-start | bytes 3076
  55.1 19.0 %copy-start.19 = (f32[256]{0:T(256)S(1)}, f32[256]{0:T(256)}, u32[]{:S(2)}) copy-start(f32[256]{0:T(256)} %param.16) | copy-start | bytes 3076
  55.3 8.9 %collective-permute-start.17 = (f32[496,128]{1,0:T(8,128)S(1)}, f32[496,128]{1,0:T(8,128)S(1)}, u32[]{:S(2)}, u32[]{:S(2)}) collective-permute-start(f32[496,128]{1,0:T(8,128)S(1)} %get-tuple-element.44), channel_id=1, source_target_pairs={{0,16},{16,32},{32,48},{48,0},{1,17},{17,33},{33,49},{49,1},{2,18}... | collective-permute-start | bytes 761864 | tf_op jit(solution)/shard_map/ppermute | solution.py:174
  56.3 7.9 %collective-permute-start.18 = (f32[496,128]{1,0:T(8,128)S(1)}, f32[496,128]{1,0:T(8,128)S(1)}, u32[]{:S(2)}, u32[]{:S(2)}) collective-permute-start(f32[496,128]{1,0:T(8,128)S(1)} %get-tuple-element.45), channel_id=1, source_target_pairs={{0,48},{16,0},{32,16},{48,32},{1,49},{17,1},{33,17},{49,33},{2,50}... | collective-permute-start | bytes 761864 | tf_op jit(solution)/shard_map/ppermute | solution.py:175
  65.2 19.6 %all-to-all-start.2 = ((f32[32,8,496]{2,1,0:T(8,128)}), f32[32,8,496]{2,1,0:T(8,128)S(1)}, u32[]{:S(2)}, u32[]{:S(2)}) async-start(f32[32,8,496]{2,1,0:T(8,128)} %bitcast.16), calls=%async_computation.2 | async-start | bytes 1048576 | tf_op jit(solution)/shard_map/all_to_all | solution.py:186
  84.8 15.7 %all-to-all-start.1 = ((f32[32,8,496]{2,1,0:T(8,128)}), f32[32,8,496]{2,1,0:T(8,128)S(1)}, u32[]{:S(2)}, u32[]{:S(2)}) async-start(f32[32,8,496]{2,1,0:T(8,128)} %get-tuple-element.39), calls=%async_computation.1 | async-start | bytes 1048576 | tf_op jit(solution)/shard_map/all_to_all | solution.py:218
  100.4 15.7 %all-to-all-start.3 = ((f32[32,8,496]{2,1,0:T(8,128)}), f32[32,8,496]{2,1,0:T(8,128)S(1)}, u32[]{:S(2)}, u32[]{:S(2)}) async-start(f32[32,8,496]{2,1,0:T(8,128)} %get-tuple-element.46), calls=%async_computation.3 | async-start | bytes 1048576 | tf_op jit(solution)/shard_map/all_to_all | solution.py:218
  104.6 20.9 %collective-permute-start.6 = (f32[2,496,128]{2,1,0:T(8,128)S(1)}, f32[2,496,128]{2,1,0:T(8,128)S(1)}, u32[]{:S(2)}, u32[]{:S(2)}) collective-permute-start(f32[2,496,128]{2,1,0:T(8,128)S(1)} %unturn.2.refs_0_), channel_id=1, source_target_pairs={{0,48},{16,0},{32,16},{48,32},{1,49},{17,1},{33,17},{49,33},{2,50}... | collective-permute-start | bytes 1523720 | tf_op jit(solution)/shard_map/ppermute | solution.py:229
  116.3 13.4 %collective-permute-start.20 = (f32[2,496,128]{2,1,0:T(8,128)S(1)}, f32[2,496,128]{2,1,0:T(8,128)S(1)}, u32[]{:S(2)}, u32[]{:S(2)}) collective-permute-start(f32[2,496,128]{2,1,0:T(8,128)S(1)} %unturn.3.refs_0_), channel_id=1, source_target_pairs={{0,48},{16,0},{32,16},{48,32},{1,49},{17,1},{33,17},{49,33},{2,50}... | collective-permute-start | bytes 1523720 | tf_op jit(solution)/shard_map/ppermute | solution.py:229
  123.3 31.6 %copy-start.20 = (f32[62,2048]{1,0:T(8,128)S(1)}, f32[62,2048]{1,0:T(8,128)}, u32[]{:S(2)}) copy-start(f32[62,2048]{1,0:T(8,128)} %reshape.67) | copy-start | bytes 1523716
  123.3 13.7 %collective-permute-start.19 = (f32[2,496,128]{2,1,0:T(8,128)S(1)}, f32[2,496,128]{2,1,0:T(8,128)S(1)}, u32[]{:S(2)}, u32[]{:S(2)}) collective-permute-start(f32[2,496,128]{2,1,0:T(8,128)S(1)} %unturn.3.refs_0_), channel_id=1, source_target_pairs={{0,16},{16,32},{32,48},{48,0},{1,17},{17,33},{33,49},{49,1},{2,18}... | collective-permute-start | bytes 1523720 | tf_op jit(solution)/shard_map/ppermute | solution.py:228
  124.5 34.4 %copy-start.23 = (f32[62]{0:T(128)}, f32[62]{0:T(128)S(1)}, u32[]{:S(2)}) copy-start(f32[62]{0:T(128)S(1)} %abs_reduce_fusion) | copy-start | bytes 748
  124.5 23.3 %collective-permute-start.5 = (f32[2,496,128]{2,1,0:T(8,128)S(1)}, f32[2,496,128]{2,1,0:T(8,128)S(1)}, u32[]{:S(2)}, u32[]{:S(2)}) collective-permute-start(f32[2,496,128]{2,1,0:T(8,128)S(1)} %unturn.2.refs_0_), channel_id=1, source_target_pairs={{0,16},{16,32},{32,48},{48,0},{1,17},{17,33},{33,49},{49,1},{2,18}... | collective-permute-start | bytes 1523720 | tf_op jit(solution)/shard_map/ppermute | solution.py:228
  124.6 26.6 %collective-permute-start.23 = (f32[2,496,128]{2,1,0:T(8,128)S(1)}, f32[2,496,128]{2,1,0:T(8,128)S(1)}, u32[]{:S(2)}, u32[]{:S(2)}) collective-permute-start(f32[2,496,128]{2,1,0:T(8,128)S(1)} %unturn.3.refs_0_), channel_id=1, source_target_pairs={{0,8},{8,0},{1,9},{9,1},{2,10},{10,2},{3,11},{11,3},{4,12},{12,4},... | collective-permute-start | bytes 1523720 | tf_op jit(solution)/shard_map/ppermute | solution.py:233
  125.6 26.5 %collective-permute-start.8 = (f32[496,128]{1,0:T(8,128)S(1)}, f32[496,128]{1,0:T(8,128)}, u32[]{:S(2)}, u32[]{:S(2)}) collective-permute-start(f32[496,128]{1,0:T(8,128)S(1)} %slice_bitcast_fusion.6), channel_id=1, source_target_pairs={{0,48},{16,0},{32,16},{48,32},{1,49},{17,1},{33,17},{49,33},{2,50}... | collective-permute-start | bytes 761864 | tf_op jit(solution)/shard_map/ppermute | solution.py:231
  129.7 22.4 %collective-permute-start.22 = (f32[496,128]{1,0:T(8,128)S(1)}, f32[496,128]{1,0:T(8,128)S(1)}, u32[]{:S(2)}, u32[]{:S(2)}) collective-permute-start(f32[496,128]{1,0:T(8,128)S(1)} %slice_bitcast_fusion.4), channel_id=1, source_target_pairs={{0,48},{16,0},{32,16},{48,32},{1,49},{17,1},{33,17},{49,33},{2,50}... | collective-permute-start | bytes 761864 | tf_op jit(solution)/shard_map/ppermute | solution.py:231
  137.0 16.4 %collective-permute-start.21 = (f32[496,128]{1,0:T(8,128)S(1)}, f32[496,128]{1,0:T(8,128)}, u32[]{:S(2)}, u32[]{:S(2)}) collective-permute-start(f32[496,128]{1,0:T(8,128)S(1)} %slice_bitcast_fusion.5), channel_id=1, source_target_pairs={{0,16},{16,32},{32,48},{48,0},{1,17},{17,33},{33,49},{49,1},{2,18}... | collective-permute-start | bytes 761864 | tf_op jit(solution)/shard_map/ppermute | solution.py:230
  147.8 14.3 %collective-permute-start.25 = (f32[2,496,128]{2,1,0:T(8,128)S(1)}, f32[2,496,128]{2,1,0:T(8,128)}, u32[]{:S(2)}, u32[]{:S(2)}) collective-permute-start(f32[2,496,128]{2,1,0:T(8,128)S(1)} %collective-permute-done.20.refs_2_), channel_id=1, source_target_pairs={{0,8},{8,0},{1,9},{9,1},{2,10},{10,2},{3,11},{11,3},{4,12},{12,4},... | collective-permute-start | bytes 1523720 | tf_op jit(solution)/shard_map/ppermute | solution.py:233
  152.0 9.3 %collective-permute-start.7 = (f32[496,128]{1,0:T(8,128)}, f32[496,128]{1,0:T(8,128)}, u32[]{:S(2)}, u32[]{:S(2)}) collective-permute-start(f32[496,128]{1,0:T(8,128)} %slice_bitcast_fusion.7), channel_id=1, source_target_pairs={{0,16},{16,32},{32,48},{48,0},{1,17},{17,33},{33,49},{49,1},{2,18}... | collective-permute-start | bytes 761864 | tf_op jit(solution)/shard_map/ppermute | solution.py:230
  152.0 10.7 %collective-permute-start.24 = (f32[2,496,128]{2,1,0:T(8,128)S(1)}, f32[2,496,128]{2,1,0:T(8,128)}, u32[]{:S(2)}, u32[]{:S(2)}) collective-permute-start(f32[2,496,128]{2,1,0:T(8,128)S(1)} %collective-permute-done.19.refs_1_), channel_id=1, source_target_pairs={{0,8},{8,0},{1,9},{9,1},{2,10},{10,2},{3,11},{11,3},{4,12},{12,4},... | collective-permute-start | bytes 1523720 | tf_op jit(solution)/shard_map/ppermute | solution.py:233
  152.1 10.0 %collective-permute-start.27 = (f32[496,128]{1,0:T(8,128)S(1)}, f32[496,128]{1,0:T(8,128)}, u32[]{:S(2)}, u32[]{:S(2)}) collective-permute-start(f32[496,128]{1,0:T(8,128)S(1)} %collective-permute-done.22.refs_4_), channel_id=1, source_target_pairs={{0,8},{8,0},{1,9},{9,1},{2,10},{10,2},{3,11},{11,3},{4,12},{12,4},... | collective-permute-start | bytes 761864 | tf_op jit(solution)/shard_map/ppermute | solution.py:233
  153.4 9.3 %collective-permute-start.26 = (f32[496,128]{1,0:T(8,128)}, f32[496,128]{1,0:T(8,128)}, u32[]{:S(2)}, u32[]{:S(2)}) collective-permute-start(f32[496,128]{1,0:T(8,128)} %collective-permute-done.21.refs_3_), channel_id=1, source_target_pairs={{0,8},{8,0},{1,9},{9,1},{2,10},{10,2},{3,11},{11,3},{4,12},{12,4},... | collective-permute-start | bytes 761864 | tf_op jit(solution)/shard_map/ppermute | solution.py:233
  158.9 15.3 %copy-start.24 = (f32[62]{0:T(128)}, f32[62]{0:T(128)S(1)}, u32[]{:S(2)}) copy-start(f32[62]{0:T(128)S(1)} %reduce_max.19) | copy-start | bytes 748
  161.3 13.0 %collective-permute-start.9 = (f32[2,496,128]{2,1,0:T(8,128)S(1)}, f32[2,496,128]{2,1,0:T(8,128)S(1)}, u32[]{:S(2)}, u32[]{:S(2)}) collective-permute-start(f32[2,496,128]{2,1,0:T(8,128)S(1)} %unturn.2.refs_0_), channel_id=1, source_target_pairs={{0,8},{8,0},{1,9},{9,1},{2,10},{10,2},{3,11},{11,3},{4,12},{12,4},... | collective-permute-start | bytes 1523720 | tf_op jit(solution)/shard_map/ppermute | solution.py:233
  162.1 12.2 %collective-permute-start.11 = (f32[2,496,128]{2,1,0:T(8,128)S(1)}, f32[2,496,128]{2,1,0:T(8,128)S(1)}, u32[]{:S(2)}, u32[]{:S(2)}) collective-permute-start(f32[2,496,128]{2,1,0:T(8,128)S(1)} %collective-permute-done.6.refs_2_), channel_id=1, source_target_pairs={{0,8},{8,0},{1,9},{9,1},{2,10},{10,2},{3,11},{11,3},{4,12},{12,4},... | collective-permute-start | bytes 1523720 | tf_op jit(solution)/shard_map/ppermute | solution.py:233
  162.1 12.2 %collective-permute-start.10 = (f32[2,496,128]{2,1,0:T(8,128)S(1)}, f32[2,496,128]{2,1,0:T(8,128)S(1)}, u32[]{:S(2)}, u32[]{:S(2)}) collective-permute-start(f32[2,496,128]{2,1,0:T(8,128)S(1)} %collective-permute-done.5.refs_1_), channel_id=1, source_target_pairs={{0,8},{8,0},{1,9},{9,1},{2,10},{10,2},{3,11},{11,3},{4,12},{12,4},... | collective-permute-start | bytes 1523720 | tf_op jit(solution)/shard_map/ppermute | solution.py:233
  162.6 11.7 %collective-permute-start.13 = (f32[496,128]{1,0:T(8,128)}, f32[496,128]{1,0:T(8,128)S(1)}, u32[]{:S(2)}, u32[]{:S(2)}) collective-permute-start(f32[496,128]{1,0:T(8,128)} %collective-permute-done.8.refs_4_), channel_id=1, source_target_pairs={{0,8},{8,0},{1,9},{9,1},{2,10},{10,2},{3,11},{11,3},{4,12},{12,4},... | collective-permute-start | bytes 761864 | tf_op jit(solution)/shard_map/ppermute | solution.py:233
  162.7 11.6 %collective-permute-start.12 = (f32[496,128]{1,0:T(8,128)}, f32[496,128]{1,0:T(8,128)S(1)}, u32[]{:S(2)}, u32[]{:S(2)}) collective-permute-start(f32[496,128]{1,0:T(8,128)} %collective-permute-done.7.refs_3_), channel_id=1, source_target_pairs={{0,8},{8,0},{1,9},{9,1},{2,10},{10,2},{3,11},{11,3},{4,12},{12,4},... | collective-permute-start | bytes 761864 | tf_op jit(solution)/shard_map/ppermute | solution.py:233
  165.0 3.3 %copy-start.1 = (f32[1024,1984]{0,1:T(8,128)S(1)}, f32[1024,1984]{0,1:T(8,128)}, u32[]{:S(2)}) copy-start(f32[1024,1984]{0,1:T(8,128)} %param.9) | copy-start | bytes 24379396
  168.3 1.0 copy-start.8
  (11 other events, 9.3 us)

commit v3 on v0

v3 whole, which is shorter than its diff:
```python
import functools

import jax
import jax.numpy as jnp
from jax import lax
from jax.experimental import pallas as pl
from jax.experimental.pallas import tpu as pltpu
from jax.sharding import Mesh, PartitionSpec as P

BLOCK = 2048
LANES = 128
N_YH, N_Z, N_CORE, N_YL, N_X = 2, 4, 2, 2, 4
N_TENSOR = N_YL * N_X
OWNERS = N_CORE * N_TENSOR
AXES = ("yh", "z", "core", "yl", "x")
DP = ("yh", "z", "core")
TENSOR = ("yl", "x")
ROW_OWNERS = ("yh", "core", "yl", "x")
PARTS = 2

beta_one = 0.9
beta_two = 0.999
adam_eps = 1e-08
learn_rate = 0.02
decay_rate = 0.1
scale_eps = 1e-06

SWAP = [(0, 1), (1, 0)]
UP = [(i, (i + 1) % N_Z) for i in range(N_Z)]
DOWN = [(i, (i - 1) % N_Z) for i in range(N_Z)]

ANY = pl.BlockSpec(memory_space=pl.ANY)
SMEM = pl.BlockSpec(memory_space=pltpu.SMEM)
VMEM = pl.BlockSpec(memory_space=pltpu.VMEM)
f32 = jnp.float32
COST = pl.CostEstimate(flops=1, bytes_accessed=1024, transcendentals=0)


def shape(*dims):
    return jax.ShapeDtypeStruct(dims, f32)


def params():
    return pltpu.CompilerParams(vmem_limit_bytes=10 * 2**20)


def lane_tile(yh, z):
    return pl.ds(pl.multiple_of((yh * N_Z + lax.rem(z, N_Z)) * LANES, LANES), LANES)


STEP = 248


def each(count, body):
    @pl.loop(0, count // STEP)
    def _(i):
        for k in range(0, STEP, 8):
            body(pl.multiple_of(i * STEP + k, 8))


def segments(rows, row):
    for r in range(rows):
        at = r * row
        while at < (r + 1) * row:
            end = min((r + 1) * row, (at // BLOCK + 1) * BLOCK)
            b = at // BLOCK
            yield r, slice(at - r * row, end - r * row), b, slice(at - b * BLOCK, end - b * BLOCK)
            at = end


def owned(half, owner):
    c, j = divmod(owner, N_TENSOR)
    at = j * N_CORE * half + c * half
    return slice(at, at + half)


def old_state_kernel(half, m_codes, v_codes, m_scale, v_scale, code_m, code_v, m_out, v_out, held, flat):
    outs = (m_out, v_out)
    blocks = m_codes.shape[0]
    for which, (codes, scale, table) in enumerate(((m_codes, m_scale, code_m), (v_codes, v_scale, code_v))):
        low = jnp.broadcast_to(table[0:1, :], (8, LANES))
        high = jnp.broadcast_to(table[1:2, :], (8, LANES))
        for r in range(0, blocks, 8):
            rows = slice(min(r, blocks - 8), min(r, blocks - 8) + 8)
            for k in range(0, BLOCK, LANES):
                index = codes[rows, k : k + LANES]
                lane = index & (LANES - 1)
                a = jnp.take_along_axis(low, lane, axis=1)
                b = jnp.take_along_axis(high, lane, axis=1)
                held[rows, k : k + LANES] = jnp.where(index < LANES, a, b)
        for r, columns, b, inside in segments(*flat.shape):
            flat[r : r + 1, columns] = held[b : b + 1, inside] * scale[b]
        for owner in range(OWNERS):
            outs[which][owner] = flat[:, owned(half, owner)]


def old_state(m_codes, v_codes, m_absmax, v_absmax, code_m, code_v, half):
    rows = LANES // OWNERS
    return pl.pallas_call(
        functools.partial(old_state_kernel, half),
        in_specs=[VMEM, VMEM, SMEM, SMEM, VMEM, VMEM],
        out_specs=[VMEM] * 2,
        out_shape=[shape(OWNERS, rows, half)] * 2,
        scratch_shapes=[pltpu.VMEM(m_codes.shape, f32), pltpu.VMEM((rows, N_CORE * half * N_TENSOR), f32)],
        compiler_params=params(),
        cost_estimate=COST,
        name="old_state",
    )(m_codes, v_codes, m_absmax, v_absmax, code_m.reshape(2, LANES), code_v.reshape(2, LANES))


def new_state_kernel(half, m_in, v_in, *refs):
    outs, (held, flat) = refs[:4], refs[4:]
    blocks = outs[0].shape[0]
    for which, values in enumerate((m_in, v_in)):
        for owner in range(OWNERS):
            flat[:, owned(half, owner)] = values[owner]
        for r, columns, b, inside in segments(*flat.shape):
            held[b : b + 1, inside] = flat[r : r + 1, columns]
        value = held[...]
        largest = jnp.max(jnp.abs(value) if which == 0 else value, axis=1, keepdims=True)
        outs[which][...] = (value / (largest + scale_eps)).astype(jnp.bfloat16)[:blocks]
        outs[2 + which][...] = jnp.broadcast_to(largest, (held.shape[0], LANES)).T[0:1, :blocks]


def new_state(m_new, v_new, blocks, half):
    rows = LANES // OWNERS
    scaled = jax.ShapeDtypeStruct((blocks, BLOCK), jnp.bfloat16)
    m_scaled, v_scaled, m_absmax, v_absmax = pl.pallas_call(
        functools.partial(new_state_kernel, half),
        in_specs=[VMEM] * 2,
        out_specs=[VMEM] * 4,
        out_shape=[scaled, scaled, shape(1, blocks), shape(1, blocks)],
        scratch_shapes=[
            pltpu.VMEM((pl.cdiv(blocks, 8) * 8, BLOCK), f32),
            pltpu.VMEM((rows, N_CORE * half * N_TENSOR), f32),
        ],
        compiler_params=params(),
        cost_estimate=COST,
        name="new_state",
    )(m_new, v_new)
    return m_scaled, v_scaled, m_absmax[0], v_absmax[0]


def rows_of(core, part, width):
    return pl.ds(pl.multiple_of(core * (width * PARTS) + part * width, 8), width)


def in_hbm(array):
    return pltpu.with_memory_space_constraint(array, pltpu.HBM)


def take_kernel(part, width, place, source, send, sem):
    copy = pltpu.make_async_copy(source.at[rows_of(1 - place[0], part, width)], send, sem)
    copy.start()
    copy.wait()


def take(place, source, part, width, spec):
    return pl.pallas_call(
        functools.partial(take_kernel, part, width),
        in_specs=[SMEM, spec],
        out_specs=VMEM,
        out_shape=shape(width, source.shape[1]),
        scratch_shapes=[pltpu.SemaphoreType.DMA],
        compiler_params=params(),
        cost_estimate=COST,
        name="take_part",
    )(place, source)


def pack_kernel(part, width, place, grad, other, up, down, keep):
    c, z = place[0], place[1]
    base = c * (width * PARTS) + part * width
    spots = (
        (up, 0, 0, 2),
        (down, 0, 1, 2),
        (up, 1, 1, 1),
        (down, 1, 0, 3),
        (keep, 0, 0, 1),
        (keep, 1, 1, 3),
        (keep, 2, 0, 0),
        (keep, 3, 1, 0),
    )

    def body(r):
        own = pl.ds(pl.multiple_of(base + r, 8), 8)
        rows = pl.ds(r, 8)
        for out, slot, yh, to in spots:
            lanes = lane_tile(yh, z + to)
            out[slot, rows, :] = grad[own, lanes] + other[rows, lanes]

    each(width, body)


def pack(place, grad_t, other, part, width):
    outs = [shape(n, width, LANES) for n in (2, 2, 4)]
    return pl.pallas_call(
        functools.partial(pack_kernel, part, width),
        in_specs=[SMEM, VMEM, VMEM],
        out_specs=[VMEM] * 3,
        out_shape=outs,
        compiler_params=params(),
        cost_estimate=COST,
        name="pack",
    )(place, grad_t, other)


def relay_kernel(keep, up, down, up2, down2, rest):
    def body(r):
        rows = pl.ds(r, 8)
        up2[rows, :] = keep[0, rows, :] + up[0, rows, :]
        down2[rows, :] = keep[1, rows, :] + down[0, rows, :]
        rest[0, rows, :] = keep[2, rows, :] + down[1, rows, :]
        rest[1, rows, :] = keep[3, rows, :] + up[1, rows, :]

    each(keep.shape[1], body)


def relay(keep, up, down):
    tile = keep.shape[1:]
    return pl.pallas_call(
        relay_kernel,
        in_specs=[VMEM] * 3,
        out_specs=[VMEM] * 3,
        out_shape=[shape(*tile), shape(*tile), shape(N_YH, *tile)],
        compiler_params=params(),
        cost_estimate=COST,
        name="relay",
    )(keep, up, down)


def ring(up, down):
    return lax.ppermute(up, "z", UP), lax.ppermute(down, "z", DOWN)


def turn_kernel(width, *refs):
    parts, (out, held) = refs[:-2], refs[-2:]
    for yh in range(N_YH):
        for part in range(PARTS):
            rest, arrived = parts[3 * part], parts[3 * part + 1 + yh]
            held[part * width : (part + 1) * width, :] = rest[yh] + arrived[...]
        rows = held[...].T[:, : PARTS * width]
        out[yh * OWNERS : (yh + 1) * OWNERS] = rows.reshape(OWNERS, -1, PARTS * width)


def turn(sums, width):
    return pl.pallas_call(
        functools.partial(turn_kernel, width),
        in_specs=[VMEM] * len(sums),
        out_specs=VMEM,
        out_shape=shape(N_YH * OWNERS, LANES // OWNERS, PARTS * width),
        scratch_shapes=[pltpu.VMEM((pl.cdiv(PARTS * width, LANES) * LANES, LANES), f32)],
        compiler_params=params(),
        cost_estimate=COST,
        name="turn",
    )(*sums)


def exchange(array):
    return lax.all_to_all(array, ROW_OWNERS, split_axis=0, concat_axis=0, tiled=True)


def adam_kernel(fixes, grads, m_old, v_old, m_out, v_out, update):
    def body(owner):
        grad = grads[owner] + grads[OWNERS + owner]
        m_new = beta_one * m_old[owner] + (1.0 - beta_one) * grad
        v_new = beta_two * v_old[owner] + (1.0 - beta_two) * grad * grad
        m_out[owner] = m_new
        v_out[owner] = v_new
        value = m_new / fixes[0] / (jnp.sqrt(v_new / fixes[1]) + adam_eps)
        update[owner] = value
        update[OWNERS + owner] = value

    pl.loop(0, OWNERS)(body)


def adam(fixes, grads, m_old, v_old):
    return pl.pallas_call(
        adam_kernel,
        in_specs=[SMEM] + [VMEM] * 3,
        out_specs=[VMEM] * 3,
        out_shape=[shape(*m_old.shape), shape(*m_old.shape), shape(*grads.shape)],
        compiler_params=params(),
        cost_estimate=COST,
        name="adam",
    )(fixes, grads, m_old, v_old)


def unturn_kernel(width, rows, *refs):
    outs, near, held = refs[:PARTS], refs[PARTS], refs[PARTS + 1]
    for yh in range(N_YH):
        held[:, 0 : PARTS * width] = rows[yh * OWNERS : (yh + 1) * OWNERS].reshape(LANES, PARTS * width)
        turned = held[...].T
        for part, out in enumerate(outs):
            value = turned[part * width : (part + 1) * width, :]
            out[yh] = value
            near[N_YH * part + yh] = value


def unturn(back, width):
    pair = shape(N_YH, width, LANES)
    return pl.pallas_call(
        functools.partial(unturn_kernel, width),
        in_specs=[VMEM],
        out_specs=[VMEM] * (PARTS + 1),
        out_shape=[pair] * PARTS + [shape(PARTS * N_YH, width, LANES)],
        scratch_shapes=[pltpu.VMEM((LANES, pl.cdiv(PARTS * width, LANES) * LANES), f32)],
        compiler_params=params(),
        cost_estimate=COST,
        name="unturn",
    )(back)


def relayed_kernel(up, down, up_out, down_out):
    up_out[...] = up[0]
    down_out[...] = down[1]


def relayed(up, down):
    return pl.pallas_call(
        relayed_kernel,
        in_specs=[VMEM] * 2,
        out_specs=[VMEM] * 2,
        out_shape=[shape(*up.shape[1:])] * 2,
        compiler_params=params(),
        cost_estimate=COST,
        name="relayed",
    )(up, down)


def gathered_kernel(*refs):
    pieces, out = refs[:-1], refs[-1]
    at = 0
    for piece in pieces:
        if len(piece.shape) == 2:
            out[at] = piece[...]
            at += 1
        else:
            out[at : at + piece.shape[0]] = piece[...]
            at += piece.shape[0]


def gathered(*pieces):
    count = sum(p.shape[0] if p.ndim == 3 else 1 for p in pieces)
    return pl.pallas_call(
        gathered_kernel,
        in_specs=[VMEM] * len(pieces),
        out_specs=VMEM,
        out_shape=shape(count, *pieces[0].shape[-2:]),
        compiler_params=params(),
        cost_estimate=COST,
        name="gathered",
    )(*pieces)


def swapped(pieces):
    return list(pieces) + [lax.ppermute(p, "core", SWAP) for p in pieces]


def places_of(width, places, place):
    c, z = place[0], place[1]
    work = []
    for side in range(2):
        for k, spots in enumerate(places):
            for slot, (part, yh, to) in enumerate(spots):
                rows = rows_of(c if side == 0 else 1 - c, part, width)
                work.append((side * len(places) + k, slot, rows, lane_tile(yh, z + to)))
    return work


def weight_kernel(width, places, place, weight, *refs):
    count = 2 * len(places)
    pieces, (out, held, sem) = refs[:count], refs[-3:]
    stores = []
    for k, (piece, slot, spot, lanes) in enumerate(places_of(width, places, place)):

        def body(r):
            rows = pl.ds(r, 8)
            old = weight[pl.ds(pl.multiple_of(spot.start + r, 8), 8), lanes]
            if len(pieces[piece].shape) == 3:
                update = pieces[piece][slot, rows, :]
            else:
                update = pieces[piece][rows, :]
            held[k, rows, :] = old - learn_rate * (update + decay_rate * old)

        each(width, body)
        stores.append(pltpu.make_async_copy(held.at[k], out.at[spot, lanes], sem.at[k]))
        stores[k].start()
    for store in stores:
        store.wait()


def hold_kernel(source, out, sem):
    copy = pltpu.make_async_copy(source, out, sem)
    copy.start()
    copy.wait()


def hold(array):
    return pl.pallas_call(
        hold_kernel,
        in_specs=[pl.BlockSpec(memory_space=pltpu.HBM)],
        out_specs=VMEM,
        out_shape=shape(*array.shape),
        scratch_shapes=[pltpu.SemaphoreType.DMA],
        compiler_params=params(),
        cost_estimate=COST,
        name="hold",
    )(in_hbm(array))


NEAR = (((0, 0, 0), (0, 1, 0), (1, 0, 0), (1, 1, 0)),)
SIDES = (((0, 0, 3), (0, 1, 3), (0, 0, 1), (0, 1, 1), (1, 0, 3), (1, 1, 3), (1, 0, 1), (1, 1, 1), (0, 0, 2), (0, 1, 2)),)
LAST = (((1, 0, 2), (1, 1, 2)),)


def write_weight(place, held, pieces, places, so_far, width):
    done = [] if so_far is None else [so_far]
    stores = 2 * sum(len(spots) for spots in places)
    hbm = pl.BlockSpec(memory_space=pltpu.HBM)
    return pl.pallas_call(
        functools.partial(weight_kernel, width, places),
        in_specs=[SMEM, VMEM] + [VMEM] * len(pieces) + [hbm] * len(done),
        out_specs=hbm,
        out_shape=shape(*held.shape),
        input_output_aliases={2 + len(pieces): 0} if done else {},
        scratch_shapes=[pltpu.VMEM((stores, width, LANES), f32), pltpu.SemaphoreType.DMA((stores,))],
        compiler_params=params(),
        cost_estimate=COST,
        name="write_weight",
    )(place, held, *pieces, *done)


def after(value, *others):
    return lax.optimization_barrier((value, *others))[0]


def shards(weight, grad_parts, m_codes, v_codes, m_absmax, v_absmax, code_m, code_v, step):
    columns = weight.shape[1]
    half = columns // N_CORE
    width = half // PARTS
    place = jnp.stack([lax.axis_index("core"), lax.axis_index("z")]).astype(jnp.int32)
    grad_t = grad_parts[0].T
    weight_t = weight.T

    send_0 = take(place, in_hbm(grad_t), 0, width, pl.BlockSpec(memory_space=pltpu.HBM))
    other_0 = lax.ppermute(send_0, "core", SWAP)
    send_1 = take(after(place, send_0), grad_t, 1, width, VMEM)
    other_1 = lax.ppermute(after(send_1, other_0), "core", SWAP)

    up, down, keep_0 = pack(place, grad_t, other_0, 0, width)
    other_1 = after(other_1, keep_0)
    up_0, down_0 = ring(up, down)
    up, down, keep_1 = pack(place, grad_t, other_1, 1, width)
    up_1, down_1 = ring(up, down)
    up2, down2, rest_0 = relay(keep_0, up_0, down_0)
    keep_1 = after(keep_1, rest_0)
    sums_0 = (rest_0, *ring(up2, down2))
    up2, down2, rest_1 = relay(keep_1, up_1, down_1)
    sums_1 = (rest_1, *ring(up2, down2))

    count = step[0].astype(f32)
    fix_one = 1.0 - jnp.power(f32(beta_one), count)
    fix_two = 1.0 - jnp.power(f32(beta_two), count)
    fixes = jnp.stack([fix_one, fix_two])
    olds = old_state(after(m_codes, rest_1), v_codes, m_absmax, v_absmax, code_m, code_v, half)
    held = hold(after(weight_t, olds[0]))
    *sums, held = lax.optimization_barrier((*sums_0, *sums_1, held, *olds, fixes))[:7]

    grads = exchange(turn(sums, width))
    m_new, v_new, update = adam(fixes, grads, *olds)
    pair_0, pair_1, near = unturn(exchange(update), width)

    up_0, down_0 = ring(pair_0, pair_0)
    up_1, down_1 = ring(pair_1, pair_1)
    new_weight = write_weight(place, held, swapped((near,)), NEAR, None, width)
    state = new_state(m_new, v_new, m_codes.shape[0], half)
    up_0, down_0, new_weight, *state = lax.optimization_barrier((up_0, down_0, new_weight, *state))
    up2, down2 = relayed(up_0, down_0)
    up_1, down_1 = lax.optimization_barrier((up_1, down_1, up2))[:2]
    up2_0, down2_0 = ring(up2, down2)
    up2, down2 = relayed(up_1, down_1)
    sides = gathered(up_0, down_0, up_1, after(down_1, up2), up2_0, down2_0)
    up2, down2 = ring(up2, down2)
    new_weight = write_weight(place, held, swapped((sides,)), SIDES, new_weight, width)
    far = lax.optimization_barrier((up2, down2, new_weight))
    new_weight = write_weight(place, held, swapped((gathered(*far[:2]),)), LAST, far[2], width)
    return (new_weight.T, *state)


def solution(mesh):
    fine = Mesh(mesh.devices.reshape(N_YH, N_Z, N_CORE, N_YL, N_X), AXES)
    blocks = P(DP + TENSOR)
    in_specs = (P(None, TENSOR), P(DP, None, TENSOR), blocks, blocks, blocks, blocks, P(), P(), P())
    out_specs = (P(None, TENSOR), blocks, blocks, blocks, blocks)
    return jax.shard_map(shards, mesh=fine, in_specs=in_specs, out_specs=out_specs, check_vma=False)
```

time: 256 us -> 144 us (0.56)
  waiting for transfers between devices: 167 us -> 46.1 us
  blocking collectives: 12.9 us -> 45.7 us
  local copies, waits for them, and re-layouts: 30.2 us -> 0.04 us
  Pallas kernels: 0 us -> 23.9 us
  starting transfers between devices: 4.09 us -> 25.8 us
  other arithmetic: 14.5 us -> 0.15 us
  between operations: 14.9 us -> 1.77 us
  matrix products: 11.1 us -> 0 us
    reduce_scatter x1 -> x0, waiting for transfers between devices: 103 us -> none  [shards(): lax.psum_scatter(partial_value, 'dp', scatter_dimension=0, tiled=True)]
    all_gather x1 -> x0, waiting for transfers between devices: 63.9 us -> none  [shards(): mine = lax.all_gather(columns, 'dp', axis=0, tiled=True)]
    ppermute x0 -> x21, waiting for transfers between devices: none -> 46.1 us  [the longest x16 38.8 us: ring(): return (lax.ppermute(up, 'z', UP), lax.ppermute(down, 'z', DOWN))]
    all_to_all x1 -> x2, blocking collectives: 12.9 us -> 45.7 us  [exchange(): lax.all_to_all(array, ROW_OWNERS, split_axis=0, concat_axis=0, tiled=True)]
    unnamed x21 -> x14, local copies, waits for them, and re-layouts: 28.4 us -> 0.04 us
    ppermute x0 -> x21, starting transfers between devices: none -> 25.8 us  [the longest x16 20.7 us: ring(): return (lax.ppermute(up, 'z', UP), lax.ppermute(down, 'z', DOWN))]
    pallas_call x0 -> x19, Pallas kernels: none -> 23.9 us  [the longest x3 8.21 us: write_weight(): pl.pallas_call(functools.partial(weight_kernel, width, places), in_specs=...]
    sub x3 -> x0, other arithmetic: 12.7 us -> none  [the longest x1 12 us: shards(): new_weight = weight - learn_rate * (mine + decay_rate * weight)]
  transfers between devices with their start and end apart: 3 -> 21, of which waited for: 2 -> 13; matrix products, arithmetic and copies ran while one was open for 9% -> 0% of each run, Pallas kernels for 0% -> 12%
where the time goes in v3:
time: 144 us; the launch traced here: 143 us
  waiting for transfers between devices  46.1 us (32%)
  blocking collectives  45.7 us (32%)
  starting transfers between devices  25.8 us (18%)
  Pallas kernels  23.9 us (17%)
  between operations  1.77 us (1%)
    all_to_all x2, blocking collectives, exchange(): lax.all_to_all(array, ROW_OWNERS, split_axis=0, concat_axis=0, tiled=True)  45.7 us
    ppermute x16, waiting for transfers between devices, ring(): return (lax.ppermute(up, 'z', UP), lax.ppermute(down, 'z', DOWN))  38.8 us
    ppermute x16, starting transfers between devices, ring(): return (lax.ppermute(up, 'z', UP), lax.ppermute(down, 'z', DOWN))  20.7 us
    pallas_call x3, Pallas kernels, write_weight(): pl.pallas_call(functools.partial(weight_kernel, width, places), in_specs=...  8.21 us
    ppermute x3, waiting for transfers between devices, swapped(): return list(pieces) + [lax.ppermute(p, 'core', SWAP) for p in pieces]  4.45 us
    pallas_call x1, Pallas kernels, hold(): pl.pallas_call(hold_kernel, in_specs=[pl.BlockSpec(memory_space=pltpu.HBM...  3.32 us
    pallas_call x2, Pallas kernels, take(): pl.pallas_call(functools.partial(take_kernel, part, width), in_specs=[SME...  3.32 us
    ppermute x3, starting transfers between devices, swapped(): return list(pieces) + [lax.ppermute(p, 'core', SWAP) for p in pieces]  3.26 us
  transfers between devices with their start and end apart: 21, of which 13 were waited for; matrix products, arithmetic and copies ran while one was open for 0% of the time, Pallas kernels for 12%

profile of v3, /device:TPU:1, one launch (start us, length us, event | category | flops | bytes accessed | tf_op | source)
XLA Modules:
  0.0 143.4 jit_solution(13450342845903728661)
XLA Ops:
  0.7 2.4 %take_part.2 = f32[496,1024]{1,0:T(8,128)S(1)} custom-call(s32[2]{0:T(128)S(1)} %pad_add_fusion.place, f32[1984,1024]{1,0:T(8,128)} %bitcast.11), custom_call_target="tpu_custom_call" | custom-call | flops 1 | bytes 1024 | tf_op jit(solution)/shard_map/take_part/pallas_call | solution.py:159
  3.1 1.5 %collective-permute-start = (f32[496,1024]{1,0:T(8,128)S(1)}, f32[496,1024]{1,0:T(8,128)S(1)}, u32[]{:S(2)}, u32[]{:S(2)}) collective-permute-start(f32[496,1024]{1,0:T(8,128)S(1)} %take_part.2), channel_id=1, source_target_pairs={{0,8},{8,0},{1,9},{9,1},{2,10},{10,2},{3,11},{11,3},{4,12},{12,4},... | collective-permute-start | bytes 6094856 | tf_op jit(solution)/shard_map/ppermute | solution.py:447
  4.6 0.9 take_part.3
  5.6 2.7 %collective-permute-done.other = f32[496,1024]{1,0:T(8,128)S(1)} collective-permute-done((f32[496,1024]{1,0:T(8,128)S(1)}, f32[496,1024]{1,0:T(8,128)S(1)}, u32[]{:S(2)}, u32[]{:S(2)}) %collective-permute-start) | collective-permute-done | bytes 2031648 | tf_op jit(solution)/shard_map/ppermute | solution.py:447
  8.3 0.4 collective-permute-start.5
  8.7 1.5 %pack.2 = (f32[2,496,128]{2,1,0:T(8,128)S(1)}, f32[2,496,128]{2,1,0:T(8,128)S(1)}, f32[4,496,128]{2,1,0:T(8,128)S(1)}) custom-call(s32[2]{0:T(128)S(1)} %pad_add_fusion.place, f32[1984,1024]{1,0:T(8,128)S(1)} %bitcast.13, f32[496,1024]{1,0:T(8,128)S(1)} %collective-permute-done.other), custom_call_target="tpu_custom_call" | custom-call | flops 1 | bytes 1024 | tf_op jit(solution)/shard_map/pack/pallas_call | solution.py:197
  10.2 1.8 %collective-permute-start.1 = (f32[2,496,128]{2,1,0:T(8,128)S(1)}, f32[2,496,128]{2,1,0:T(8,128)S(1)}, u32[]{:S(2)}, u32[]{:S(2)}) collective-permute-start(f32[2,496,128]{2,1,0:T(8,128)S(1)} %get-tuple-element.60), channel_id=1, source_target_pairs={{0,16},{16,32},{32,48},{48,0},{1,17},{17,33},{33,49},{49,1},{2,18}... | collective-permute-start | bytes 1523720 | tf_op jit(solution)/shard_map/ppermute | solution.py:233
  12.0 2.2 %collective-permute-start.2 = (f32[2,496,128]{2,1,0:T(8,128)S(1)}, f32[2,496,128]{2,1,0:T(8,128)S(1)}, u32[]{:S(2)}, u32[]{:S(2)}) collective-permute-start(f32[2,496,128]{2,1,0:T(8,128)S(1)} %get-tuple-element.61), channel_id=1, source_target_pairs={{0,48},{16,0},{32,16},{48,32},{1,49},{17,1},{33,17},{49,33},{2,50}... | collective-permute-start | bytes 1523720 | tf_op jit(solution)/shard_map/ppermute | solution.py:233
  14.2 1.5 %pack.3 = (f32[2,496,128]{2,1,0:T(8,128)S(1)}, f32[2,496,128]{2,1,0:T(8,128)S(1)}, f32[4,496,128]{2,1,0:T(8,128)S(1)}) custom-call(s32[2]{0:T(128)S(1)} %pad_add_fusion.place, f32[1984,1024]{1,0:T(8,128)S(1)} %bitcast.14, f32[496,1024]{1,0:T(8,128)S(1)} %collective-permute-done.5.other), custom_call_target="tpu_custom_call" | custom-call | flops 1 | bytes 1024 | tf_op jit(solution)/shard_map/pack/pallas_call | solution.py:197
  15.8 2.7 %collective-permute-start.7 = (f32[2,496,128]{2,1,0:T(8,128)S(1)}, f32[2,496,128]{2,1,0:T(8,128)S(1)}, u32[]{:S(2)}, u32[]{:S(2)}) collective-permute-start(f32[2,496,128]{2,1,0:T(8,128)S(1)} %get-tuple-element.71), channel_id=1, source_target_pairs={{0,48},{16,0},{32,16},{48,32},{1,49},{17,1},{33,17},{49,33},{2,50}... | collective-permute-start | bytes 1523720 | tf_op jit(solution)/shard_map/ppermute | solution.py:233
  18.5 7.5 %collective-permute-done.1.up = f32[2,496,128]{2,1,0:T(8,128)S(1)} collective-permute-done((f32[2,496,128]{2,1,0:T(8,128)S(1)}, f32[2,496,128]{2,1,0:T(8,128)S(1)}, u32[]{:S(2)}, u32[]{:S(2)}) %collective-permute-start.1) | collective-permute-done | bytes 507936 | tf_op jit(solution)/shard_map/ppermute | solution.py:233
  26.0 0.1 relay.2
  26.1 0.5 collective-permute-start.3
  26.6 2.3 %collective-permute-start.4 = (f32[496,128]{1,0:T(8,128)S(1)}, f32[496,128]{1,0:T(8,128)S(1)}, u32[]{:S(2)}, u32[]{:S(2)}) collective-permute-start(f32[496,128]{1,0:T(8,128)S(1)} %get-tuple-element.64), channel_id=1, source_target_pairs={{0,48},{16,0},{32,16},{48,32},{1,49},{17,1},{33,17},{49,33},{2,50}... | collective-permute-start | bytes 761864 | tf_op jit(solution)/shard_map/ppermute | solution.py:233
  28.8 8.0 %collective-permute-done.6.up = f32[2,496,128]{2,1,0:T(8,128)S(1)} collective-permute-done((f32[2,496,128]{2,1,0:T(8,128)S(1)}, f32[2,496,128]{2,1,0:T(8,128)S(1)}, u32[]{:S(2)}, u32[]{:S(2)}) %collective-permute-start.6) | collective-permute-done | bytes 507936 | tf_op jit(solution)/shard_map/ppermute | solution.py:233
  36.8 0.2 relay.3
  37.0 0.5 collective-permute-start.8
  37.5 2.3 %collective-permute-start.9 = (f32[496,128]{1,0:T(8,128)S(1)}, f32[496,128]{1,0:T(8,128)S(1)}, u32[]{:S(2)}, u32[]{:S(2)}) collective-permute-start(f32[496,128]{1,0:T(8,128)S(1)} %get-tuple-element.74), channel_id=1, source_target_pairs={{0,48},{16,0},{32,16},{48,32},{1,49},{17,1},{33,17},{49,33},{2,50}... | collective-permute-start | bytes 761864 | tf_op jit(solution)/shard_map/ppermute | solution.py:233
  40.6 2.4 %old_state.1 = (f32[16,8,992]{2,1,0:T(8,128)S(1)}, f32[16,8,992]{2,1,0:T(8,128)S(1)}) custom-call(s32[62,2048]{1,0:T(8,128)S(1)} %copy-done.1, s32[62,2048]{1,0:T(8,128)S(1)} %copy-done.2, f32[62]{0:T(128)S(1)} %copy-done.5, f32[62]{0:T(128)S(1)} %copy-done.6, f32[2,128]{1,0:T(2,128)S(1)} %bitcast.15, f32[2,128]{1,0:T(2,128)S(1)} %bitcast.16), custom_call_target="tpu_custom_call" | custom-call | flops 1 | bytes 1024 | tf_op jit(solution)/shard_map/old_state/pallas_call | solution.py:99
  43.0 3.3 %hold.1.weight = f32[1984,1024]{1,0:T(8,128)S(1)} custom-call(f32[1984,1024]{1,0:T(8,128)} %bitcast.18), custom_call_target="tpu_custom_call" | custom-call | flops 1 | bytes 1024 | tf_op jit(solution)/shard_map/hold/pallas_call | solution.py:400
  46.4 1.4 collective-permute-done.8.refs_4_
  47.7 0.4 turn.1
  48.1 24.9 %all_to_all.10.grads = f32[32,8,992]{2,1,0:T(8,128)S(1)} all-to-all(f32[32,8,992]{2,1,0:T(8,128)S(1)} %turn.1), channel_id=1, replica_groups=mesh['yh'=2,'z'=4,'core'=2,'yl'=2,'x'=4] {'yh','core','yl','x'}, dimensions={0} | all-to-all | bytes 2031616 | tf_op jit(solution)/shard_map/all_to_all | solution.py:260
  73.0 1.1 adam.1
  74.1 20.8 %all_to_all.11.rows = f32[32,8,992]{2,1,0:T(8,128)S(1)} all-to-all(f32[32,8,992]{2,1,0:T(8,128)S(1)} %get-tuple-element.86), channel_id=1, replica_groups=mesh['yh'=2,'z'=4,'core'=2,'yl'=2,'x'=4] {'yh','core','yl','x'}, dimensions={0} | all-to-all | bytes 2031616 | tf_op jit(solution)/shard_map/all_to_all | solution.py:260
  94.8 0.4 unturn.1
  95.2 0.2 collective-permute-start.14
  95.3 2.8 %collective-permute-start.13 = (f32[2,496,128]{2,1,0:T(8,128)S(1)}, f32[2,496,128]{2,1,0:T(8,128)S(1)}, u32[]{:S(2)}, u32[]{:S(2)}) collective-permute-start(f32[2,496,128]{2,1,0:T(8,128)S(1)} %get-tuple-element.88), channel_id=1, source_target_pairs={{0,48},{16,0},{32,16},{48,32},{1,49},{17,1},{33,17},{49,33},{2,50}... | collective-permute-start | bytes 1523720 | tf_op jit(solution)/shard_map/ppermute | solution.py:233
  98.1 2.7 %collective-permute-start.11 = (f32[2,496,128]{2,1,0:T(8,128)S(1)}, f32[2,496,128]{2,1,0:T(8,128)S(1)}, u32[]{:S(2)}, u32[]{:S(2)}) collective-permute-start(f32[2,496,128]{2,1,0:T(8,128)S(1)} %get-tuple-element.87), channel_id=1, source_target_pairs={{0,48},{16,0},{32,16},{48,32},{1,49},{17,1},{33,17},{49,33},{2,50}... | collective-permute-start | bytes 1523720 | tf_op jit(solution)/shard_map/ppermute | solution.py:233
  100.8 1.4 %new_state.1 = (bf16[62,2048]{1,0:T(8,128)(2,1)}, bf16[62,2048]{1,0:T(8,128)(2,1)}, f32[1,62]{1,0:T(1,128)}, f32[1,62]{1,0:T(1,128)}) custom-call(f32[16,8,992]{2,1,0:T(8,128)S(1)} %get-tuple-element.90.m_in, f32[16,8,992]{2,1,0:T(8,128)S(1)} %get-tuple-element.91.v_in), custom_call_target="tpu_custom_call" | custom-call | flops 1 | bytes 1024 | tf_op jit(solution)/shard_map/new_state/pallas_call | solution.py:128
  102.2 2.4 %write_weight.3.refs_2_ = f32[1984,1024]{1,0:T(8,128)} custom-call(s32[2]{0:T(128)S(1)} %pad_add_fusion.place, f32[1984,1024]{1,0:T(8,128)S(1)} %hold.1.weight, f32[4,496,128]{2,1,0:T(8,128)S(1)} %get-tuple-element.89.refs_0_, f32[4,496,128]{2,1,0:T(8,128)S(1)} %collective-permute-done.14.refs_1_), custom_call_target="tpu_custom_call" | custom-call | flops 1 | bytes 1024 | tf_op jit(solution)/shard_map/write_weight/pallas_call | solution.py:421
  104.6 4.0 %collective-permute-done.13.down.refs_1_ = f32[2,496,128]{2,1,0:T(8,128)S(1)} collective-permute-done((f32[2,496,128]{2,1,0:T(8,128)S(1)}, f32[2,496,128]{2,1,0:T(8,128)S(1)}, u32[]{:S(2)}, u32[]{:S(2)}) %collective-permute-start.13) | collective-permute-done | bytes 507936 | tf_op jit(solution)/shard_map/ppermute | solution.py:233
  108.6 3.1 %collective-permute-done.12.up.refs_0_ = f32[2,496,128]{2,1,0:T(8,128)S(1)} collective-permute-done((f32[2,496,128]{2,1,0:T(8,128)S(1)}, f32[2,496,128]{2,1,0:T(8,128)S(1)}, u32[]{:S(2)}, u32[]{:S(2)}) %collective-permute-start.12) | collective-permute-done | bytes 507936 | tf_op jit(solution)/shard_map/ppermute | solution.py:233
  111.8 0.4 collective-permute-start.18
  112.1 1.1 collective-permute-start.17
  113.3 6.2 %collective-permute-done.11.down.refs_3_ = f32[2,496,128]{2,1,0:T(8,128)S(1)} collective-permute-done((f32[2,496,128]{2,1,0:T(8,128)S(1)}, f32[2,496,128]{2,1,0:T(8,128)S(1)}, u32[]{:S(2)}, u32[]{:S(2)}) %collective-permute-start.11) | collective-permute-done | bytes 507936 | tf_op jit(solution)/shard_map/ppermute | solution.py:233
  119.5 3.1 %collective-permute-done.10.up.refs_2_ = f32[2,496,128]{2,1,0:T(8,128)S(1)} collective-permute-done((f32[2,496,128]{2,1,0:T(8,128)S(1)}, f32[2,496,128]{2,1,0:T(8,128)S(1)}, u32[]{:S(2)}, u32[]{:S(2)}) %collective-permute-start.10) | collective-permute-done | bytes 507936 | tf_op jit(solution)/shard_map/ppermute | solution.py:233
  122.6 2.3 %collective-permute-done.18.refs_5_ = f32[496,128]{1,0:T(8,128)S(1)} collective-permute-done((f32[496,128]{1,0:T(8,128)S(1)}, f32[496,128]{1,0:T(8,128)S(1)}, u32[]{:S(2)}, u32[]{:S(2)}) %collective-permute-start.18) | collective-permute-done | bytes 253984 | tf_op jit(solution)/shard_map/ppermute | solution.py:233
  124.9 3.1 %collective-permute-done.17.refs_4_ = f32[496,128]{1,0:T(8,128)S(1)} collective-permute-done((f32[496,128]{1,0:T(8,128)S(1)}, f32[496,128]{1,0:T(8,128)S(1)}, u32[]{:S(2)}, u32[]{:S(2)}) %collective-permute-start.17) | collective-permute-done | bytes 253984 | tf_op jit(solution)/shard_map/ppermute | solution.py:233
  128.0 0.2 gathered.2.refs_0_
  128.2 1.8 %collective-permute-start.19 = (f32[10,496,128]{2,1,0:T(8,128)S(1)}, f32[10,496,128]{2,1,0:T(8,128)S(1)}, u32[]{:S(2)}, u32[]{:S(2)}) collective-permute-start(f32[10,496,128]{2,1,0:T(8,128)S(1)} %gathered.2.refs_0_), channel_id=1, source_target_pairs={{0,8},{8,0},{1,9},{9,1},{2,10},{10,2},{3,11},{11,3},{4,12},{12,4},... | collective-permute-start | bytes 7618568 | tf_op jit(solution)/shard_map/ppermute | solution.py:357
  130.1 1.5 %collective-permute-start.15 = (f32[496,128]{1,0:T(8,128)S(1)}, f32[496,128]{1,0:T(8,128)S(1)}, u32[]{:S(2)}, u32[]{:S(2)}) collective-permute-start(f32[496,128]{1,0:T(8,128)S(1)} %get-tuple-element.101), channel_id=1, source_target_pairs={{0,16},{16,32},{32,48},{48,0},{1,17},{17,33},{33,49},{49,1},{2,18}... | collective-permute-start | bytes 761864 | tf_op jit(solution)/shard_map/ppermute | solution.py:233
  131.5 2.9 %collective-permute-done.19.refs_1_ = f32[10,496,128]{2,1,0:T(8,128)S(1)} collective-permute-done((f32[10,496,128]{2,1,0:T(8,128)S(1)}, f32[10,496,128]{2,1,0:T(8,128)S(1)}, u32[]{:S(2)}, u32[]{:S(2)}) %collective-permute-start.19) | collective-permute-done | bytes 2539552 | tf_op jit(solution)/shard_map/ppermute | solution.py:357
  134.5 4.1 %write_weight.4.refs_2_ = f32[1984,1024]{1,0:T(8,128)} custom-call(s32[2]{0:T(128)S(1)} %pad_add_fusion.place, f32[1984,1024]{1,0:T(8,128)S(1)} %hold.1.weight, f32[10,496,128]{2,1,0:T(8,128)S(1)} %gathered.2.refs_0_, f32[10,496,128]{2,1,0:T(8,128)S(1)} %collective-permute-done.19.refs_1_, ...), custom_call_target="tpu_custom_call", output_to_operand_aliasing={{}: (4, {})} | custom-call | flops 1 | bytes 1024 | tf_op jit(solution)/shard_map/write_weight/pallas_call | solution.py:421
  138.5 0.1 collective-permute-done.15.refs_0_
  138.7 1.3 collective-permute-start.20
  139.9 1.5 %collective-permute-done.20.refs_1_ = f32[2,496,128]{2,1,0:T(8,128)S(1)} collective-permute-done((f32[2,496,128]{2,1,0:T(8,128)S(1)}, f32[2,496,128]{2,1,0:T(8,128)S(1)}, u32[]{:S(2)}, u32[]{:S(2)}) %collective-permute-start.20) | collective-permute-done | bytes 507936 | tf_op jit(solution)/shard_map/ppermute | solution.py:357
  141.5 1.8 %write_weight.5 = f32[1984,1024]{1,0:T(8,128)} custom-call(s32[2]{0:T(128)S(1)} %pad_add_fusion.place, f32[1984,1024]{1,0:T(8,128)S(1)} %hold.1.weight, f32[2,496,128]{2,1,0:T(8,128)S(1)} %gathered.3.refs_0_, f32[2,496,128]{2,1,0:T(8,128)S(1)} %collective-permute-done.20.refs_1_, f32[1984,1024]{1,0:T(8,128)} %write_weight.4.refs_2_), custom_call_target="tpu_custom_call", output_to_operand_aliasing={{}: (4, {})} | custom-call | flops 1 | bytes 1024 | tf_op jit(solution)/shard_map/write_weight/pallas_call | solution.py:421
  (31 shorter events, 0.4 us)
Async XLA Ops:
  0.6 4.0 %copy-start = (f32[1,1024,1984]{1,2,0:T(8,128)S(1)}, f32[1,1024,1984]{1,2,0:T(8,128)}, u32[]{:S(2)}) copy-start(f32[1,1024,1984]{1,2,0:T(8,128)} %param.10) | copy-start | bytes 24379396
  3.1 5.2 %collective-permute-start = (f32[496,1024]{1,0:T(8,128)S(1)}, f32[496,1024]{1,0:T(8,128)S(1)}, u32[]{:S(2)}, u32[]{:S(2)}) collective-permute-start(f32[496,1024]{1,0:T(8,128)S(1)} %take_part.2), channel_id=1, source_target_pairs={{0,8},{8,0},{1,9},{9,1},{2,10},{10,2},{3,11},{11,3},{4,12},{12,4},... | collective-permute-start | bytes 6094856 | tf_op jit(solution)/shard_map/ppermute | solution.py:447
  8.3 5.9 %collective-permute-start.5 = (f32[496,1024]{1,0:T(8,128)S(1)}, f32[496,1024]{1,0:T(8,128)S(1)}, u32[]{:S(2)}, u32[]{:S(2)}) collective-permute-start(f32[496,1024]{1,0:T(8,128)S(1)} %take_part.3), channel_id=1, source_target_pairs={{0,8},{8,0},{1,9},{9,1},{2,10},{10,2},{3,11},{11,3},{4,12},{12,4},... | collective-permute-start | bytes 6094856 | tf_op jit(solution)/shard_map/ppermute | solution.py:449
  10.2 30.4 %copy-start.1 = (s32[62,2048]{1,0:T(8,128)S(1)}, s32[62,2048]{1,0:T(8,128)}, u32[]{:S(2)}) copy-start(s32[62,2048]{1,0:T(8,128)} %m_codes) | copy-start | bytes 1523716
  10.2 30.4 %copy-start.2 = (s32[62,2048]{1,0:T(8,128)S(1)}, s32[62,2048]{1,0:T(8,128)}, u32[]{:S(2)}) copy-start(s32[62,2048]{1,0:T(8,128)} %v_codes.1) | copy-start | bytes 1523716
  10.2 30.4 %copy-start.3 = (f32[256]{0:T(256)S(1)}, f32[256]{0:T(256)}, u32[]{:S(2)}) copy-start(f32[256]{0:T(256)} %param.15) | copy-start | bytes 3076
  10.2 30.4 %copy-start.4 = (f32[256]{0:T(256)S(1)}, f32[256]{0:T(256)}, u32[]{:S(2)}) copy-start(f32[256]{0:T(256)} %param.16) | copy-start | bytes 3076
  10.2 30.4 %copy-start.5 = (f32[62]{0:T(128)S(1)}, f32[62]{0:T(128)}, u32[]{:S(2)}) copy-start(f32[62]{0:T(128)} %m_scale.1) | copy-start | bytes 748
  10.2 30.4 %copy-start.6 = (f32[62]{0:T(128)S(1)}, f32[62]{0:T(128)}, u32[]{:S(2)}) copy-start(f32[62]{0:T(128)} %v_scale.1) | copy-start | bytes 748
  10.2 15.7 %collective-permute-start.1 = (f32[2,496,128]{2,1,0:T(8,128)S(1)}, f32[2,496,128]{2,1,0:T(8,128)S(1)}, u32[]{:S(2)}, u32[]{:S(2)}) collective-permute-start(f32[2,496,128]{2,1,0:T(8,128)S(1)} %get-tuple-element.60), channel_id=1, source_target_pairs={{0,16},{16,32},{32,48},{48,0},{1,17},{17,33},{33,49},{49,1},{2,18}... | collective-permute-start | bytes 1523720 | tf_op jit(solution)/shard_map/ppermute | solution.py:233
  12.0 13.9 %collective-permute-start.2 = (f32[2,496,128]{2,1,0:T(8,128)S(1)}, f32[2,496,128]{2,1,0:T(8,128)S(1)}, u32[]{:S(2)}, u32[]{:S(2)}) collective-permute-start(f32[2,496,128]{2,1,0:T(8,128)S(1)} %get-tuple-element.61), channel_id=1, source_target_pairs={{0,48},{16,0},{32,16},{48,32},{1,49},{17,1},{33,17},{49,33},{2,50}... | collective-permute-start | bytes 1523720 | tf_op jit(solution)/shard_map/ppermute | solution.py:233
  15.7 21.1 %collective-permute-start.6 = (f32[2,496,128]{2,1,0:T(8,128)S(1)}, f32[2,496,128]{2,1,0:T(8,128)S(1)}, u32[]{:S(2)}, u32[]{:S(2)}) collective-permute-start(f32[2,496,128]{2,1,0:T(8,128)S(1)} %get-tuple-element.70), channel_id=1, source_target_pairs={{0,16},{16,32},{32,48},{48,0},{1,17},{17,33},{33,49},{49,1},{2,18}... | collective-permute-start | bytes 1523720 | tf_op jit(solution)/shard_map/ppermute | solution.py:233
  15.8 21.1 %collective-permute-start.7 = (f32[2,496,128]{2,1,0:T(8,128)S(1)}, f32[2,496,128]{2,1,0:T(8,128)S(1)}, u32[]{:S(2)}, u32[]{:S(2)}) collective-permute-start(f32[2,496,128]{2,1,0:T(8,128)S(1)} %get-tuple-element.71), channel_id=1, source_target_pairs={{0,48},{16,0},{32,16},{48,32},{1,49},{17,1},{33,17},{49,33},{2,50}... | collective-permute-start | bytes 1523720 | tf_op jit(solution)/shard_map/ppermute | solution.py:233
  26.1 20.3 %collective-permute-start.3 = (f32[496,128]{1,0:T(8,128)S(1)}, f32[496,128]{1,0:T(8,128)S(1)}, u32[]{:S(2)}, u32[]{:S(2)}) collective-permute-start(f32[496,128]{1,0:T(8,128)S(1)} %get-tuple-element.63), channel_id=1, source_target_pairs={{0,16},{16,32},{32,48},{48,0},{1,17},{17,33},{33,49},{49,1},{2,18}... | collective-permute-start | bytes 761864 | tf_op jit(solution)/shard_map/ppermute | solution.py:233
  26.6 19.8 %collective-permute-start.4 = (f32[496,128]{1,0:T(8,128)S(1)}, f32[496,128]{1,0:T(8,128)S(1)}, u32[]{:S(2)}, u32[]{:S(2)}) collective-permute-start(f32[496,128]{1,0:T(8,128)S(1)} %get-tuple-element.64), channel_id=1, source_target_pairs={{0,48},{16,0},{32,16},{48,32},{1,49},{17,1},{33,17},{49,33},{2,50}... | collective-permute-start | bytes 761864 | tf_op jit(solution)/shard_map/ppermute | solution.py:233
  37.0 10.7 %collective-permute-start.8 = (f32[496,128]{1,0:T(8,128)S(1)}, f32[496,128]{1,0:T(8,128)S(1)}, u32[]{:S(2)}, u32[]{:S(2)}) collective-permute-start(f32[496,128]{1,0:T(8,128)S(1)} %get-tuple-element.73), channel_id=1, source_target_pairs={{0,16},{16,32},{32,48},{48,0},{1,17},{17,33},{33,49},{49,1},{2,18}... | collective-permute-start | bytes 761864 | tf_op jit(solution)/shard_map/ppermute | solution.py:233
  37.5 10.2 %collective-permute-start.9 = (f32[496,128]{1,0:T(8,128)S(1)}, f32[496,128]{1,0:T(8,128)S(1)}, u32[]{:S(2)}, u32[]{:S(2)}) collective-permute-start(f32[496,128]{1,0:T(8,128)S(1)} %get-tuple-element.74), channel_id=1, source_target_pairs={{0,48},{16,0},{32,16},{48,32},{1,49},{17,1},{33,17},{49,33},{2,50}... | collective-permute-start | bytes 761864 | tf_op jit(solution)/shard_map/ppermute | solution.py:233
  95.2 7.0 %collective-permute-start.14 = (f32[4,496,128]{2,1,0:T(8,128)S(1)}, f32[4,496,128]{2,1,0:T(8,128)S(1)}, u32[]{:S(2)}, u32[]{:S(2)}) collective-permute-start(f32[4,496,128]{2,1,0:T(8,128)S(1)} %get-tuple-element.89.refs_0_), channel_id=1, source_target_pairs={{0,8},{8,0},{1,9},{9,1},{2,10},{10,2},{3,11},{11,3},{4,12},{12,4},... | collective-permute-start | bytes 3047432 | tf_op jit(solution)/shard_map/ppermute | solution.py:357
  95.3 13.3 %collective-permute-start.13 = (f32[2,496,128]{2,1,0:T(8,128)S(1)}, f32[2,496,128]{2,1,0:T(8,128)S(1)}, u32[]{:S(2)}, u32[]{:S(2)}) collective-permute-start(f32[2,496,128]{2,1,0:T(8,128)S(1)} %get-tuple-element.88), channel_id=1, source_target_pairs={{0,48},{16,0},{32,16},{48,32},{1,49},{17,1},{33,17},{49,33},{2,50}... | collective-permute-start | bytes 1523720 | tf_op jit(solution)/shard_map/ppermute | solution.py:233
  98.1 13.6 %collective-permute-start.12 = (f32[2,496,128]{2,1,0:T(8,128)S(1)}, f32[2,496,128]{2,1,0:T(8,128)S(1)}, u32[]{:S(2)}, u32[]{:S(2)}) collective-permute-start(f32[2,496,128]{2,1,0:T(8,128)S(1)} %get-tuple-element.88), channel_id=1, source_target_pairs={{0,16},{16,32},{32,48},{48,0},{1,17},{17,33},{33,49},{49,1},{2,18}... | collective-permute-start | bytes 1523720 | tf_op jit(solution)/shard_map/ppermute | solution.py:233
  98.1 21.4 %collective-permute-start.11 = (f32[2,496,128]{2,1,0:T(8,128)S(1)}, f32[2,496,128]{2,1,0:T(8,128)S(1)}, u32[]{:S(2)}, u32[]{:S(2)}) collective-permute-start(f32[2,496,128]{2,1,0:T(8,128)S(1)} %get-tuple-element.87), channel_id=1, source_target_pairs={{0,48},{16,0},{32,16},{48,32},{1,49},{17,1},{33,17},{49,33},{2,50}... | collective-permute-start | bytes 1523720 | tf_op jit(solution)/shard_map/ppermute | solution.py:233
  100.8 21.8 %collective-permute-start.10 = (f32[2,496,128]{2,1,0:T(8,128)S(1)}, f32[2,496,128]{2,1,0:T(8,128)S(1)}, u32[]{:S(2)}, u32[]{:S(2)}) collective-permute-start(f32[2,496,128]{2,1,0:T(8,128)S(1)} %get-tuple-element.87), channel_id=1, source_target_pairs={{0,16},{16,32},{32,48},{48,0},{1,17},{17,33},{33,49},{49,1},{2,18}... | collective-permute-start | bytes 1523720 | tf_op jit(solution)/shard_map/ppermute | solution.py:233
  111.8 13.2 %collective-permute-start.18 = (f32[496,128]{1,0:T(8,128)S(1)}, f32[496,128]{1,0:T(8,128)S(1)}, u32[]{:S(2)}, u32[]{:S(2)}) collective-permute-start(f32[496,128]{1,0:T(8,128)S(1)} %get-tuple-element.104), channel_id=1, source_target_pairs={{0,48},{16,0},{32,16},{48,32},{1,49},{17,1},{33,17},{49,33},{2,50}... | collective-permute-start | bytes 761864 | tf_op jit(solution)/shard_map/ppermute | solution.py:233
  112.1 15.9 %collective-permute-start.17 = (f32[496,128]{1,0:T(8,128)S(1)}, f32[496,128]{1,0:T(8,128)S(1)}, u32[]{:S(2)}, u32[]{:S(2)}) collective-permute-start(f32[496,128]{1,0:T(8,128)S(1)} %get-tuple-element.98), channel_id=1, source_target_pairs={{0,16},{16,32},{32,48},{48,0},{1,17},{17,33},{33,49},{49,1},{2,18}... | collective-permute-start | bytes 761864 | tf_op jit(solution)/shard_map/ppermute | solution.py:233
  128.2 6.3 %collective-permute-start.19 = (f32[10,496,128]{2,1,0:T(8,128)S(1)}, f32[10,496,128]{2,1,0:T(8,128)S(1)}, u32[]{:S(2)}, u32[]{:S(2)}) collective-permute-start(f32[10,496,128]{2,1,0:T(8,128)S(1)} %gathered.2.refs_0_), channel_id=1, source_target_pairs={{0,8},{8,0},{1,9},{9,1},{2,10},{10,2},{3,11},{11,3},{4,12},{12,4},... | collective-permute-start | bytes 7618568 | tf_op jit(solution)/shard_map/ppermute | solution.py:357
  130.1 8.5 %collective-permute-start.16 = (f32[496,128]{1,0:T(8,128)S(1)}, f32[496,128]{1,0:T(8,128)S(1)}, u32[]{:S(2)}, u32[]{:S(2)}) collective-permute-start(f32[496,128]{1,0:T(8,128)S(1)} %get-tuple-element.102), channel_id=1, source_target_pairs={{0,48},{16,0},{32,16},{48,32},{1,49},{17,1},{33,17},{49,33},{2,50}... | collective-permute-start | bytes 761864 | tf_op jit(solution)/shard_map/ppermute | solution.py:233
  130.1 8.6 %collective-permute-start.15 = (f32[496,128]{1,0:T(8,128)S(1)}, f32[496,128]{1,0:T(8,128)S(1)}, u32[]{:S(2)}, u32[]{:S(2)}) collective-permute-start(f32[496,128]{1,0:T(8,128)S(1)} %get-tuple-element.101), channel_id=1, source_target_pairs={{0,16},{16,32},{32,48},{48,0},{1,17},{17,33},{33,49},{49,1},{2,18}... | collective-permute-start | bytes 761864 | tf_op jit(solution)/shard_map/ppermute | solution.py:233
  138.7 2.8 %collective-permute-start.20 = (f32[2,496,128]{2,1,0:T(8,128)S(1)}, f32[2,496,128]{2,1,0:T(8,128)S(1)}, u32[]{:S(2)}, u32[]{:S(2)}) collective-permute-start(f32[2,496,128]{2,1,0:T(8,128)S(1)} %gathered.3.refs_0_), channel_id=1, source_target_pairs={{0,8},{8,0},{1,9},{9,1},{2,10},{10,2},{3,11},{11,3},{4,12},{12,4},... | collective-permute-start | bytes 1523720 | tf_op jit(solution)/shard_map/ppermute | solution.py:357

commit v4 on v3

v4 whole, which is shorter than its diff:
```python
import functools

import jax
import jax.numpy as jnp
from jax import lax
from jax.experimental import pallas as pl
from jax.experimental.pallas import tpu as pltpu
from jax.sharding import Mesh, PartitionSpec as P

BLOCK = 2048
LANES = 128
N_YH, N_Z, N_CORE, N_YL, N_X = 2, 4, 2, 2, 4
N_TENSOR = N_YL * N_X
OWNERS = N_CORE * N_TENSOR
AXES = ("yh", "z", "core", "yl", "x")
DP = ("yh", "z", "core")
TENSOR = ("yl", "x")
ROW_OWNERS = ("yh", "core", "yl", "x")
WIDTH = 400
BACK = 496
FIRST = 192
HALF = FIRST // 2
PLAIN = 2 * WIDTH
SENT = PLAIN + HALF

beta_one = 0.9
beta_two = 0.999
adam_eps = 1e-08
learn_rate = 0.02
decay_rate = 0.1
scale_eps = 1e-06

SWAP = [(0, 1), (1, 0)]
UP = [(i, (i + 1) % N_Z) for i in range(N_Z)]
DOWN = [(i, (i - 1) % N_Z) for i in range(N_Z)]
ACROSS = [(i, (i + 2) % N_Z) for i in range(N_Z)]

ANY = pl.BlockSpec(memory_space=pl.ANY)
SMEM = pl.BlockSpec(memory_space=pltpu.SMEM)
VMEM = pl.BlockSpec(memory_space=pltpu.VMEM)
f32 = jnp.float32
COST = pl.CostEstimate(flops=1, bytes_accessed=1024, transcendentals=0)


def shape(*dims):
    return jax.ShapeDtypeStruct(dims, f32)


def params():
    return pltpu.CompilerParams(vmem_limit_bytes=10 * 2**20)


def lane_tile(yh, z):
    return pl.ds(pl.multiple_of((yh * N_Z + lax.rem(z, N_Z)) * LANES, LANES), LANES)


def each(count, body):
    for r in range(0, count, 8):
        body(slice(r, r + 8))


def segments(rows, row):
    for r in range(rows):
        at = r * row
        while at < (r + 1) * row:
            end = min((r + 1) * row, (at // BLOCK + 1) * BLOCK)
            b = at // BLOCK
            yield r, slice(at - r * row, end - r * row), b, slice(at - b * BLOCK, end - b * BLOCK)
            at = end


def owned(half, owner):
    c, j = divmod(owner, N_TENSOR)
    at = j * N_CORE * half + c * half
    return slice(at, at + half)


def old_state_kernel(half, m_codes, v_codes, m_scale, v_scale, code_m, code_v, m_out, v_out, held, flat):
    outs = (m_out, v_out)
    blocks = m_codes.shape[0]
    for which, (codes, scale, table) in enumerate(((m_codes, m_scale, code_m), (v_codes, v_scale, code_v))):
        low = jnp.broadcast_to(table[0:1, :], (8, LANES))
        high = jnp.broadcast_to(table[1:2, :], (8, LANES))
        for r in range(0, blocks, 8):
            rows = slice(min(r, blocks - 8), min(r, blocks - 8) + 8)
            for k in range(0, BLOCK, LANES):
                index = codes[rows, k : k + LANES]
                lane = index & (LANES - 1)
                a = jnp.take_along_axis(low, lane, axis=1)
                b = jnp.take_along_axis(high, lane, axis=1)
                held[rows, k : k + LANES] = jnp.where(index < LANES, a, b)
        for r, columns, b, inside in segments(*flat.shape):
            flat[r : r + 1, columns] = held[b : b + 1, inside] * scale[b]
        for owner in range(OWNERS):
            outs[which][owner] = flat[:, owned(half, owner)]


def old_state(m_codes, v_codes, m_absmax, v_absmax, code_m, code_v, half):
    rows = LANES // OWNERS
    return pl.pallas_call(
        functools.partial(old_state_kernel, half),
        in_specs=[VMEM, VMEM, SMEM, SMEM, VMEM, VMEM],
        out_specs=[VMEM] * 2,
        out_shape=[shape(OWNERS, rows, half)] * 2,
        scratch_shapes=[pltpu.VMEM(m_codes.shape, f32), pltpu.VMEM((rows, N_CORE * half * N_TENSOR), f32)],
        compiler_params=params(),
        cost_estimate=COST,
        name="old_state",
    )(m_codes, v_codes, m_absmax, v_absmax, code_m.reshape(2, LANES), code_v.reshape(2, LANES))


def new_state_kernel(half, m_in, v_in, *refs):
    outs, (held, flat) = refs[:4], refs[4:]
    blocks = outs[0].shape[0]
    for which, values in enumerate((m_in, v_in)):
        for owner in range(OWNERS):
            flat[:, owned(half, owner)] = values[owner]
        for r, columns, b, inside in segments(*flat.shape):
            held[b : b + 1, inside] = flat[r : r + 1, columns]
        value = held[...]
        largest = jnp.max(jnp.abs(value) if which == 0 else value, axis=1, keepdims=True)
        outs[which][...] = (value / (largest + scale_eps)).astype(jnp.bfloat16)[:blocks]
        outs[2 + which][...] = jnp.broadcast_to(largest, (held.shape[0], LANES)).T[0:1, :blocks]


def new_state(m_new, v_new, blocks, half):
    rows = LANES // OWNERS
    scaled = jax.ShapeDtypeStruct((blocks, BLOCK), jnp.bfloat16)
    m_scaled, v_scaled, m_absmax, v_absmax = pl.pallas_call(
        functools.partial(new_state_kernel, half),
        in_specs=[VMEM] * 2,
        out_specs=[VMEM] * 4,
        out_shape=[scaled, scaled, shape(1, blocks), shape(1, blocks)],
        scratch_shapes=[
            pltpu.VMEM((pl.cdiv(blocks, 8) * 8, BLOCK), f32),
            pltpu.VMEM((rows, N_CORE * half * N_TENSOR), f32),
        ],
        compiler_params=params(),
        cost_estimate=COST,
        name="new_state",
    )(m_new, v_new)
    return m_scaled, v_scaled, m_absmax[0], v_absmax[0]


def in_hbm(array):
    return pltpu.with_memory_space_constraint(array, pltpu.HBM)


def columns_at(core, half, start, width):
    return pl.ds(pl.multiple_of(core * half + start, 8), width)


def take_kernel(half, start, place, source, send, sem):
    rows = columns_at(1 - place[0], half, start, send.shape[0])
    copy = pltpu.make_async_copy(source.at[rows], send, sem)
    copy.start()
    copy.wait()


def take(place, source, start, width, spec):
    return pl.pallas_call(
        functools.partial(take_kernel, source.shape[0] // N_CORE, start),
        in_specs=[SMEM, spec],
        out_specs=VMEM,
        out_shape=shape(width, source.shape[1]),
        scratch_shapes=[pltpu.SemaphoreType.DMA],
        compiler_params=params(),
        cost_estimate=COST,
        name="take_part",
    )(place, source)


def pack_tiles(place, source, base, other, up, down, keep):
    z = place[1]
    rows = other.shape[0]
    for out, slot, yh, to in (
        (up, 0, 0, 2),
        (down, 0, 1, 2),
        (up, 1, 1, 1),
        (down, 1, 0, 3),
        (keep, 0, 0, 1),
        (keep, 1, 1, 3),
        (keep, 2, 0, 0),
        (keep, 3, 1, 0),
    ):
        lanes = lane_tile(yh, z + to)
        one = source.at[pl.ds(pl.multiple_of(base, 8), rows), lanes]
        two = other.at[:, lanes]

        def body(r):
            out[slot, r, :] = one[r, :] + two[r, :]

        each(rows, body)


def pack_kernel(half, start, place, source, other, up, down, keep):
    pack_tiles(place, source, place[0] * half + start, other, up, down, keep)


def packed(width):
    return [shape(n, width, LANES) for n in (2, 2, 4)]


def pack(place, source, other, half, start):
    return pl.pallas_call(
        functools.partial(pack_kernel, half, start),
        in_specs=[SMEM, VMEM, VMEM],
        out_specs=[VMEM] * 3,
        out_shape=packed(other.shape[0]),
        compiler_params=params(),
        cost_estimate=COST,
        name="pack",
    )(place, source, other)


def pack_rest_kernel(half, place, grad, other, up, down, keep, send, mine):
    c, yh = place[0], place[2]
    for out, which in ((send, 1 - yh), (mine, yh)):
        at = which * HALF
        one = grad.at[pl.ds(pl.multiple_of(c * half + PLAIN + at, 8), HALF)]
        two = other.at[pl.ds(pl.multiple_of(WIDTH + at, 8), HALF)]

        def body(r):
            out[r, :] = one[r, :] + two[r, :]

        each(HALF, body)
    pack_tiles(place, grad, c * half + WIDTH, other.at[:WIDTH], up, down, keep)


def pack_rest(place, grad_t, other):
    return pl.pallas_call(
        functools.partial(pack_rest_kernel, grad_t.shape[0] // N_CORE),
        in_specs=[SMEM, VMEM, VMEM],
        out_specs=[VMEM] * 5,
        out_shape=packed(WIDTH) + [shape(HALF, grad_t.shape[1])] * 2,
        compiler_params=params(),
        cost_estimate=COST,
        name="pack_rest",
    )(place, grad_t, other)


def relay_kernel(keep, up, down, up2, down2, rest):
    def body(r):
        up2[r, :] = keep[0, r, :] + up[0, r, :]
        down2[r, :] = keep[1, r, :] + down[0, r, :]
        rest[0, r, :] = keep[2, r, :] + down[1, r, :]
        rest[1, r, :] = keep[3, r, :] + up[1, r, :]

    each(keep.shape[1], body)


def relay(keep, up, down):
    tile = keep.shape[1:]
    return pl.pallas_call(
        relay_kernel,
        in_specs=[VMEM] * 3,
        out_specs=[VMEM] * 3,
        out_shape=[shape(*tile), shape(*tile), shape(N_YH, *tile)],
        compiler_params=params(),
        cost_estimate=COST,
        name="relay",
    )(keep, up, down)


def relay_pack_kernel(place, keep, up, down, mine, arrived, up2, down2, across, rest, own):
    z = place[1]

    def body(r):
        up2[r, :] = keep[0, r, :] + up[0, r, :]
        down2[r, :] = keep[1, r, :] + down[0, r, :]
        rest[0, r, :] = keep[2, r, :] + down[1, r, :]
        rest[1, r, :] = keep[3, r, :] + up[1, r, :]

    each(WIDTH, body)
    for yh in range(N_YH):
        part = pl.ds(WIDTH + yh * HALF, HALF)
        for out, to in ((own.at[yh], 0), (up2.at[part], 1), (across.at[yh], 2), (down2.at[part], 3)):
            lanes = lane_tile(yh, z + to)
            one, two = mine.at[:, lanes], arrived.at[:, lanes]

            def third(r):
                out[r, :] = one[r, :] + two[r, :]

            each(HALF, third)


def relay_pack(place, keep, up, down, mine, arrived):
    sent = shape(WIDTH + N_YH * HALF, LANES)
    third = shape(N_YH, HALF, LANES)
    return pl.pallas_call(
        relay_pack_kernel,
        in_specs=[SMEM] + [VMEM] * 5,
        out_specs=[VMEM] * 5,
        out_shape=[sent, sent, third, shape(N_YH, WIDTH, LANES), third],
        compiler_params=params(),
        cost_estimate=COST,
        name="relay_pack",
    )(place, keep, up, down, mine, arrived)


def ring(up, down):
    return lax.ppermute(up, "z", UP), lax.ppermute(down, "z", DOWN)


def turn_kernel(rest_0, up_0, down_0, own, across, rest_1, up_1, down_1, out, held):
    for yh in range(N_YH):
        low, high = ((up_0, up_1), (down_0, down_1))[yh]
        held[:WIDTH, :] = rest_0[yh] + low[:WIDTH, :]
        held[WIDTH:PLAIN, :] = rest_1[yh] + high[...]
        part = pl.ds(WIDTH + yh * HALF, HALF)
        held[PLAIN:SENT, :] = own[yh] + up_0[part, :] + down_0[part, :] + across[yh]
        out[yh * OWNERS : (yh + 1) * OWNERS] = held[...].T[:, :SENT].reshape(OWNERS, -1, SENT)


def turn(sums):
    return pl.pallas_call(
        turn_kernel,
        in_specs=[VMEM] * len(sums),
        out_specs=VMEM,
        out_shape=shape(N_YH * OWNERS, LANES // OWNERS, SENT),
        scratch_shapes=[pltpu.VMEM((pl.cdiv(SENT, LANES) * LANES, LANES), f32)],
        compiler_params=params(),
        cost_estimate=COST,
        name="turn",
    )(*sums)


def exchange(array):
    return lax.all_to_all(array, ROW_OWNERS, split_axis=0, concat_axis=0, tiled=True)


def adam_kernel(fixes, grads, m_old, v_old, m_out, v_out, update, held):
    for owner in range(OWNERS):
        held[owner, :, :SENT] = grads[owner]
        held[owner, :, :PLAIN] += grads[OWNERS + owner, :, :PLAIN]
        held[owner, :, SENT:] = grads[OWNERS + owner, :, PLAIN:]
        grad = held[owner]
        m_new = beta_one * m_old[owner] + (1.0 - beta_one) * grad
        v_new = beta_two * v_old[owner] + (1.0 - beta_two) * grad * grad
        m_out[owner] = m_new
        v_out[owner] = v_new
        value = m_new / fixes[0] / (jnp.sqrt(v_new / fixes[1]) + adam_eps)
        update[owner] = value
        update[OWNERS + owner] = value


def adam(fixes, grads, m_old, v_old):
    return pl.pallas_call(
        adam_kernel,
        in_specs=[SMEM] + [VMEM] * 3,
        out_specs=[VMEM] * 3,
        out_shape=[shape(*m_old.shape), shape(*m_old.shape), shape(2 * OWNERS, *m_old.shape[1:])],
        scratch_shapes=[pltpu.VMEM(m_old.shape, f32)],
        compiler_params=params(),
        cost_estimate=COST,
        name="adam",
    )(fixes, grads, m_old, v_old)


def unturn_kernel(rows, low, high, near, held):
    columns = rows.shape[2]
    for yh in range(N_YH):
        held[:, :columns] = rows[yh * OWNERS : (yh + 1) * OWNERS].reshape(LANES, columns)
        turned = held[...].T
        low[yh] = turned[:BACK]
        high[yh] = turned[BACK : 2 * BACK]
        near[yh] = turned[: 2 * BACK]


def unturn(back):
    columns = back.shape[2]
    return pl.pallas_call(
        unturn_kernel,
        in_specs=[VMEM],
        out_specs=[VMEM] * 3,
        out_shape=[shape(N_YH, width, LANES) for width in (BACK, BACK, columns)],
        scratch_shapes=[pltpu.VMEM((LANES, pl.cdiv(columns, LANES) * LANES), f32)],
        compiler_params=params(),
        cost_estimate=COST,
        name="unturn",
    )(back)


def relayed_kernel(up, down, up_out, down_out):
    up_out[...] = up[0]
    down_out[...] = down[1]


def relayed(up, down):
    return pl.pallas_call(
        relayed_kernel,
        in_specs=[VMEM] * 2,
        out_specs=[VMEM] * 2,
        out_shape=[shape(*up.shape[1:])] * 2,
        compiler_params=params(),
        cost_estimate=COST,
        name="relayed",
    )(up, down)


def gathered_kernel(*refs):
    pieces, out = refs[:-1], refs[-1]
    at = 0
    for piece in pieces:
        tiles = [piece[...]] if len(piece.shape) == 2 else [piece[k] for k in range(piece.shape[0])]
        for tile in tiles:
            out[at] = tile
            at += 1


def gathered(*pieces):
    count = sum(p.shape[0] if p.ndim == 3 else 1 for p in pieces)
    return pl.pallas_call(
        gathered_kernel,
        in_specs=[VMEM] * len(pieces),
        out_specs=VMEM,
        out_shape=shape(count, *pieces[0].shape[-2:]),
        compiler_params=params(),
        cost_estimate=COST,
        name="gathered",
    )(*pieces)


def weight_kernel(spots, place, weight, mine, theirs, *refs):
    out, held, sem = refs[-3:]
    c, z = place[0], place[1]
    half = weight.shape[0] // N_CORE
    width = mine.shape[1]
    stores = []
    for piece, core in ((mine, c), (theirs, 1 - c)):
        for slot, (start, yh, to) in enumerate(spots):
            rows = pl.ds(pl.multiple_of(core * half + start, 8), width)
            lanes = lane_tile(yh, z + to)
            old = weight.at[rows, lanes]
            where = held.at[len(stores)]

            def body(r):
                where[r, :] = old[r, :] - learn_rate * (piece[slot, r, :] + decay_rate * old[r, :])

            each(width, body)
            stores.append(pltpu.make_async_copy(where, out.at[rows, lanes], sem.at[len(stores)]))
            stores[-1].start()
    for store in stores:
        store.wait()


def hold_kernel(source, out, sem):
    copy = pltpu.make_async_copy(source, out, sem)
    copy.start()
    copy.wait()


def hold(array):
    return pl.pallas_call(
        hold_kernel,
        in_specs=[pl.BlockSpec(memory_space=pltpu.HBM)],
        out_specs=VMEM,
        out_shape=shape(*array.shape),
        scratch_shapes=[pltpu.SemaphoreType.DMA],
        compiler_params=params(),
        cost_estimate=COST,
        name="hold",
    )(in_hbm(array))


NEAR = ((0, 0, 0), (0, 1, 0))
SIDES = tuple((at, yh, to) for at in (0, BACK) for to in (3, 1) for yh in range(N_YH)) + ((0, 0, 2), (0, 1, 2))
FAR = ((BACK, 0, 2), (BACK, 1, 2))


def write_weight(place, held, piece, spots, so_far):
    done = [] if so_far is None else [so_far]
    stores = N_CORE * len(spots)
    hbm = pl.BlockSpec(memory_space=pltpu.HBM)
    return pl.pallas_call(
        functools.partial(weight_kernel, spots),
        in_specs=[SMEM] + [VMEM] * 3 + [hbm] * len(done),
        out_specs=hbm,
        out_shape=shape(*held.shape),
        input_output_aliases={4: 0} if done else {},
        scratch_shapes=[pltpu.VMEM((stores, *piece.shape[1:]), f32), pltpu.SemaphoreType.DMA((stores,))],
        compiler_params=params(),
        cost_estimate=COST,
        name="write_weight",
    )(place, held, piece, lax.ppermute(piece, "core", SWAP), *done)


def after(value, *others):
    return lax.optimization_barrier((value, *others))[0]


def shards(weight, grad_parts, m_codes, v_codes, m_absmax, v_absmax, code_m, code_v, step):
    half = weight.shape[1] // N_CORE
    place = jnp.stack([lax.axis_index(a) for a in ("core", "z", "yh")]).astype(jnp.int32)
    grad_t = grad_parts[0].T
    weight_t = weight.T

    send_0 = take(place, in_hbm(grad_t), 0, WIDTH, pl.BlockSpec(memory_space=pltpu.HBM))
    other_0 = lax.ppermute(send_0, "core", SWAP)
    send_1 = take(after(place, send_0), grad_t, WIDTH, WIDTH + FIRST, VMEM)
    up, down, keep_0 = pack(place, grad_t, other_0, half, 0)
    up_0, down_0 = ring(up, down)
    other_1 = lax.ppermute(after(send_1, keep_0), "core", SWAP)
    up, down, keep_1, send, mine = pack_rest(place, grad_t, other_1)
    arrived = lax.ppermute(send, "yh", SWAP)
    up_1, down_1 = ring(up, down)
    up2, down2, across, rest_0, own = relay_pack(place, keep_0, up_0, down_0, mine, arrived)
    across = lax.ppermute(across, "z", ACROSS)
    sums_0 = (rest_0, *ring(up2, down2), own, across)
    up2, down2, rest_1 = relay(after(keep_1, rest_0), up_1, down_1)
    sums_1 = (rest_1, *ring(up2, down2))

    count = step[0].astype(f32)
    fix_one = 1.0 - jnp.power(f32(beta_one), count)
    fix_two = 1.0 - jnp.power(f32(beta_two), count)
    fixes = jnp.stack([fix_one, fix_two])
    olds = old_state(after(m_codes, rest_1), v_codes, m_absmax, v_absmax, code_m, code_v, half)
    sums = lax.optimization_barrier((*sums_0, *sums_1, *olds, fixes))[:8]

    grads = exchange(turn(sums))
    m_new, v_new, update = adam(fixes, grads, *olds)
    pair_0, pair_1, near = unturn(exchange(update))

    up_0, down_0 = ring(pair_0, pair_0)
    up_1, down_1 = ring(pair_1, pair_1)
    held = hold(after(weight_t, near))
    new_weight = write_weight(place, held, near, NEAR, None)
    state = new_state(m_new, v_new, m_codes.shape[0], half)
    up_0, down_0, new_weight, *state = lax.optimization_barrier((up_0, down_0, new_weight, *state))
    up2, down2 = relayed(up_0, down_0)
    up_1, down_1 = lax.optimization_barrier((up_1, down_1, up2))[:2]
    far_0 = ring(up2, down2)
    up2, down2 = relayed(up_1, down_1)
    sides = gathered(up_0, down_0, up_1, after(down_1, up2), *far_0)
    up2, down2 = ring(up2, down2)
    new_weight = write_weight(place, held, sides, SIDES, new_weight)
    up2, down2, new_weight = lax.optimization_barrier((up2, down2, new_weight))
    new_weight = write_weight(place, held, gathered(up2, down2), FAR, new_weight)
    return (new_weight.T, *state)


def solution(mesh):
    fine = Mesh(mesh.devices.reshape(N_YH, N_Z, N_CORE, N_YL, N_X), AXES)
    blocks = P(DP + TENSOR)
    in_specs = (P(None, TENSOR), P(DP, None, TENSOR), blocks, blocks, blocks, blocks, P(), P(), P())
    out_specs = (P(None, TENSOR), blocks, blocks, blocks, blocks)
    return jax.shard_map(shards, mesh=fine, in_specs=in_specs, out_specs=out_specs, check_vma=False)
```

time: 144 us -> 139 us (0.965)
  waiting for transfers between devices: 46.1 us -> 38.3 us
  starting transfers between devices: 25.8 us -> 30.9 us
  Pallas kernels: 23.9 us -> 21.5 us
    ppermute x16, waiting for transfers between devices: 38.8 us -> 21.5 us  [ring(): return (lax.ppermute(up, 'z', UP), lax.ppermute(down, 'z', DOWN))]
    ppermute x4 -> x6, waiting for transfers between devices: 4.46 us -> 14.5 us  [the longest x1 5.92 us: shards(): across = lax.ppermute(across, 'z', ACROSS)]
    ppermute x4 -> x6, starting transfers between devices: 3.63 us -> 7.64 us  [the longest x3 3.08 us: write_weight(): lax.ppermute(piece, 'core', SWAP)]
    pallas_call x9 -> x10, Pallas kernels: 15.2 us -> 13.1 us  [the longest x3 6.58 us: write_weight(): pl.pallas_call(functools.partial(weight_kernel, spots), in_specs=[SMEM] +...]
  transfers between devices with their start and end apart: 21 -> 23, of which waited for: 13 -> 16; matrix products, arithmetic and copies ran while one was open for 0% -> 0% of each run, Pallas kernels for 12% -> 11%
where the time goes in v4:
time: 139 us
  blocking collectives  46 us (33%)
  waiting for transfers between devices  38.3 us (28%)
  starting transfers between devices  30.9 us (22%)
  Pallas kernels  21.5 us (15%)
  between operations  1.76 us (1%)
    all_to_all x2, blocking collectives, exchange(): lax.all_to_all(array, ROW_OWNERS, split_axis=0, concat_axis=0, tiled=True)  46 us
    ppermute x16, starting transfers between devices, ring(): return (lax.ppermute(up, 'z', UP), lax.ppermute(down, 'z', DOWN))  21.7 us
    ppermute x16, waiting for transfers between devices, ring(): return (lax.ppermute(up, 'z', UP), lax.ppermute(down, 'z', DOWN))  21.5 us
    pallas_call x3, Pallas kernels, write_weight(): pl.pallas_call(functools.partial(weight_kernel, spots), in_specs=[SMEM] +...  6.58 us
    ppermute x1, waiting for transfers between devices, shards(): across = lax.ppermute(across, 'z', ACROSS)  5.92 us
    ppermute x3, waiting for transfers between devices, write_weight(): lax.ppermute(piece, 'core', SWAP)  4.45 us
    ppermute x1, waiting for transfers between devices, shards(): arrived = lax.ppermute(send, 'yh', SWAP)  3.74 us
    pallas_call x1, Pallas kernels, hold(): pl.pallas_call(hold_kernel, in_specs=[pl.BlockSpec(memory_space=pltpu.HBM...  3.31 us
  transfers between devices with their start and end apart: 23, of which 16 were waited for; matrix products, arithmetic and copies ran while one was open for 0% of the time, Pallas kernels for 11%

profile of v4, /device:TPU:1, one launch (start us, length us, event | category | flops | bytes accessed | tf_op | source)
XLA Modules:
  0.0 138.6 jit_solution(6295724851916441027)
XLA Ops:
  0.7 2.2 %take_part.2 = f32[400,1024]{1,0:T(8,128)S(1)} custom-call(s32[3]{0:T(128)S(1)} %pad_add_fusion.place, f32[1984,1024]{1,0:T(8,128)} %bitcast.12), custom_call_target="tpu_custom_call" | custom-call | flops 1 | bytes 1024 | tf_op jit(solution)/shard_map/take_part/pallas_call | solution.py:161
  3.0 1.5 %collective-permute-start = (f32[400,1024]{1,0:T(8,128)S(1)}, f32[400,1024]{1,0:T(8,128)S(1)}, u32[]{:S(2)}, u32[]{:S(2)}) collective-permute-start(f32[400,1024]{1,0:T(8,128)S(1)} %take_part.2), channel_id=1, source_target_pairs={{0,8},{8,0},{1,9},{9,1},{2,10},{10,2},{3,11},{11,3},{4,12},{12,4},... | collective-permute-start | bytes 4915208 | tf_op jit(solution)/shard_map/ppermute | solution.py:499
  4.5 0.8 take_part.3
  5.3 2.3 %collective-permute-done.other = f32[400,1024]{1,0:T(8,128)S(1)} collective-permute-done((f32[400,1024]{1,0:T(8,128)S(1)}, f32[400,1024]{1,0:T(8,128)S(1)}, u32[]{:S(2)}, u32[]{:S(2)}) %collective-permute-start) | collective-permute-done | bytes 1638432 | tf_op jit(solution)/shard_map/ppermute | solution.py:499
  7.6 1.0 pack.1
  8.7 0.5 collective-permute-start.3
  9.1 1.7 %collective-permute-start.1 = (f32[2,400,128]{2,1,0:T(8,128)S(1)}, f32[2,400,128]{2,1,0:T(8,128)S(1)}, u32[]{:S(2)}, u32[]{:S(2)}) collective-permute-start(f32[2,400,128]{2,1,0:T(8,128)S(1)} %get-tuple-element.64), channel_id=1, source_target_pairs={{0,16},{16,32},{32,48},{48,0},{1,17},{17,33},{33,49},{49,1},{2,18}... | collective-permute-start | bytes 1228808 | tf_op jit(solution)/shard_map/ppermute | solution.py:302
  10.8 2.1 %collective-permute-start.2 = (f32[2,400,128]{2,1,0:T(8,128)S(1)}, f32[2,400,128]{2,1,0:T(8,128)S(1)}, u32[]{:S(2)}, u32[]{:S(2)}) collective-permute-start(f32[2,400,128]{2,1,0:T(8,128)S(1)} %get-tuple-element.65), channel_id=1, source_target_pairs={{0,48},{16,0},{32,16},{48,32},{1,49},{17,1},{33,17},{49,33},{2,50}... | collective-permute-start | bytes 1228808 | tf_op jit(solution)/shard_map/ppermute | solution.py:302
  13.0 0.4 collective-permute-done.3.other
  13.4 1.1 pack_rest.1
  14.5 3.1 %collective-permute-start.4 = (f32[96,1024]{1,0:T(8,128)S(1)}, f32[96,1024]{1,0:T(8,128)S(1)}, u32[]{:S(2)}, u32[]{:S(2)}) collective-permute-start(f32[96,1024]{1,0:T(8,128)S(1)} %get-tuple-element.69), channel_id=1, source_target_pairs={{0,64},{64,0},{1,65},{65,1},{2,66},{66,2},{3,67},{67,3},{4,68},{68... | collective-permute-start | bytes 1179656 | tf_op jit(solution)/shard_map/ppermute | solution.py:505
  17.5 1.6 %collective-permute-start.8 = (f32[2,400,128]{2,1,0:T(8,128)S(1)}, f32[2,400,128]{2,1,0:T(8,128)S(1)}, u32[]{:S(2)}, u32[]{:S(2)}) collective-permute-start(f32[2,400,128]{2,1,0:T(8,128)S(1)} %get-tuple-element.77), channel_id=1, source_target_pairs={{0,16},{16,32},{32,48},{48,0},{1,17},{17,33},{33,49},{49,1},{2,18}... | collective-permute-start | bytes 1228808 | tf_op jit(solution)/shard_map/ppermute | solution.py:302
  19.2 2.1 %collective-permute-start.9 = (f32[2,400,128]{2,1,0:T(8,128)S(1)}, f32[2,400,128]{2,1,0:T(8,128)S(1)}, u32[]{:S(2)}, u32[]{:S(2)}) collective-permute-start(f32[2,400,128]{2,1,0:T(8,128)S(1)} %get-tuple-element.78), channel_id=1, source_target_pairs={{0,48},{16,0},{32,16},{48,32},{1,49},{17,1},{33,17},{49,33},{2,50}... | collective-permute-start | bytes 1228808 | tf_op jit(solution)/shard_map/ppermute | solution.py:302
  21.3 1.4 collective-permute-done.1.up
  22.7 3.7 %collective-permute-done.4.arrived = f32[96,1024]{1,0:T(8,128)S(1)} collective-permute-done((f32[96,1024]{1,0:T(8,128)S(1)}, f32[96,1024]{1,0:T(8,128)S(1)}, u32[]{:S(2)}, u32[]{:S(2)}) %collective-permute-start.4) | collective-permute-done | bytes 393248 | tf_op jit(solution)/shard_map/ppermute | solution.py:505
  26.4 0.7 relay_pack.1
  27.1 1.7 %collective-permute-start.5 = (f32[592,128]{1,0:T(8,128)S(1)}, f32[592,128]{1,0:T(8,128)S(1)}, u32[]{:S(2)}, u32[]{:S(2)}) collective-permute-start(f32[592,128]{1,0:T(8,128)S(1)} %get-tuple-element.71), channel_id=1, source_target_pairs={{0,16},{16,32},{32,48},{48,0},{1,17},{17,33},{33,49},{49,1},{2,18}... | collective-permute-start | bytes 909320 | tf_op jit(solution)/shard_map/ppermute | solution.py:302
  28.9 2.2 %collective-permute-start.6 = (f32[592,128]{1,0:T(8,128)S(1)}, f32[592,128]{1,0:T(8,128)S(1)}, u32[]{:S(2)}, u32[]{:S(2)}) collective-permute-start(f32[592,128]{1,0:T(8,128)S(1)} %get-tuple-element.72), channel_id=1, source_target_pairs={{0,48},{16,0},{32,16},{48,32},{1,49},{17,1},{33,17},{49,33},{2,50}... | collective-permute-start | bytes 909320 | tf_op jit(solution)/shard_map/ppermute | solution.py:302
  31.4 0.5 collective-permute-start.10
  31.9 2.2 %collective-permute-start.11 = (f32[400,128]{1,0:T(8,128)S(1)}, f32[400,128]{1,0:T(8,128)S(1)}, u32[]{:S(2)}, u32[]{:S(2)}) collective-permute-start(f32[400,128]{1,0:T(8,128)S(1)} %get-tuple-element.81), channel_id=1, source_target_pairs={{0,48},{16,0},{32,16},{48,32},{1,49},{17,1},{33,17},{49,33},{2,50}... | collective-permute-start | bytes 614408 | tf_op jit(solution)/shard_map/ppermute | solution.py:302
  34.9 1.0 collective-permute-start.7
  36.0 2.4 %old_state.1 = (f32[16,8,992]{2,1,0:T(8,128)S(1)}, f32[16,8,992]{2,1,0:T(8,128)S(1)}) custom-call(s32[62,2048]{1,0:T(8,128)S(1)} %copy-done.1, s32[62,2048]{1,0:T(8,128)S(1)} %copy-done.2, f32[62]{0:T(128)S(1)} %copy-done.5, f32[62]{0:T(128)S(1)} %copy-done.6, f32[2,128]{1,0:T(2,128)S(1)} %bitcast.16, f32[2,128]{1,0:T(2,128)S(1)} %bitcast.17), custom_call_target="tpu_custom_call" | custom-call | flops 1 | bytes 1024 | tf_op jit(solution)/shard_map/old_state/pallas_call | solution.py:100
  38.5 5.9 %collective-permute-done.7.across = f32[2,96,128]{2,1,0:T(8,128)S(1)} collective-permute-done((f32[2,96,128]{2,1,0:T(8,128)S(1)}, f32[2,96,128]{2,1,0:T(8,128)S(1)}, u32[]{:S(2)}, u32[]{:S(2)}) %collective-permute-start.7) | collective-permute-done | bytes 98336 | tf_op jit(solution)/shard_map/ppermute | solution.py:508
  44.7 25.2 %all_to_all.10.grads = f32[32,8,896]{2,1,0:T(8,128)S(1)} all-to-all(f32[32,8,896]{2,1,0:T(8,128)S(1)} %turn.1), channel_id=1, replica_groups=mesh['yh'=2,'z'=4,'core'=2,'yl'=2,'x'=4] {'yh','core','yl','x'}, dimensions={0} | all-to-all | bytes 1835008 | tf_op jit(solution)/shard_map/all_to_all | solution.py:329
  69.9 0.9 adam.1
  70.9 20.8 %all_to_all.11.rows = f32[32,8,992]{2,1,0:T(8,128)S(1)} all-to-all(f32[32,8,992]{2,1,0:T(8,128)S(1)} %get-tuple-element.93), channel_id=1, replica_groups=mesh['yh'=2,'z'=4,'core'=2,'yl'=2,'x'=4] {'yh','core','yl','x'}, dimensions={0} | all-to-all | bytes 2031616 | tf_op jit(solution)/shard_map/all_to_all | solution.py:329
  91.6 0.4 unturn.1
  92.2 1.6 %collective-permute-start.15 = (f32[2,496,128]{2,1,0:T(8,128)S(1)}, f32[2,496,128]{2,1,0:T(8,128)S(1)}, u32[]{:S(2)}, u32[]{:S(2)}) collective-permute-start(f32[2,496,128]{2,1,0:T(8,128)S(1)} %get-tuple-element.97), channel_id=1, source_target_pairs={{0,48},{16,0},{32,16},{48,32},{1,49},{17,1},{33,17},{49,33},{2,50}... | collective-permute-start | bytes 1523720 | tf_op jit(solution)/shard_map/ppermute | solution.py:302
  93.7 2.7 %collective-permute-start.13 = (f32[2,496,128]{2,1,0:T(8,128)S(1)}, f32[2,496,128]{2,1,0:T(8,128)S(1)}, u32[]{:S(2)}, u32[]{:S(2)}) collective-permute-start(f32[2,496,128]{2,1,0:T(8,128)S(1)} %get-tuple-element.96), channel_id=1, source_target_pairs={{0,48},{16,0},{32,16},{48,32},{1,49},{17,1},{33,17},{49,33},{2,50}... | collective-permute-start | bytes 1523720 | tf_op jit(solution)/shard_map/ppermute | solution.py:302
  96.4 1.4 %new_state.1 = (bf16[62,2048]{1,0:T(8,128)(2,1)}, bf16[62,2048]{1,0:T(8,128)(2,1)}, f32[1,62]{1,0:T(1,128)}, f32[1,62]{1,0:T(1,128)}) custom-call(f32[16,8,992]{2,1,0:T(8,128)S(1)} %get-tuple-element.98.m_in, f32[16,8,992]{2,1,0:T(8,128)S(1)} %get-tuple-element.99.v_in), custom_call_target="tpu_custom_call" | custom-call | flops 1 | bytes 1024 | tf_op jit(solution)/shard_map/new_state/pallas_call | solution.py:129
  97.8 3.3 %hold.1.weight = f32[1984,1024]{1,0:T(8,128)S(1)} custom-call(f32[1984,1024]{1,0:T(8,128)} %bitcast.19), custom_call_target="tpu_custom_call" | custom-call | flops 1 | bytes 1024 | tf_op jit(solution)/shard_map/hold/pallas_call | solution.py:454
  101.2 2.0 %write_weight.3.refs_0_ = f32[1984,1024]{1,0:T(8,128)} custom-call(s32[3]{0:T(128)S(1)} %pad_add_fusion.place, f32[1984,1024]{1,0:T(8,128)S(1)} %hold.1.weight, f32[2,992,128]{2,1,0:T(8,128)S(1)} %get-tuple-element.94.mine, f32[2,992,128]{2,1,0:T(8,128)S(1)} %collective-permute-done.16.theirs), custom_call_target="tpu_custom_call" | custom-call | flops 1 | bytes 1024 | tf_op jit(solution)/shard_map/write_weight/pallas_call | solution.py:475
  103.1 1.7 %collective-permute-done.15.down.refs_1_ = f32[2,496,128]{2,1,0:T(8,128)S(1)} collective-permute-done((f32[2,496,128]{2,1,0:T(8,128)S(1)}, f32[2,496,128]{2,1,0:T(8,128)S(1)}, u32[]{:S(2)}, u32[]{:S(2)}) %collective-permute-start.15) | collective-permute-done | bytes 507936 | tf_op jit(solution)/shard_map/ppermute | solution.py:302
  104.9 2.4 %collective-permute-done.14.up.refs_0_ = f32[2,496,128]{2,1,0:T(8,128)S(1)} collective-permute-done((f32[2,496,128]{2,1,0:T(8,128)S(1)}, f32[2,496,128]{2,1,0:T(8,128)S(1)}, u32[]{:S(2)}, u32[]{:S(2)}) %collective-permute-start.14) | collective-permute-done | bytes 507936 | tf_op jit(solution)/shard_map/ppermute | solution.py:302
  107.4 0.6 collective-permute-start.20
  107.9 1.1 collective-permute-start.19
  109.1 6.7 %collective-permute-done.13.down.refs_3_ = f32[2,496,128]{2,1,0:T(8,128)S(1)} collective-permute-done((f32[2,496,128]{2,1,0:T(8,128)S(1)}, f32[2,496,128]{2,1,0:T(8,128)S(1)}, u32[]{:S(2)}, u32[]{:S(2)}) %collective-permute-start.13) | collective-permute-done | bytes 507936 | tf_op jit(solution)/shard_map/ppermute | solution.py:302
  115.8 2.4 %collective-permute-done.12.up.refs_2_ = f32[2,496,128]{2,1,0:T(8,128)S(1)} collective-permute-done((f32[2,496,128]{2,1,0:T(8,128)S(1)}, f32[2,496,128]{2,1,0:T(8,128)S(1)}, u32[]{:S(2)}, u32[]{:S(2)}) %collective-permute-start.12) | collective-permute-done | bytes 507936 | tf_op jit(solution)/shard_map/ppermute | solution.py:302
  118.3 3.0 %collective-permute-done.20.refs_5_ = f32[496,128]{1,0:T(8,128)S(1)} collective-permute-done((f32[496,128]{1,0:T(8,128)S(1)}, f32[496,128]{1,0:T(8,128)S(1)}, u32[]{:S(2)}, u32[]{:S(2)}) %collective-permute-start.20) | collective-permute-done | bytes 253984 | tf_op jit(solution)/shard_map/ppermute | solution.py:302
  121.2 2.4 %collective-permute-done.19.refs_4_ = f32[496,128]{1,0:T(8,128)S(1)} collective-permute-done((f32[496,128]{1,0:T(8,128)S(1)}, f32[496,128]{1,0:T(8,128)S(1)}, u32[]{:S(2)}, u32[]{:S(2)}) %collective-permute-start.19) | collective-permute-done | bytes 253984 | tf_op jit(solution)/shard_map/ppermute | solution.py:302
  123.8 1.7 %collective-permute-start.21 = (f32[10,496,128]{2,1,0:T(8,128)S(1)}, f32[10,496,128]{2,1,0:T(8,128)S(1)}, u32[]{:S(2)}, u32[]{:S(2)}) collective-permute-start(f32[10,496,128]{2,1,0:T(8,128)S(1)} %gathered.2.mine), channel_id=1, source_target_pairs={{0,8},{8,0},{1,9},{9,1},{2,10},{10,2},{3,11},{11,3},{4,12},{12,4},... | collective-permute-start | bytes 7618568 | tf_op jit(solution)/shard_map/ppermute | solution.py:485
  125.5 1.5 %collective-permute-start.17 = (f32[496,128]{1,0:T(8,128)S(1)}, f32[496,128]{1,0:T(8,128)S(1)}, u32[]{:S(2)}, u32[]{:S(2)}) collective-permute-start(f32[496,128]{1,0:T(8,128)S(1)} %get-tuple-element.109), channel_id=1, source_target_pairs={{0,16},{16,32},{32,48},{48,0},{1,17},{17,33},{33,49},{49,1},{2,18}... | collective-permute-start | bytes 761864 | tf_op jit(solution)/shard_map/ppermute | solution.py:302
  127.0 2.9 %collective-permute-done.21.theirs = f32[10,496,128]{2,1,0:T(8,128)S(1)} collective-permute-done((f32[10,496,128]{2,1,0:T(8,128)S(1)}, f32[10,496,128]{2,1,0:T(8,128)S(1)}, u32[]{:S(2)}, u32[]{:S(2)}) %collective-permute-start.21) | collective-permute-done | bytes 2539552 | tf_op jit(solution)/shard_map/ppermute | solution.py:485
  129.9 3.0 %write_weight.4.refs_0_ = f32[1984,1024]{1,0:T(8,128)} custom-call(s32[3]{0:T(128)S(1)} %pad_add_fusion.place, f32[1984,1024]{1,0:T(8,128)S(1)} %hold.1.weight, f32[10,496,128]{2,1,0:T(8,128)S(1)} %gathered.2.mine, f32[10,496,128]{2,1,0:T(8,128)S(1)} %collective-permute-done.21.theirs, f32[1984,1024]{1,0:T(8,128)} %write_weight.3.refs_0_), custom_call_target="tpu_custom_call", output_to_operand_aliasing={{}: (4, {})} | custom-call | flops 1 | bytes 1024 | tf_op jit(solution)/shard_map/write_weight/pallas_call | solution.py:475
  133.2 0.9 collective-permute-done.17.refs_0_
  134.1 1.3 collective-permute-start.22
  135.4 1.5 %collective-permute-done.22.theirs = f32[2,496,128]{2,1,0:T(8,128)S(1)} collective-permute-done((f32[2,496,128]{2,1,0:T(8,128)S(1)}, f32[2,496,128]{2,1,0:T(8,128)S(1)}, u32[]{:S(2)}, u32[]{:S(2)}) %collective-permute-start.22) | collective-permute-done | bytes 507936 | tf_op jit(solution)/shard_map/ppermute | solution.py:485
  136.9 1.6 %write_weight.5 = f32[1984,1024]{1,0:T(8,128)} custom-call(s32[3]{0:T(128)S(1)} %pad_add_fusion.place, f32[1984,1024]{1,0:T(8,128)S(1)} %hold.1.weight, f32[2,496,128]{2,1,0:T(8,128)S(1)} %gathered.3.mine, f32[2,496,128]{2,1,0:T(8,128)S(1)} %collective-permute-done.22.theirs, f32[1984,1024]{1,0:T(8,128)} %write_weight.4.refs_0_), custom_call_target="tpu_custom_call", output_to_operand_aliasing={{}: (4, {})} | custom-call | flops 1 | bytes 1024 | tf_op jit(solution)/shard_map/write_weight/pallas_call | solution.py:475
  (35 shorter events, 1.5 us)
Async XLA Ops:
  0.6 3.8 %copy-start = (f32[1,1024,1984]{1,2,0:T(8,128)S(1)}, f32[1,1024,1984]{1,2,0:T(8,128)}, u32[]{:S(2)}) copy-start(f32[1,1024,1984]{1,2,0:T(8,128)} %param.10) | copy-start | bytes 24379396
  3.0 4.6 %collective-permute-start = (f32[400,1024]{1,0:T(8,128)S(1)}, f32[400,1024]{1,0:T(8,128)S(1)}, u32[]{:S(2)}, u32[]{:S(2)}) collective-permute-start(f32[400,1024]{1,0:T(8,128)S(1)} %take_part.2), channel_id=1, source_target_pairs={{0,8},{8,0},{1,9},{9,1},{2,10},{10,2},{3,11},{11,3},{4,12},{12,4},... | collective-permute-start | bytes 4915208 | tf_op jit(solution)/shard_map/ppermute | solution.py:499
  8.6 27.4 %copy-start.1 = (s32[62,2048]{1,0:T(8,128)S(1)}, s32[62,2048]{1,0:T(8,128)}, u32[]{:S(2)}) copy-start(s32[62,2048]{1,0:T(8,128)} %m_codes) | copy-start | bytes 1523716
  8.6 27.4 %copy-start.2 = (s32[62,2048]{1,0:T(8,128)S(1)}, s32[62,2048]{1,0:T(8,128)}, u32[]{:S(2)}) copy-start(s32[62,2048]{1,0:T(8,128)} %v_codes.1) | copy-start | bytes 1523716
  8.6 27.4 %copy-start.3 = (f32[256]{0:T(256)S(1)}, f32[256]{0:T(256)}, u32[]{:S(2)}) copy-start(f32[256]{0:T(256)} %param.15) | copy-start | bytes 3076
  8.6 27.4 %copy-start.4 = (f32[256]{0:T(256)S(1)}, f32[256]{0:T(256)}, u32[]{:S(2)}) copy-start(f32[256]{0:T(256)} %param.16) | copy-start | bytes 3076
  8.6 27.4 %copy-start.5 = (f32[62]{0:T(128)S(1)}, f32[62]{0:T(128)}, u32[]{:S(2)}) copy-start(f32[62]{0:T(128)} %m_scale.1) | copy-start | bytes 748
  8.7 27.4 %copy-start.6 = (f32[62]{0:T(128)S(1)}, f32[62]{0:T(128)}, u32[]{:S(2)}) copy-start(f32[62]{0:T(128)} %v_scale.1) | copy-start | bytes 748
  8.7 4.7 %collective-permute-start.3 = (f32[592,1024]{1,0:T(8,128)S(1)}, f32[592,1024]{1,0:T(8,128)S(1)}, u32[]{:S(2)}, u32[]{:S(2)}) collective-permute-start(f32[592,1024]{1,0:T(8,128)S(1)} %take_part.3), channel_id=1, source_target_pairs={{0,8},{8,0},{1,9},{9,1},{2,10},{10,2},{3,11},{11,3},{4,12},{12,4},... | collective-permute-start | bytes 7274504 | tf_op jit(solution)/shard_map/ppermute | solution.py:503
  9.1 13.5 %collective-permute-start.1 = (f32[2,400,128]{2,1,0:T(8,128)S(1)}, f32[2,400,128]{2,1,0:T(8,128)S(1)}, u32[]{:S(2)}, u32[]{:S(2)}) collective-permute-start(f32[2,400,128]{2,1,0:T(8,128)S(1)} %get-tuple-element.64), channel_id=1, source_target_pairs={{0,16},{16,32},{32,48},{48,0},{1,17},{17,33},{33,49},{49,1},{2,18}... | collective-permute-start | bytes 1228808 | tf_op jit(solution)/shard_map/ppermute | solution.py:302
  10.8 11.8 %collective-permute-start.2 = (f32[2,400,128]{2,1,0:T(8,128)S(1)}, f32[2,400,128]{2,1,0:T(8,128)S(1)}, u32[]{:S(2)}, u32[]{:S(2)}) collective-permute-start(f32[2,400,128]{2,1,0:T(8,128)S(1)} %get-tuple-element.65), channel_id=1, source_target_pairs={{0,48},{16,0},{32,16},{48,32},{1,49},{17,1},{33,17},{49,33},{2,50}... | collective-permute-start | bytes 1228808 | tf_op jit(solution)/shard_map/ppermute | solution.py:302
  14.5 12.0 %collective-permute-start.4 = (f32[96,1024]{1,0:T(8,128)S(1)}, f32[96,1024]{1,0:T(8,128)S(1)}, u32[]{:S(2)}, u32[]{:S(2)}) collective-permute-start(f32[96,1024]{1,0:T(8,128)S(1)} %get-tuple-element.69), channel_id=1, source_target_pairs={{0,64},{64,0},{1,65},{65,1},{2,66},{66,2},{3,67},{67,3},{4,68},{68... | collective-permute-start | bytes 1179656 | tf_op jit(solution)/shard_map/ppermute | solution.py:505
  17.5 13.8 %collective-permute-start.8 = (f32[2,400,128]{2,1,0:T(8,128)S(1)}, f32[2,400,128]{2,1,0:T(8,128)S(1)}, u32[]{:S(2)}, u32[]{:S(2)}) collective-permute-start(f32[2,400,128]{2,1,0:T(8,128)S(1)} %get-tuple-element.77), channel_id=1, source_target_pairs={{0,16},{16,32},{32,48},{48,0},{1,17},{17,33},{33,49},{49,1},{2,18}... | collective-permute-start | bytes 1228808 | tf_op jit(solution)/shard_map/ppermute | solution.py:302
  19.2 12.2 %collective-permute-start.9 = (f32[2,400,128]{2,1,0:T(8,128)S(1)}, f32[2,400,128]{2,1,0:T(8,128)S(1)}, u32[]{:S(2)}, u32[]{:S(2)}) collective-permute-start(f32[2,400,128]{2,1,0:T(8,128)S(1)} %get-tuple-element.78), channel_id=1, source_target_pairs={{0,48},{16,0},{32,16},{48,32},{1,49},{17,1},{33,17},{49,33},{2,50}... | collective-permute-start | bytes 1228808 | tf_op jit(solution)/shard_map/ppermute | solution.py:302
  27.1 17.2 %collective-permute-start.5 = (f32[592,128]{1,0:T(8,128)S(1)}, f32[592,128]{1,0:T(8,128)S(1)}, u32[]{:S(2)}, u32[]{:S(2)}) collective-permute-start(f32[592,128]{1,0:T(8,128)S(1)} %get-tuple-element.71), channel_id=1, source_target_pairs={{0,16},{16,32},{32,48},{48,0},{1,17},{17,33},{33,49},{49,1},{2,18}... | collective-permute-start | bytes 909320 | tf_op jit(solution)/shard_map/ppermute | solution.py:302
  28.9 15.5 %collective-permute-start.6 = (f32[592,128]{1,0:T(8,128)S(1)}, f32[592,128]{1,0:T(8,128)S(1)}, u32[]{:S(2)}, u32[]{:S(2)}) collective-permute-start(f32[592,128]{1,0:T(8,128)S(1)} %get-tuple-element.72), channel_id=1, source_target_pairs={{0,48},{16,0},{32,16},{48,32},{1,49},{17,1},{33,17},{49,33},{2,50}... | collective-permute-start | bytes 909320 | tf_op jit(solution)/shard_map/ppermute | solution.py:302
  31.4 13.0 %collective-permute-start.10 = (f32[400,128]{1,0:T(8,128)S(1)}, f32[400,128]{1,0:T(8,128)S(1)}, u32[]{:S(2)}, u32[]{:S(2)}) collective-permute-start(f32[400,128]{1,0:T(8,128)S(1)} %get-tuple-element.80), channel_id=1, source_target_pairs={{0,16},{16,32},{32,48},{48,0},{1,17},{17,33},{33,49},{49,1},{2,18}... | collective-permute-start | bytes 614408 | tf_op jit(solution)/shard_map/ppermute | solution.py:302
  31.9 12.5 %collective-permute-start.11 = (f32[400,128]{1,0:T(8,128)S(1)}, f32[400,128]{1,0:T(8,128)S(1)}, u32[]{:S(2)}, u32[]{:S(2)}) collective-permute-start(f32[400,128]{1,0:T(8,128)S(1)} %get-tuple-element.81), channel_id=1, source_target_pairs={{0,48},{16,0},{32,16},{48,32},{1,49},{17,1},{33,17},{49,33},{2,50}... | collective-permute-start | bytes 614408 | tf_op jit(solution)/shard_map/ppermute | solution.py:302
  34.9 9.5 %collective-permute-start.7 = (f32[2,96,128]{2,1,0:T(8,128)S(1)}, f32[2,96,128]{2,1,0:T(8,128)S(1)}, u32[]{:S(2)}, u32[]{:S(2)}) collective-permute-start(f32[2,96,128]{2,1,0:T(8,128)S(1)} %get-tuple-element.74), channel_id=1, source_target_pairs={{0,32},{16,48},{32,0},{48,16},{1,33},{17,49},{33,1},{49,17},{2,34}... | collective-permute-start | bytes 294920 | tf_op jit(solution)/shard_map/ppermute | solution.py:508
  92.0 9.2 %collective-permute-start.16 = (f32[2,992,128]{2,1,0:T(8,128)S(1)}, f32[2,992,128]{2,1,0:T(8,128)S(1)}, u32[]{:S(2)}, u32[]{:S(2)}) collective-permute-start(f32[2,992,128]{2,1,0:T(8,128)S(1)} %get-tuple-element.94.mine), channel_id=1, source_target_pairs={{0,8},{8,0},{1,9},{9,1},{2,10},{10,2},{3,11},{11,3},{4,12},{12,4},... | collective-permute-start | bytes 3047432 | tf_op jit(solution)/shard_map/ppermute | solution.py:485
  92.2 12.7 %collective-permute-start.15 = (f32[2,496,128]{2,1,0:T(8,128)S(1)}, f32[2,496,128]{2,1,0:T(8,128)S(1)}, u32[]{:S(2)}, u32[]{:S(2)}) collective-permute-start(f32[2,496,128]{2,1,0:T(8,128)S(1)} %get-tuple-element.97), channel_id=1, source_target_pairs={{0,48},{16,0},{32,16},{48,32},{1,49},{17,1},{33,17},{49,33},{2,50}... | collective-permute-start | bytes 1523720 | tf_op jit(solution)/shard_map/ppermute | solution.py:302
  93.7 13.6 %collective-permute-start.14 = (f32[2,496,128]{2,1,0:T(8,128)S(1)}, f32[2,496,128]{2,1,0:T(8,128)S(1)}, u32[]{:S(2)}, u32[]{:S(2)}) collective-permute-start(f32[2,496,128]{2,1,0:T(8,128)S(1)} %get-tuple-element.97), channel_id=1, source_target_pairs={{0,16},{16,32},{32,48},{48,0},{1,17},{17,33},{33,49},{49,1},{2,18}... | collective-permute-start | bytes 1523720 | tf_op jit(solution)/shard_map/ppermute | solution.py:302
  93.7 22.0 %collective-permute-start.13 = (f32[2,496,128]{2,1,0:T(8,128)S(1)}, f32[2,496,128]{2,1,0:T(8,128)S(1)}, u32[]{:S(2)}, u32[]{:S(2)}) collective-permute-start(f32[2,496,128]{2,1,0:T(8,128)S(1)} %get-tuple-element.96), channel_id=1, source_target_pairs={{0,48},{16,0},{32,16},{48,32},{1,49},{17,1},{33,17},{49,33},{2,50}... | collective-permute-start | bytes 1523720 | tf_op jit(solution)/shard_map/ppermute | solution.py:302
  96.4 21.8 %collective-permute-start.12 = (f32[2,496,128]{2,1,0:T(8,128)S(1)}, f32[2,496,128]{2,1,0:T(8,128)S(1)}, u32[]{:S(2)}, u32[]{:S(2)}) collective-permute-start(f32[2,496,128]{2,1,0:T(8,128)S(1)} %get-tuple-element.96), channel_id=1, source_target_pairs={{0,16},{16,32},{32,48},{48,0},{1,17},{17,33},{33,49},{49,1},{2,18}... | collective-permute-start | bytes 1523720 | tf_op jit(solution)/shard_map/ppermute | solution.py:302
  107.4 13.8 %collective-permute-start.20 = (f32[496,128]{1,0:T(8,128)S(1)}, f32[496,128]{1,0:T(8,128)S(1)}, u32[]{:S(2)}, u32[]{:S(2)}) collective-permute-start(f32[496,128]{1,0:T(8,128)S(1)} %get-tuple-element.112), channel_id=1, source_target_pairs={{0,48},{16,0},{32,16},{48,32},{1,49},{17,1},{33,17},{49,33},{2,50}... | collective-permute-start | bytes 761864 | tf_op jit(solution)/shard_map/ppermute | solution.py:302
  107.9 15.7 %collective-permute-start.19 = (f32[496,128]{1,0:T(8,128)S(1)}, f32[496,128]{1,0:T(8,128)S(1)}, u32[]{:S(2)}, u32[]{:S(2)}) collective-permute-start(f32[496,128]{1,0:T(8,128)S(1)} %get-tuple-element.106), channel_id=1, source_target_pairs={{0,16},{16,32},{32,48},{48,0},{1,17},{17,33},{33,49},{49,1},{2,18}... | collective-permute-start | bytes 761864 | tf_op jit(solution)/shard_map/ppermute | solution.py:302
  123.8 6.1 %collective-permute-start.21 = (f32[10,496,128]{2,1,0:T(8,128)S(1)}, f32[10,496,128]{2,1,0:T(8,128)S(1)}, u32[]{:S(2)}, u32[]{:S(2)}) collective-permute-start(f32[10,496,128]{2,1,0:T(8,128)S(1)} %gathered.2.mine), channel_id=1, source_target_pairs={{0,8},{8,0},{1,9},{9,1},{2,10},{10,2},{3,11},{11,3},{4,12},{12,4},... | collective-permute-start | bytes 7618568 | tf_op jit(solution)/shard_map/ppermute | solution.py:485
  125.5 7.7 %collective-permute-start.18 = (f32[496,128]{1,0:T(8,128)S(1)}, f32[496,128]{1,0:T(8,128)S(1)}, u32[]{:S(2)}, u32[]{:S(2)}) collective-permute-start(f32[496,128]{1,0:T(8,128)S(1)} %get-tuple-element.110), channel_id=1, source_target_pairs={{0,48},{16,0},{32,16},{48,32},{1,49},{17,1},{33,17},{49,33},{2,50}... | collective-permute-start | bytes 761864 | tf_op jit(solution)/shard_map/ppermute | solution.py:302
  125.5 8.6 %collective-permute-start.17 = (f32[496,128]{1,0:T(8,128)S(1)}, f32[496,128]{1,0:T(8,128)S(1)}, u32[]{:S(2)}, u32[]{:S(2)}) collective-permute-start(f32[496,128]{1,0:T(8,128)S(1)} %get-tuple-element.109), channel_id=1, source_target_pairs={{0,16},{16,32},{32,48},{48,0},{1,17},{17,33},{33,49},{49,1},{2,18}... | collective-permute-start | bytes 761864 | tf_op jit(solution)/shard_map/ppermute | solution.py:302
  134.1 2.8 %collective-permute-start.22 = (f32[2,496,128]{2,1,0:T(8,128)S(1)}, f32[2,496,128]{2,1,0:T(8,128)S(1)}, u32[]{:S(2)}, u32[]{:S(2)}) collective-permute-start(f32[2,496,128]{2,1,0:T(8,128)S(1)} %gathered.3.mine), channel_id=1, source_target_pairs={{0,8},{8,0},{1,9},{9,1},{2,10},{10,2},{3,11},{11,3},{4,12},{12,4},... | collective-permute-start | bytes 1523720 | tf_op jit(solution)/shard_map/ppermute | solution.py:485

commit v5 on v4

--- a/solution.py
+++ b/solution.py
@@ -33,6 +33,7 @@
 SWAP = [(0, 1), (1, 0)]
 UP = [(i, (i + 1) % N_Z) for i in range(N_Z)]
 DOWN = [(i, (i - 1) % N_Z) for i in range(N_Z)]
+ROUND = [(i * N_CORE + c, (i + (1, -1)[c]) % N_Z * N_CORE + c) for i in range(N_Z) for c in range(N_CORE)]
 ACROSS = [(i, (i + 2) % N_Z) for i in range(N_Z)]
 
 ANY = pl.BlockSpec(memory_space=pl.ANY)
@@ -381,61 +382,23 @@
     )(back)
 
 
-def relayed_kernel(up, down, up_out, down_out):
-    up_out[...] = up[0]
-    down_out[...] = down[1]
-
-
-def relayed(up, down):
-    return pl.pallas_call(
-        relayed_kernel,
-        in_specs=[VMEM] * 2,
-        out_specs=[VMEM] * 2,
-        out_shape=[shape(*up.shape[1:])] * 2,
-        compiler_params=params(),
-        cost_estimate=COST,
-        name="relayed",
-    )(up, down)
-
-
-def gathered_kernel(*refs):
-    pieces, out = refs[:-1], refs[-1]
-    at = 0
-    for piece in pieces:
-        tiles = [piece[...]] if len(piece.shape) == 2 else [piece[k] for k in range(piece.shape[0])]
-        for tile in tiles:
-            out[at] = tile
-            at += 1
-
-
-def gathered(*pieces):
-    count = sum(p.shape[0] if p.ndim == 3 else 1 for p in pieces)
-    return pl.pallas_call(
-        gathered_kernel,
-        in_specs=[VMEM] * len(pieces),
-        out_specs=VMEM,
-        out_shape=shape(count, *pieces[0].shape[-2:]),
-        compiler_params=params(),
-        cost_estimate=COST,
-        name="gathered",
-    )(*pieces)
-
-
-def weight_kernel(spots, place, weight, mine, theirs, *refs):
-    out, held, sem = refs[-3:]
+def weight_kernel(spots, place, weight, *refs):
+    pieces, (out, held, sem) = refs[: 2 * len(spots)], refs[-3:]
     c, z = place[0], place[1]
     half = weight.shape[0] // N_CORE
-    width = mine.shape[1]
     stores = []
-    for piece, core in ((mine, c), (theirs, 1 - c)):
-        for slot, (start, yh, to) in enumerate(spots):
-            rows = pl.ds(pl.multiple_of(core * half + start, 8), width)
-            lanes = lane_tile(yh, z + to)
+    for k, piece in enumerate(pieces):
+        core = c if k < len(spots) else 1 - c
+        start, steps = spots[k % len(spots)]
+        width = piece.shape[1]
+        rows = pl.ds(pl.multiple_of(core * half + start, 8), width)
+        for yh in range(N_YH):
+            lanes = lane_tile(yh, z + steps + (1 - core) * (N_Z - 2 * steps))
             old = weight.at[rows, lanes]
             where = held.at[len(stores)]
 
             def body(r):
-                where[r, :] = old[r, :] - learn_rate * (piece[slot, r, :] + decay_rate * old[r, :])
+                where[r, :] = old[r, :] - learn_rate * (piece[yh, r, :] + decay_rate * old[r, :])
 
             each(width, body)
             stores.append(pltpu.make_async_copy(where, out.at[rows, lanes], sem.at[len(stores)]))
@@ -463,26 +426,22 @@
     )(in_hbm(array))
 
 
-NEAR = ((0, 0, 0), (0, 1, 0))
-SIDES = tuple((at, yh, to) for at in (0, BACK) for to in (3, 1) for yh in range(N_YH)) + ((0, 0, 2), (0, 1, 2))
-FAR = ((BACK, 0, 2), (BACK, 1, 2))
-
-
-def write_weight(place, held, piece, spots, so_far):
+def write_weight(place, held, pieces, spots, so_far):
     done = [] if so_far is None else [so_far]
-    stores = N_CORE * len(spots)
+    pieces = list(pieces) + [lax.ppermute(p, "core", SWAP) for p in pieces]
+    stores = N_YH * len(pieces)
     hbm = pl.BlockSpec(memory_space=pltpu.HBM)
     return pl.pallas_call(
         functools.partial(weight_kernel, spots),
-        in_specs=[SMEM] + [VMEM] * 3 + [hbm] * len(done),
+        in_specs=[SMEM] + [VMEM] * (1 + len(pieces)) + [hbm] * len(done),
         out_specs=hbm,
         out_shape=shape(*held.shape),
-        input_output_aliases={4: 0} if done else {},
-        scratch_shapes=[pltpu.VMEM((stores, *piece.shape[1:]), f32), pltpu.SemaphoreType.DMA((stores,))],
+        input_output_aliases={2 + len(pieces): 0} if done else {},
+        scratch_shapes=[pltpu.VMEM((stores, *pieces[0].shape[1:]), f32), pltpu.SemaphoreType.DMA((stores,))],
         compiler_params=params(),
         cost_estimate=COST,
         name="write_weight",
-    )(place, held, piece, lax.ppermute(piece, "core", SWAP), *done)
+    )(place, held, *pieces, *done)
 
 
 def after(value, *others):
@@ -521,21 +480,21 @@
     m_new, v_new, update = adam(fixes, grads, *olds)
     pair_0, pair_1, near = unturn(exchange(update))
 
-    up_0, down_0 = ring(pair_0, pair_0)
-    up_1, down_1 = ring(pair_1, pair_1)
+    def step(piece):
+        return lax.ppermute(piece, ("z", "core"), ROUND)
+
+    low_1, high_1 = step(pair_0), step(pair_1)
     held = hold(after(weight_t, near))
-    new_weight = write_weight(place, held, near, NEAR, None)
+    new_weight = write_weight(place, held, (near,), ((0, 0),), None)
     state = new_state(m_new, v_new, m_codes.shape[0], half)
-    up_0, down_0, new_weight, *state = lax.optimization_barrier((up_0, down_0, new_weight, *state))
-    up2, down2 = relayed(up_0, down_0)
-    up_1, down_1 = lax.optimization_barrier((up_1, down_1, up2))[:2]
-    far_0 = ring(up2, down2)
-    up2, down2 = relayed(up_1, down_1)
-    sides = gathered(up_0, down_0, up_1, after(down_1, up2), *far_0)
-    up2, down2 = ring(up2, down2)
-    new_weight = write_weight(place, held, sides, SIDES, new_weight)
-    up2, down2, new_weight = lax.optimization_barrier((up2, down2, new_weight))
-    new_weight = write_weight(place, held, gathered(up2, down2), FAR, new_weight)
+    low_1, new_weight, *state = lax.optimization_barrier((low_1, new_weight, *state))
+    low_2, high_2 = step(low_1), step(high_1)
+    low_3, high_3 = step(low_2), step(high_2)
+    pieces = lax.optimization_barrier((low_1, high_1, new_weight))
+    new_weight = write_weight(place, held, pieces[:2], ((0, 1), (BACK, 1)), pieces[2])
+    pieces = lax.optimization_barrier((low_2, high_2, low_3, high_3, new_weight))
+    new_weight = write_weight(place, held, pieces[:2], ((0, 2), (BACK, 2)), pieces[4])
+    new_weight = write_weight(place, held, pieces[2:4], ((0, 3), (BACK, 3)), new_weight)
     return (new_weight.T, *state)
 
 

time: 139 us -> 137 us (0.986)
  waiting for transfers between devices: 38.3 us -> 30.4 us
  starting transfers between devices: 30.9 us -> 35.5 us
    ppermute x16 -> x8, waiting for transfers between devices: 21.5 us -> 1.65 us  [ring(): return (lax.ppermute(up, 'z', UP), lax.ppermute(down, 'z', DOWN))]
    ppermute x3 -> x13, starting transfers between devices: 3.08 us -> 15.2 us  [the longest x6 11.5 us: step(): return lax.ppermute(piece, ('z', 'core'), ROUND)]
    ppermute x3 -> x13, waiting for transfers between devices: 4.45 us -> 16.3 us  [the longest x6 14.6 us: step(): return lax.ppermute(piece, ('z', 'core'), ROUND)]
    ppermute x16 -> x8, starting transfers between devices: 21.7 us -> 14.3 us  [ring(): return (lax.ppermute(up, 'z', UP), lax.ppermute(down, 'z', DOWN))]
    pallas_call x3 -> x4, Pallas kernels: 6.58 us -> 7.83 us  [write_weight(): pl.pallas_call(functools.partial(weight_kernel, spots), in_specs=[SMEM] +...]
  transfers between devices with their start and end apart: 23 -> 25, of which waited for: 16 -> 14; matrix products, arithmetic and copies ran while one was open for 0% -> 0% of each run, Pallas kernels for 11% -> 12%
where the time goes in v5:
time: 137 us; the launch traced here: 136 us
  blocking collectives  46 us (34%)
  starting transfers between devices  35.5 us (26%)
  waiting for transfers between devices  30.4 us (22%)
  Pallas kernels  22.5 us (16%)
  between operations  1.76 us (1%)
    all_to_all x2, blocking collectives, exchange(): lax.all_to_all(array, ROW_OWNERS, split_axis=0, concat_axis=0, tiled=True)  46 us
    ppermute x6, waiting for transfers between devices, step(): return lax.ppermute(piece, ('z', 'core'), ROUND)  14.6 us
    ppermute x8, starting transfers between devices, ring(): return (lax.ppermute(up, 'z', UP), lax.ppermute(down, 'z', DOWN))  14.3 us
    ppermute x6, starting transfers between devices, step(): return lax.ppermute(piece, ('z', 'core'), ROUND)  11.5 us
    pallas_call x4, Pallas kernels, write_weight(): pl.pallas_call(functools.partial(weight_kernel, spots), in_specs=[SMEM] +...  7.83 us
    ppermute x1, waiting for transfers between devices, shards(): across = lax.ppermute(across, 'z', ACROSS)  5.93 us
    ppermute x1, waiting for transfers between devices, shards(): arrived = lax.ppermute(send, 'yh', SWAP)  3.74 us
    ppermute x7, starting transfers between devices, write_weight(): pieces = list(pieces) + [lax.ppermute(p, 'core', SWAP) for p in pieces]  3.67 us
  transfers between devices with their start and end apart: 25, of which 14 were waited for; matrix products, arithmetic and copies ran while one was open for 0% of the time, Pallas kernels for 12%

profile of v5, /device:TPU:1, one launch (start us, length us, event | category | flops | bytes accessed | tf_op | source)
XLA Modules:
  0.0 136.4 jit_solution(12936692076338872428)
XLA Ops:
  0.7 2.2 %take_part.2 = f32[400,1024]{1,0:T(8,128)S(1)} custom-call(s32[3]{0:T(128)S(1)} %pad_add_fusion.place, f32[1984,1024]{1,0:T(8,128)} %bitcast.12), custom_call_target="tpu_custom_call" | custom-call | flops 1 | bytes 1024 | tf_op jit(solution)/shard_map/take_part/pallas_call | solution.py:162
  3.0 1.5 %collective-permute-start = (f32[400,1024]{1,0:T(8,128)S(1)}, f32[400,1024]{1,0:T(8,128)S(1)}, u32[]{:S(2)}, u32[]{:S(2)}) collective-permute-start(f32[400,1024]{1,0:T(8,128)S(1)} %take_part.2), channel_id=1, source_target_pairs={{0,8},{8,0},{1,9},{9,1},{2,10},{10,2},{3,11},{11,3},{4,12},{12,4},... | collective-permute-start | bytes 4915208 | tf_op jit(solution)/shard_map/ppermute | solution.py:458
  4.5 0.8 take_part.3
  5.3 2.3 %collective-permute-done.other = f32[400,1024]{1,0:T(8,128)S(1)} collective-permute-done((f32[400,1024]{1,0:T(8,128)S(1)}, f32[400,1024]{1,0:T(8,128)S(1)}, u32[]{:S(2)}, u32[]{:S(2)}) %collective-permute-start) | collective-permute-done | bytes 1638432 | tf_op jit(solution)/shard_map/ppermute | solution.py:458
  7.6 1.0 pack.1
  8.7 0.5 collective-permute-start.3
  9.1 1.7 %collective-permute-start.1 = (f32[2,400,128]{2,1,0:T(8,128)S(1)}, f32[2,400,128]{2,1,0:T(8,128)S(1)}, u32[]{:S(2)}, u32[]{:S(2)}) collective-permute-start(f32[2,400,128]{2,1,0:T(8,128)S(1)} %get-tuple-element.61), channel_id=1, source_target_pairs={{0,16},{16,32},{32,48},{48,0},{1,17},{17,33},{33,49},{49,1},{2,18}... | collective-permute-start | bytes 1228808 | tf_op jit(solution)/shard_map/ppermute | solution.py:303
  10.8 2.1 %collective-permute-start.2 = (f32[2,400,128]{2,1,0:T(8,128)S(1)}, f32[2,400,128]{2,1,0:T(8,128)S(1)}, u32[]{:S(2)}, u32[]{:S(2)}) collective-permute-start(f32[2,400,128]{2,1,0:T(8,128)S(1)} %get-tuple-element.62), channel_id=1, source_target_pairs={{0,48},{16,0},{32,16},{48,32},{1,49},{17,1},{33,17},{49,33},{2,50}... | collective-permute-start | bytes 1228808 | tf_op jit(solution)/shard_map/ppermute | solution.py:303
  13.0 0.4 collective-permute-done.3.other
  13.4 1.1 pack_rest.1
  14.5 3.1 %collective-permute-start.4 = (f32[96,1024]{1,0:T(8,128)S(1)}, f32[96,1024]{1,0:T(8,128)S(1)}, u32[]{:S(2)}, u32[]{:S(2)}) collective-permute-start(f32[96,1024]{1,0:T(8,128)S(1)} %get-tuple-element.66), channel_id=1, source_target_pairs={{0,64},{64,0},{1,65},{65,1},{2,66},{66,2},{3,67},{67,3},{4,68},{68... | collective-permute-start | bytes 1179656 | tf_op jit(solution)/shard_map/ppermute | solution.py:464
  17.5 1.6 %collective-permute-start.8 = (f32[2,400,128]{2,1,0:T(8,128)S(1)}, f32[2,400,128]{2,1,0:T(8,128)S(1)}, u32[]{:S(2)}, u32[]{:S(2)}) collective-permute-start(f32[2,400,128]{2,1,0:T(8,128)S(1)} %get-tuple-element.74), channel_id=1, source_target_pairs={{0,16},{16,32},{32,48},{48,0},{1,17},{17,33},{33,49},{49,1},{2,18}... | collective-permute-start | bytes 1228808 | tf_op jit(solution)/shard_map/ppermute | solution.py:303
  19.2 2.1 %collective-permute-start.9 = (f32[2,400,128]{2,1,0:T(8,128)S(1)}, f32[2,400,128]{2,1,0:T(8,128)S(1)}, u32[]{:S(2)}, u32[]{:S(2)}) collective-permute-start(f32[2,400,128]{2,1,0:T(8,128)S(1)} %get-tuple-element.75), channel_id=1, source_target_pairs={{0,48},{16,0},{32,16},{48,32},{1,49},{17,1},{33,17},{49,33},{2,50}... | collective-permute-start | bytes 1228808 | tf_op jit(solution)/shard_map/ppermute | solution.py:303
  21.3 1.4 %collective-permute-done.1.up = f32[2,400,128]{2,1,0:T(8,128)S(1)} collective-permute-done((f32[2,400,128]{2,1,0:T(8,128)S(1)}, f32[2,400,128]{2,1,0:T(8,128)S(1)}, u32[]{:S(2)}, u32[]{:S(2)}) %collective-permute-start.1) | collective-permute-done | bytes 409632 | tf_op jit(solution)/shard_map/ppermute | solution.py:303
  22.7 3.7 %collective-permute-done.4.arrived = f32[96,1024]{1,0:T(8,128)S(1)} collective-permute-done((f32[96,1024]{1,0:T(8,128)S(1)}, f32[96,1024]{1,0:T(8,128)S(1)}, u32[]{:S(2)}, u32[]{:S(2)}) %collective-permute-start.4) | collective-permute-done | bytes 393248 | tf_op jit(solution)/shard_map/ppermute | solution.py:464
  26.4 0.7 relay_pack.1
  27.1 1.7 %collective-permute-start.5 = (f32[592,128]{1,0:T(8,128)S(1)}, f32[592,128]{1,0:T(8,128)S(1)}, u32[]{:S(2)}, u32[]{:S(2)}) collective-permute-start(f32[592,128]{1,0:T(8,128)S(1)} %get-tuple-element.68), channel_id=1, source_target_pairs={{0,16},{16,32},{32,48},{48,0},{1,17},{17,33},{33,49},{49,1},{2,18}... | collective-permute-start | bytes 909320 | tf_op jit(solution)/shard_map/ppermute | solution.py:303
  28.9 2.2 %collective-permute-start.6 = (f32[592,128]{1,0:T(8,128)S(1)}, f32[592,128]{1,0:T(8,128)S(1)}, u32[]{:S(2)}, u32[]{:S(2)}) collective-permute-start(f32[592,128]{1,0:T(8,128)S(1)} %get-tuple-element.69), channel_id=1, source_target_pairs={{0,48},{16,0},{32,16},{48,32},{1,49},{17,1},{33,17},{49,33},{2,50}... | collective-permute-start | bytes 909320 | tf_op jit(solution)/shard_map/ppermute | solution.py:303
  31.4 0.5 collective-permute-start.10
  31.9 2.2 %collective-permute-start.11 = (f32[400,128]{1,0:T(8,128)S(1)}, f32[400,128]{1,0:T(8,128)S(1)}, u32[]{:S(2)}, u32[]{:S(2)}) collective-permute-start(f32[400,128]{1,0:T(8,128)S(1)} %get-tuple-element.78), channel_id=1, source_target_pairs={{0,48},{16,0},{32,16},{48,32},{1,49},{17,1},{33,17},{49,33},{2,50}... | collective-permute-start | bytes 614408 | tf_op jit(solution)/shard_map/ppermute | solution.py:303
  34.9 1.0 collective-permute-start.7
  36.0 2.4 %old_state.1 = (f32[16,8,992]{2,1,0:T(8,128)S(1)}, f32[16,8,992]{2,1,0:T(8,128)S(1)}) custom-call(s32[62,2048]{1,0:T(8,128)S(1)} %copy-done.1, s32[62,2048]{1,0:T(8,128)S(1)} %copy-done.2, f32[62]{0:T(128)S(1)} %copy-done.5, f32[62]{0:T(128)S(1)} %copy-done.6, f32[2,128]{1,0:T(2,128)S(1)} %bitcast.16, f32[2,128]{1,0:T(2,128)S(1)} %bitcast.17), custom_call_target="tpu_custom_call" | custom-call | flops 1 | bytes 1024 | tf_op jit(solution)/shard_map/old_state/pallas_call | solution.py:101
  38.4 5.9 %collective-permute-done.7.across = f32[2,96,128]{2,1,0:T(8,128)S(1)} collective-permute-done((f32[2,96,128]{2,1,0:T(8,128)S(1)}, f32[2,96,128]{2,1,0:T(8,128)S(1)}, u32[]{:S(2)}, u32[]{:S(2)}) %collective-permute-start.7) | collective-permute-done | bytes 98336 | tf_op jit(solution)/shard_map/ppermute | solution.py:467
  44.7 25.2 %all_to_all.10.grads = f32[32,8,896]{2,1,0:T(8,128)S(1)} all-to-all(f32[32,8,896]{2,1,0:T(8,128)S(1)} %turn.1), channel_id=1, replica_groups=mesh['yh'=2,'z'=4,'core'=2,'yl'=2,'x'=4] {'yh','core','yl','x'}, dimensions={0} | all-to-all | bytes 1835008 | tf_op jit(solution)/shard_map/all_to_all | solution.py:330
  69.9 0.9 adam.1
  70.9 20.8 %all_to_all.11.rows = f32[32,8,992]{2,1,0:T(8,128)S(1)} all-to-all(f32[32,8,992]{2,1,0:T(8,128)S(1)} %get-tuple-element.90), channel_id=1, replica_groups=mesh['yh'=2,'z'=4,'core'=2,'yl'=2,'x'=4] {'yh','core','yl','x'}, dimensions={0} | all-to-all | bytes 2031616 | tf_op jit(solution)/shard_map/all_to_all | solution.py:330
  92.2 1.6 %collective-permute-start.15 = (f32[2,496,128]{2,1,0:T(8,128)S(1)}, f32[2,496,128]{2,1,0:T(8,128)S(1)}, u32[]{:S(2)}, u32[]{:S(2)}) collective-permute-start(f32[2,496,128]{2,1,0:T(8,128)S(1)} %get-tuple-element.101), channel_id=1, source_target_pairs={{0,16},{8,56},{16,32},{24,8},{32,48},{40,24},{48,0},{56,40},{1,17}... | collective-permute-start | bytes 1523720 | tf_op jit(solution)/shard_map/ppermute | solution.py:484
  93.8 1.4 %new_state.1 = (bf16[62,2048]{1,0:T(8,128)(2,1)}, bf16[62,2048]{1,0:T(8,128)(2,1)}, f32[1,62]{1,0:T(1,128)}, f32[1,62]{1,0:T(1,128)}) custom-call(f32[16,8,992]{2,1,0:T(8,128)S(1)} %get-tuple-element.94.m_in, f32[16,8,992]{2,1,0:T(8,128)S(1)} %get-tuple-element.95.v_in), custom_call_target="tpu_custom_call" | custom-call | flops 1 | bytes 1024 | tf_op jit(solution)/shard_map/new_state/pallas_call | solution.py:130
  95.2 3.3 %hold.1.weight = f32[1984,1024]{1,0:T(8,128)S(1)} custom-call(f32[1984,1024]{1,0:T(8,128)} %bitcast.19), custom_call_target="tpu_custom_call" | custom-call | flops 1 | bytes 1024 | tf_op jit(solution)/shard_map/hold/pallas_call | solution.py:417
  98.6 1.7 %collective-permute-done.15.refs_1_ = f32[2,496,128]{2,1,0:T(8,128)S(1)} collective-permute-done((f32[2,496,128]{2,1,0:T(8,128)S(1)}, f32[2,496,128]{2,1,0:T(8,128)S(1)}, u32[]{:S(2)}, u32[]{:S(2)}) %collective-permute-start.15) | collective-permute-done | bytes 507936 | tf_op jit(solution)/shard_map/ppermute | solution.py:484
  100.3 2.5 %collective-permute-start.16 = (f32[2,496,128]{2,1,0:T(8,128)S(1)}, f32[2,496,128]{2,1,0:T(8,128)S(1)}, u32[]{:S(2)}, u32[]{:S(2)}) collective-permute-start(f32[2,496,128]{2,1,0:T(8,128)S(1)} %collective-permute-done.15.refs_1_), channel_id=1, source_target_pairs={{0,16},{8,56},{16,32},{24,8},{32,48},{40,24},{48,0},{56,40},{1,17}... | collective-permute-start | bytes 1523720 | tf_op jit(solution)/shard_map/ppermute | solution.py:484
  102.8 2.0 %write_weight.4.refs_4_ = f32[1984,1024]{1,0:T(8,128)} custom-call(s32[3]{0:T(128)S(1)} %pad_add_fusion.place, f32[1984,1024]{1,0:T(8,128)S(1)} %hold.1.weight, f32[2,992,128]{2,1,0:T(8,128)S(1)} %get-tuple-element.91.refs_0_, f32[2,992,128]{2,1,0:T(8,128)S(1)} %collective-permute-done.13.refs_1_), custom_call_target="tpu_custom_call" | custom-call | flops 1 | bytes 1024 | tf_op jit(solution)/shard_map/write_weight/pallas_call | solution.py:434
  104.8 1.0 collective-permute-done.12.refs_0_
  105.8 2.5 %collective-permute-start.14 = (f32[2,496,128]{2,1,0:T(8,128)S(1)}, f32[2,496,128]{2,1,0:T(8,128)S(1)}, u32[]{:S(2)}, u32[]{:S(2)}) collective-permute-start(f32[2,496,128]{2,1,0:T(8,128)S(1)} %collective-permute-done.12.refs_0_), channel_id=1, source_target_pairs={{0,16},{8,56},{16,32},{24,8},{32,48},{40,24},{48,0},{56,40},{1,17}... | collective-permute-start | bytes 1523720 | tf_op jit(solution)/shard_map/ppermute | solution.py:484
  108.3 0.5 collective-permute-start.20
  108.7 2.5 %collective-permute-done.16.refs_1_ = f32[2,496,128]{2,1,0:T(8,128)S(1)} collective-permute-done((f32[2,496,128]{2,1,0:T(8,128)S(1)}, f32[2,496,128]{2,1,0:T(8,128)S(1)}, u32[]{:S(2)}, u32[]{:S(2)}) %collective-permute-start.16) | collective-permute-done | bytes 507936 | tf_op jit(solution)/shard_map/ppermute | solution.py:484
  111.2 2.5 %collective-permute-start.18 = (f32[2,496,128]{2,1,0:T(8,128)S(1)}, f32[2,496,128]{2,1,0:T(8,128)S(1)}, u32[]{:S(2)}, u32[]{:S(2)}) collective-permute-start(f32[2,496,128]{2,1,0:T(8,128)S(1)} %collective-permute-done.16.refs_1_), channel_id=1, source_target_pairs={{0,16},{8,56},{16,32},{24,8},{32,48},{40,24},{48,0},{56,40},{1,17}... | collective-permute-start | bytes 1523720 | tf_op jit(solution)/shard_map/ppermute | solution.py:484
  113.7 3.0 %collective-permute-done.14.refs_0_ = f32[2,496,128]{2,1,0:T(8,128)S(1)} collective-permute-done((f32[2,496,128]{2,1,0:T(8,128)S(1)}, f32[2,496,128]{2,1,0:T(8,128)S(1)}, u32[]{:S(2)}, u32[]{:S(2)}) %collective-permute-start.14) | collective-permute-done | bytes 507936 | tf_op jit(solution)/shard_map/ppermute | solution.py:484
  116.6 2.5 %collective-permute-start.17 = (f32[2,496,128]{2,1,0:T(8,128)S(1)}, f32[2,496,128]{2,1,0:T(8,128)S(1)}, u32[]{:S(2)}, u32[]{:S(2)}) collective-permute-start(f32[2,496,128]{2,1,0:T(8,128)S(1)} %collective-permute-done.14.refs_0_), channel_id=1, source_target_pairs={{0,16},{8,56},{16,32},{24,8},{32,48},{40,24},{48,0},{56,40},{1,17}... | collective-permute-start | bytes 1523720 | tf_op jit(solution)/shard_map/ppermute | solution.py:484
  119.1 2.0 %write_weight.5.refs_4_ = f32[1984,1024]{1,0:T(8,128)} custom-call(s32[3]{0:T(128)S(1)} %pad_add_fusion.place, f32[1984,1024]{1,0:T(8,128)S(1)} %hold.1.weight, f32[2,496,128]{2,1,0:T(8,128)S(1)} %collective-permute-done.12.refs_0_, f32[2,496,128]{2,1,0:T(8,128)S(1)} %collective-permute-done.15.refs_1_, ...), custom_call_target="tpu_custom_call", output_to_operand_aliasing={{}: (6, {})} | custom-call | flops 1 | bytes 1024 | tf_op jit(solution)/shard_map/write_weight/pallas_call | solution.py:434
  121.1 1.0 collective-permute-done.18.refs_1_
  122.1 5.4 %collective-permute-done.17.refs_0_ = f32[2,496,128]{2,1,0:T(8,128)S(1)} collective-permute-done((f32[2,496,128]{2,1,0:T(8,128)S(1)}, f32[2,496,128]{2,1,0:T(8,128)S(1)}, u32[]{:S(2)}, u32[]{:S(2)}) %collective-permute-start.17) | collective-permute-done | bytes 507936 | tf_op jit(solution)/shard_map/ppermute | solution.py:484
  127.5 2.5 %collective-permute-start.23 = (f32[2,496,128]{2,1,0:T(8,128)S(1)}, f32[2,496,128]{2,1,0:T(8,128)S(1)}, u32[]{:S(2)}, u32[]{:S(2)}) collective-permute-start(f32[2,496,128]{2,1,0:T(8,128)S(1)} %collective-permute-done.14.refs_0_), channel_id=1, source_target_pairs={{0,8},{8,0},{1,9},{9,1},{2,10},{10,2},{3,11},{11,3},{4,12},{12,4},... | collective-permute-start | bytes 1523720 | tf_op jit(solution)/shard_map/ppermute | solution.py:431
  130.0 0.5 collective-permute-start.21
  130.5 1.0 collective-permute-done.23.refs_2_
  131.5 0.7 collective-permute-done.24.refs_3_
  132.3 2.0 %write_weight.6.refs_4_ = f32[1984,1024]{1,0:T(8,128)} custom-call(s32[3]{0:T(128)S(1)} %pad_add_fusion.place, f32[1984,1024]{1,0:T(8,128)S(1)} %hold.1.weight, f32[2,496,128]{2,1,0:T(8,128)S(1)} %collective-permute-done.14.refs_0_, f32[2,496,128]{2,1,0:T(8,128)S(1)} %collective-permute-done.16.refs_1_, ...), custom_call_target="tpu_custom_call", output_to_operand_aliasing={{}: (6, {})} | custom-call | flops 1 | bytes 1024 | tf_op jit(solution)/shard_map/write_weight/pallas_call | solution.py:434
  134.2 2.0 %write_weight.7 = f32[1984,1024]{1,0:T(8,128)} custom-call(s32[3]{0:T(128)S(1)} %pad_add_fusion.place, f32[1984,1024]{1,0:T(8,128)S(1)} %hold.1.weight, f32[2,496,128]{2,1,0:T(8,128)S(1)} %collective-permute-done.17.refs_0_, f32[2,496,128]{2,1,0:T(8,128)S(1)} %collective-permute-done.18.refs_1_, ...), custom_call_target="tpu_custom_call", output_to_operand_aliasing={{}: (6, {})} | custom-call | flops 1 | bytes 1024 | tf_op jit(solution)/shard_map/write_weight/pallas_call | solution.py:434
  (36 shorter events, 1.5 us)
Async XLA Ops:
  0.6 3.8 %copy-start = (f32[1,1024,1984]{1,2,0:T(8,128)S(1)}, f32[1,1024,1984]{1,2,0:T(8,128)}, u32[]{:S(2)}) copy-start(f32[1,1024,1984]{1,2,0:T(8,128)} %param.10) | copy-start | bytes 24379396
  3.0 4.6 %collective-permute-start = (f32[400,1024]{1,0:T(8,128)S(1)}, f32[400,1024]{1,0:T(8,128)S(1)}, u32[]{:S(2)}, u32[]{:S(2)}) collective-permute-start(f32[400,1024]{1,0:T(8,128)S(1)} %take_part.2), channel_id=1, source_target_pairs={{0,8},{8,0},{1,9},{9,1},{2,10},{10,2},{3,11},{11,3},{4,12},{12,4},... | collective-permute-start | bytes 4915208 | tf_op jit(solution)/shard_map/ppermute | solution.py:458
  8.6 27.4 %copy-start.1 = (s32[62,2048]{1,0:T(8,128)S(1)}, s32[62,2048]{1,0:T(8,128)}, u32[]{:S(2)}) copy-start(s32[62,2048]{1,0:T(8,128)} %m_codes) | copy-start | bytes 1523716
  8.6 27.4 %copy-start.2 = (s32[62,2048]{1,0:T(8,128)S(1)}, s32[62,2048]{1,0:T(8,128)}, u32[]{:S(2)}) copy-start(s32[62,2048]{1,0:T(8,128)} %v_codes.1) | copy-start | bytes 1523716
  8.6 27.4 %copy-start.3 = (f32[256]{0:T(256)S(1)}, f32[256]{0:T(256)}, u32[]{:S(2)}) copy-start(f32[256]{0:T(256)} %param.15) | copy-start | bytes 3076
  8.6 27.4 %copy-start.4 = (f32[256]{0:T(256)S(1)}, f32[256]{0:T(256)}, u32[]{:S(2)}) copy-start(f32[256]{0:T(256)} %param.16) | copy-start | bytes 3076
  8.6 27.4 %copy-start.5 = (f32[62]{0:T(128)S(1)}, f32[62]{0:T(128)}, u32[]{:S(2)}) copy-start(f32[62]{0:T(128)} %m_scale.1) | copy-start | bytes 748
  8.7 27.4 %copy-start.6 = (f32[62]{0:T(128)S(1)}, f32[62]{0:T(128)}, u32[]{:S(2)}) copy-start(f32[62]{0:T(128)} %v_scale.1) | copy-start | bytes 748
  8.7 4.7 %collective-permute-start.3 = (f32[592,1024]{1,0:T(8,128)S(1)}, f32[592,1024]{1,0:T(8,128)S(1)}, u32[]{:S(2)}, u32[]{:S(2)}) collective-permute-start(f32[592,1024]{1,0:T(8,128)S(1)} %take_part.3), channel_id=1, source_target_pairs={{0,8},{8,0},{1,9},{9,1},{2,10},{10,2},{3,11},{11,3},{4,12},{12,4},... | collective-permute-start | bytes 7274504 | tf_op jit(solution)/shard_map/ppermute | solution.py:462
  9.1 13.5 %collective-permute-start.1 = (f32[2,400,128]{2,1,0:T(8,128)S(1)}, f32[2,400,128]{2,1,0:T(8,128)S(1)}, u32[]{:S(2)}, u32[]{:S(2)}) collective-permute-start(f32[2,400,128]{2,1,0:T(8,128)S(1)} %get-tuple-element.61), channel_id=1, source_target_pairs={{0,16},{16,32},{32,48},{48,0},{1,17},{17,33},{33,49},{49,1},{2,18}... | collective-permute-start | bytes 1228808 | tf_op jit(solution)/shard_map/ppermute | solution.py:303
  10.8 11.8 %collective-permute-start.2 = (f32[2,400,128]{2,1,0:T(8,128)S(1)}, f32[2,400,128]{2,1,0:T(8,128)S(1)}, u32[]{:S(2)}, u32[]{:S(2)}) collective-permute-start(f32[2,400,128]{2,1,0:T(8,128)S(1)} %get-tuple-element.62), channel_id=1, source_target_pairs={{0,48},{16,0},{32,16},{48,32},{1,49},{17,1},{33,17},{49,33},{2,50}... | collective-permute-start | bytes 1228808 | tf_op jit(solution)/shard_map/ppermute | solution.py:303
  14.5 12.0 %collective-permute-start.4 = (f32[96,1024]{1,0:T(8,128)S(1)}, f32[96,1024]{1,0:T(8,128)S(1)}, u32[]{:S(2)}, u32[]{:S(2)}) collective-permute-start(f32[96,1024]{1,0:T(8,128)S(1)} %get-tuple-element.66), channel_id=1, source_target_pairs={{0,64},{64,0},{1,65},{65,1},{2,66},{66,2},{3,67},{67,3},{4,68},{68... | collective-permute-start | bytes 1179656 | tf_op jit(solution)/shard_map/ppermute | solution.py:464
  17.5 13.8 %collective-permute-start.8 = (f32[2,400,128]{2,1,0:T(8,128)S(1)}, f32[2,400,128]{2,1,0:T(8,128)S(1)}, u32[]{:S(2)}, u32[]{:S(2)}) collective-permute-start(f32[2,400,128]{2,1,0:T(8,128)S(1)} %get-tuple-element.74), channel_id=1, source_target_pairs={{0,16},{16,32},{32,48},{48,0},{1,17},{17,33},{33,49},{49,1},{2,18}... | collective-permute-start | bytes 1228808 | tf_op jit(solution)/shard_map/ppermute | solution.py:303
  19.2 12.2 %collective-permute-start.9 = (f32[2,400,128]{2,1,0:T(8,128)S(1)}, f32[2,400,128]{2,1,0:T(8,128)S(1)}, u32[]{:S(2)}, u32[]{:S(2)}) collective-permute-start(f32[2,400,128]{2,1,0:T(8,128)S(1)} %get-tuple-element.75), channel_id=1, source_target_pairs={{0,48},{16,0},{32,16},{48,32},{1,49},{17,1},{33,17},{49,33},{2,50}... | collective-permute-start | bytes 1228808 | tf_op jit(solution)/shard_map/ppermute | solution.py:303
  27.1 17.2 %collective-permute-start.5 = (f32[592,128]{1,0:T(8,128)S(1)}, f32[592,128]{1,0:T(8,128)S(1)}, u32[]{:S(2)}, u32[]{:S(2)}) collective-permute-start(f32[592,128]{1,0:T(8,128)S(1)} %get-tuple-element.68), channel_id=1, source_target_pairs={{0,16},{16,32},{32,48},{48,0},{1,17},{17,33},{33,49},{49,1},{2,18}... | collective-permute-start | bytes 909320 | tf_op jit(solution)/shard_map/ppermute | solution.py:303
  28.9 15.5 %collective-permute-start.6 = (f32[592,128]{1,0:T(8,128)S(1)}, f32[592,128]{1,0:T(8,128)S(1)}, u32[]{:S(2)}, u32[]{:S(2)}) collective-permute-start(f32[592,128]{1,0:T(8,128)S(1)} %get-tuple-element.69), channel_id=1, source_target_pairs={{0,48},{16,0},{32,16},{48,32},{1,49},{17,1},{33,17},{49,33},{2,50}... | collective-permute-start | bytes 909320 | tf_op jit(solution)/shard_map/ppermute | solution.py:303
  31.4 13.0 %collective-permute-start.10 = (f32[400,128]{1,0:T(8,128)S(1)}, f32[400,128]{1,0:T(8,128)S(1)}, u32[]{:S(2)}, u32[]{:S(2)}) collective-permute-start(f32[400,128]{1,0:T(8,128)S(1)} %get-tuple-element.77), channel_id=1, source_target_pairs={{0,16},{16,32},{32,48},{48,0},{1,17},{17,33},{33,49},{49,1},{2,18}... | collective-permute-start | bytes 614408 | tf_op jit(solution)/shard_map/ppermute | solution.py:303
  31.9 12.5 %collective-permute-start.11 = (f32[400,128]{1,0:T(8,128)S(1)}, f32[400,128]{1,0:T(8,128)S(1)}, u32[]{:S(2)}, u32[]{:S(2)}) collective-permute-start(f32[400,128]{1,0:T(8,128)S(1)} %get-tuple-element.78), channel_id=1, source_target_pairs={{0,48},{16,0},{32,16},{48,32},{1,49},{17,1},{33,17},{49,33},{2,50}... | collective-permute-start | bytes 614408 | tf_op jit(solution)/shard_map/ppermute | solution.py:303
  34.9 9.5 %collective-permute-start.7 = (f32[2,96,128]{2,1,0:T(8,128)S(1)}, f32[2,96,128]{2,1,0:T(8,128)S(1)}, u32[]{:S(2)}, u32[]{:S(2)}) collective-permute-start(f32[2,96,128]{2,1,0:T(8,128)S(1)} %get-tuple-element.71), channel_id=1, source_target_pairs={{0,32},{16,48},{32,0},{48,16},{1,33},{17,49},{33,1},{49,17},{2,34}... | collective-permute-start | bytes 294920 | tf_op jit(solution)/shard_map/ppermute | solution.py:467
  92.0 10.8 %collective-permute-start.13 = (f32[2,992,128]{2,1,0:T(8,128)S(1)}, f32[2,992,128]{2,1,0:T(8,128)S(1)}, u32[]{:S(2)}, u32[]{:S(2)}) collective-permute-start(f32[2,992,128]{2,1,0:T(8,128)S(1)} %get-tuple-element.91.refs_0_), channel_id=1, source_target_pairs={{0,8},{8,0},{1,9},{9,1},{2,10},{10,2},{3,11},{11,3},{4,12},{12,4},... | collective-permute-start | bytes 3047432 | tf_op jit(solution)/shard_map/ppermute | solution.py:431
  92.2 8.2 %collective-permute-start.15 = (f32[2,496,128]{2,1,0:T(8,128)S(1)}, f32[2,496,128]{2,1,0:T(8,128)S(1)}, u32[]{:S(2)}, u32[]{:S(2)}) collective-permute-start(f32[2,496,128]{2,1,0:T(8,128)S(1)} %get-tuple-element.101), channel_id=1, source_target_pairs={{0,16},{8,56},{16,32},{24,8},{32,48},{40,24},{48,0},{56,40},{1,17}... | collective-permute-start | bytes 1523720 | tf_op jit(solution)/shard_map/ppermute | solution.py:484
  93.7 12.0 %collective-permute-start.12 = (f32[2,496,128]{2,1,0:T(8,128)S(1)}, f32[2,496,128]{2,1,0:T(8,128)S(1)}, u32[]{:S(2)}, u32[]{:S(2)}) collective-permute-start(f32[2,496,128]{2,1,0:T(8,128)S(1)} %get-tuple-element.93), channel_id=1, source_target_pairs={{0,16},{8,56},{16,32},{24,8},{32,48},{40,24},{48,0},{56,40},{1,17}... | collective-permute-start | bytes 1523720 | tf_op jit(solution)/shard_map/ppermute | solution.py:484
  100.3 10.9 %collective-permute-start.16 = (f32[2,496,128]{2,1,0:T(8,128)S(1)}, f32[2,496,128]{2,1,0:T(8,128)S(1)}, u32[]{:S(2)}, u32[]{:S(2)}) collective-permute-start(f32[2,496,128]{2,1,0:T(8,128)S(1)} %collective-permute-done.15.refs_1_), channel_id=1, source_target_pairs={{0,16},{8,56},{16,32},{24,8},{32,48},{40,24},{48,0},{56,40},{1,17}... | collective-permute-start | bytes 1523720 | tf_op jit(solution)/shard_map/ppermute | solution.py:484
  105.8 10.9 %collective-permute-start.14 = (f32[2,496,128]{2,1,0:T(8,128)S(1)}, f32[2,496,128]{2,1,0:T(8,128)S(1)}, u32[]{:S(2)}, u32[]{:S(2)}) collective-permute-start(f32[2,496,128]{2,1,0:T(8,128)S(1)} %collective-permute-done.12.refs_0_), channel_id=1, source_target_pairs={{0,16},{8,56},{16,32},{24,8},{32,48},{40,24},{48,0},{56,40},{1,17}... | collective-permute-start | bytes 1523720 | tf_op jit(solution)/shard_map/ppermute | solution.py:484
  108.2 10.9 %collective-permute-start.19 = (f32[2,496,128]{2,1,0:T(8,128)S(1)}, f32[2,496,128]{2,1,0:T(8,128)S(1)}, u32[]{:S(2)}, u32[]{:S(2)}) collective-permute-start(f32[2,496,128]{2,1,0:T(8,128)S(1)} %collective-permute-done.12.refs_0_), channel_id=1, source_target_pairs={{0,8},{8,0},{1,9},{9,1},{2,10},{10,2},{3,11},{11,3},{4,12},{12,4},... | collective-permute-start | bytes 1523720 | tf_op jit(solution)/shard_map/ppermute | solution.py:431
  108.3 10.9 %collective-permute-start.20 = (f32[2,496,128]{2,1,0:T(8,128)S(1)}, f32[2,496,128]{2,1,0:T(8,128)S(1)}, u32[]{:S(2)}, u32[]{:S(2)}) collective-permute-start(f32[2,496,128]{2,1,0:T(8,128)S(1)} %collective-permute-done.15.refs_1_), channel_id=1, source_target_pairs={{0,8},{8,0},{1,9},{9,1},{2,10},{10,2},{3,11},{11,3},{4,12},{12,4},... | collective-permute-start | bytes 1523720 | tf_op jit(solution)/shard_map/ppermute | solution.py:431
  111.2 10.9 %collective-permute-start.18 = (f32[2,496,128]{2,1,0:T(8,128)S(1)}, f32[2,496,128]{2,1,0:T(8,128)S(1)}, u32[]{:S(2)}, u32[]{:S(2)}) collective-permute-start(f32[2,496,128]{2,1,0:T(8,128)S(1)} %collective-permute-done.16.refs_1_), channel_id=1, source_target_pairs={{0,16},{8,56},{16,32},{24,8},{32,48},{40,24},{48,0},{56,40},{1,17}... | collective-permute-start | bytes 1523720 | tf_op jit(solution)/shard_map/ppermute | solution.py:484
  116.6 10.9 %collective-permute-start.17 = (f32[2,496,128]{2,1,0:T(8,128)S(1)}, f32[2,496,128]{2,1,0:T(8,128)S(1)}, u32[]{:S(2)}, u32[]{:S(2)}) collective-permute-start(f32[2,496,128]{2,1,0:T(8,128)S(1)} %collective-permute-done.14.refs_0_), channel_id=1, source_target_pairs={{0,16},{8,56},{16,32},{24,8},{32,48},{40,24},{48,0},{56,40},{1,17}... | collective-permute-start | bytes 1523720 | tf_op jit(solution)/shard_map/ppermute | solution.py:484
  127.5 4.0 %collective-permute-start.23 = (f32[2,496,128]{2,1,0:T(8,128)S(1)}, f32[2,496,128]{2,1,0:T(8,128)S(1)}, u32[]{:S(2)}, u32[]{:S(2)}) collective-permute-start(f32[2,496,128]{2,1,0:T(8,128)S(1)} %collective-permute-done.14.refs_0_), channel_id=1, source_target_pairs={{0,8},{8,0},{1,9},{9,1},{2,10},{10,2},{3,11},{11,3},{4,12},{12,4},... | collective-permute-start | bytes 1523720 | tf_op jit(solution)/shard_map/ppermute | solution.py:431
  130.0 2.2 %collective-permute-start.24 = (f32[2,496,128]{2,1,0:T(8,128)S(1)}, f32[2,496,128]{2,1,0:T(8,128)S(1)}, u32[]{:S(2)}, u32[]{:S(2)}) collective-permute-start(f32[2,496,128]{2,1,0:T(8,128)S(1)} %collective-permute-done.16.refs_1_), channel_id=1, source_target_pairs={{0,8},{8,0},{1,9},{9,1},{2,10},{10,2},{3,11},{11,3},{4,12},{12,4},... | collective-permute-start | bytes 1523720 | tf_op jit(solution)/shard_map/ppermute | solution.py:431
  130.0 4.2 %collective-permute-start.21 = (f32[2,496,128]{2,1,0:T(8,128)S(1)}, f32[2,496,128]{2,1,0:T(8,128)S(1)}, u32[]{:S(2)}, u32[]{:S(2)}) collective-permute-start(f32[2,496,128]{2,1,0:T(8,128)S(1)} %collective-permute-done.17.refs_0_), channel_id=1, source_target_pairs={{0,8},{8,0},{1,9},{9,1},{2,10},{10,2},{3,11},{11,3},{4,12},{12,4},... | collective-permute-start | bytes 1523720 | tf_op jit(solution)/shard_map/ppermute | solution.py:431
  130.5 3.7 %collective-permute-start.22 = (f32[2,496,128]{2,1,0:T(8,128)S(1)}, f32[2,496,128]{2,1,0:T(8,128)S(1)}, u32[]{:S(2)}, u32[]{:S(2)}) collective-permute-start(f32[2,496,128]{2,1,0:T(8,128)S(1)} %collective-permute-done.18.refs_1_), channel_id=1, source_target_pairs={{0,8},{8,0},{1,9},{9,1},{2,10},{10,2},{3,11},{11,3},{4,12},{12,4},... | collective-permute-start | bytes 1523720 | tf_op jit(solution)/shard_map/ppermute | solution.py:431

commit v6 on v5

--- a/solution.py
+++ b/solution.py
@@ -383,13 +383,13 @@
 
 
 def weight_kernel(spots, place, weight, *refs):
-    pieces, (out, held, sem) = refs[: 2 * len(spots)], refs[-3:]
+    pieces, (out, held, sem) = refs[: len(spots)], refs[-3:]
     c, z = place[0], place[1]
     half = weight.shape[0] // N_CORE
     stores = []
     for k, piece in enumerate(pieces):
-        core = c if k < len(spots) else 1 - c
-        start, steps = spots[k % len(spots)]
+        own, start, steps = spots[k]
+        core = c if own else 1 - c
         width = piece.shape[1]
         rows = pl.ds(pl.multiple_of(core * half + start, 8), width)
         for yh in range(N_YH):
@@ -428,7 +428,6 @@
 
 def write_weight(place, held, pieces, spots, so_far):
     done = [] if so_far is None else [so_far]
-    pieces = list(pieces) + [lax.ppermute(p, "core", SWAP) for p in pieces]
     stores = N_YH * len(pieces)
     hbm = pl.BlockSpec(memory_space=pltpu.HBM)
     return pl.pallas_call(
@@ -480,21 +479,30 @@
     m_new, v_new, update = adam(fixes, grads, *olds)
     pair_0, pair_1, near = unturn(exchange(update))
 
+    def swap(piece):
+        return lax.ppermute(piece, "core", SWAP)
+
     def step(piece):
         return lax.ppermute(piece, ("z", "core"), ROUND)
 
     low_1, high_1 = step(pair_0), step(pair_1)
     held = hold(after(weight_t, near))
-    new_weight = write_weight(place, held, (near,), ((0, 0),), None)
+    new_weight = write_weight(place, held, (near, swap(near)), ((True, 0, 0), (False, 0, 0)), None)
     state = new_state(m_new, v_new, m_codes.shape[0], half)
     low_1, new_weight, *state = lax.optimization_barrier((low_1, new_weight, *state))
     low_2, high_2 = step(low_1), step(high_1)
     low_3, high_3 = step(low_2), step(high_2)
-    pieces = lax.optimization_barrier((low_1, high_1, new_weight))
-    new_weight = write_weight(place, held, pieces[:2], ((0, 1), (BACK, 1)), pieces[2])
-    pieces = lax.optimization_barrier((low_2, high_2, low_3, high_3, new_weight))
-    new_weight = write_weight(place, held, pieces[:2], ((0, 2), (BACK, 2)), pieces[4])
-    new_weight = write_weight(place, held, pieces[2:4], ((0, 3), (BACK, 3)), new_weight)
+    low, high, new_weight = lax.optimization_barrier((low_1, high_1, new_weight))
+    spots = ((True, 0, 1), (True, BACK, 1), (False, 0, 1), (False, BACK, 1))
+    new_weight = write_weight(place, held, (low, high, swap(low), swap(high)), spots, new_weight)
+    low_2, high_2, low_3, new_weight = lax.optimization_barrier((low_2, high_2, low_3, new_weight))
+    spots = ((True, 0, 2), (True, BACK, 2), (True, 0, 3))
+    new_weight = write_weight(place, held, (low_2, high_2, low_3), spots, new_weight)
+    low_2, high_2, low_3, high_3, new_weight = lax.optimization_barrier((low_2, high_2, low_3, high_3, new_weight))
+    spots = ((False, 0, 2), (False, BACK, 2))
+    new_weight = write_weight(place, held, (swap(low_2), swap(high_2)), spots, new_weight)
+    spots = ((True, BACK, 3), (False, 0, 3), (False, BACK, 3))
+    new_weight = write_weight(place, held, (high_3, swap(low_3), swap(high_3)), spots, new_weight)
     return (new_weight.T, *state)
 
 

time: 137 us -> 136 us (level)
  waiting for transfers between devices: 30.4 us -> 28.9 us
    ppermute x6, waiting for transfers between devices: 14.6 us -> 13.1 us  [step(): return lax.ppermute(piece, ('z', 'core'), ROUND)]
    pallas_call x4 -> x5, Pallas kernels: 7.83 us -> 9.04 us  [write_weight(): pl.pallas_call(functools.partial(weight_kernel, spots), in_specs=[SMEM] +...]
  transfers between devices with their start and end apart: 25 -> 25, of which waited for: 14 -> 13; matrix products, arithmetic and copies ran while one was open for 0% -> 0% of each run, Pallas kernels for 12% -> 13%
where the time goes in v6:
time: 136 us
  blocking collectives  46 us (34%)
  starting transfers between devices  35.3 us (26%)
  waiting for transfers between devices  28.9 us (21%)
  Pallas kernels  23.7 us (17%)
  between operations  1.79 us (1%)
    all_to_all x2, blocking collectives, exchange(): lax.all_to_all(array, ROW_OWNERS, split_axis=0, concat_axis=0, tiled=True)  46 us
    ppermute x8, starting transfers between devices, ring(): return (lax.ppermute(up, 'z', UP), lax.ppermute(down, 'z', DOWN))  14.3 us
    ppermute x6, waiting for transfers between devices, step(): return lax.ppermute(piece, ('z', 'core'), ROUND)  13.1 us
    ppermute x6, starting transfers between devices, step(): return lax.ppermute(piece, ('z', 'core'), ROUND)  11.3 us
    pallas_call x5, Pallas kernels, write_weight(): pl.pallas_call(functools.partial(weight_kernel, spots), in_specs=[SMEM] +...  9.04 us
    ppermute x1, waiting for transfers between devices, shards(): across = lax.ppermute(across, 'z', ACROSS)  5.93 us
    ppermute x1, waiting for transfers between devices, shards(): arrived = lax.ppermute(send, 'yh', SWAP)  3.76 us
    ppermute x7, starting transfers between devices, swap(): return lax.ppermute(piece, 'core', SWAP)  3.67 us
  transfers between devices with their start and end apart: 25, of which 13 were waited for; matrix products, arithmetic and copies ran while one was open for 0% of the time, Pallas kernels for 13%

profile of v6, /device:TPU:1, one launch (start us, length us, event | category | flops | bytes accessed | tf_op | source)
XLA Modules:
  0.0 135.8 jit_solution(13112040687722391718)
XLA Ops:
  0.7 2.2 %take_part.2 = f32[400,1024]{1,0:T(8,128)S(1)} custom-call(s32[3]{0:T(128)S(1)} %pad_add_fusion.place, f32[1984,1024]{1,0:T(8,128)} %bitcast.12), custom_call_target="tpu_custom_call" | custom-call | flops 1 | bytes 1024 | tf_op jit(solution)/shard_map/take_part/pallas_call | solution.py:162
  3.0 1.5 %collective-permute-start = (f32[400,1024]{1,0:T(8,128)S(1)}, f32[400,1024]{1,0:T(8,128)S(1)}, u32[]{:S(2)}, u32[]{:S(2)}) collective-permute-start(f32[400,1024]{1,0:T(8,128)S(1)} %take_part.2), channel_id=1, source_target_pairs={{0,8},{8,0},{1,9},{9,1},{2,10},{10,2},{3,11},{11,3},{4,12},{12,4},... | collective-permute-start | bytes 4915208 | tf_op jit(solution)/shard_map/ppermute | solution.py:457
  4.5 0.8 take_part.3
  5.3 2.3 %collective-permute-done.other = f32[400,1024]{1,0:T(8,128)S(1)} collective-permute-done((f32[400,1024]{1,0:T(8,128)S(1)}, f32[400,1024]{1,0:T(8,128)S(1)}, u32[]{:S(2)}, u32[]{:S(2)}) %collective-permute-start) | collective-permute-done | bytes 1638432 | tf_op jit(solution)/shard_map/ppermute | solution.py:457
  7.6 1.0 pack.1
  8.7 0.5 collective-permute-start.3
  9.1 1.7 %collective-permute-start.1 = (f32[2,400,128]{2,1,0:T(8,128)S(1)}, f32[2,400,128]{2,1,0:T(8,128)S(1)}, u32[]{:S(2)}, u32[]{:S(2)}) collective-permute-start(f32[2,400,128]{2,1,0:T(8,128)S(1)} %get-tuple-element.65), channel_id=1, source_target_pairs={{0,16},{16,32},{32,48},{48,0},{1,17},{17,33},{33,49},{49,1},{2,18}... | collective-permute-start | bytes 1228808 | tf_op jit(solution)/shard_map/ppermute | solution.py:303
  10.8 2.1 %collective-permute-start.2 = (f32[2,400,128]{2,1,0:T(8,128)S(1)}, f32[2,400,128]{2,1,0:T(8,128)S(1)}, u32[]{:S(2)}, u32[]{:S(2)}) collective-permute-start(f32[2,400,128]{2,1,0:T(8,128)S(1)} %get-tuple-element.66), channel_id=1, source_target_pairs={{0,48},{16,0},{32,16},{48,32},{1,49},{17,1},{33,17},{49,33},{2,50}... | collective-permute-start | bytes 1228808 | tf_op jit(solution)/shard_map/ppermute | solution.py:303
  13.0 0.4 collective-permute-done.3.other
  13.4 1.1 pack_rest.1
  14.5 3.1 %collective-permute-start.4 = (f32[96,1024]{1,0:T(8,128)S(1)}, f32[96,1024]{1,0:T(8,128)S(1)}, u32[]{:S(2)}, u32[]{:S(2)}) collective-permute-start(f32[96,1024]{1,0:T(8,128)S(1)} %get-tuple-element.70), channel_id=1, source_target_pairs={{0,64},{64,0},{1,65},{65,1},{2,66},{66,2},{3,67},{67,3},{4,68},{68... | collective-permute-start | bytes 1179656 | tf_op jit(solution)/shard_map/ppermute | solution.py:463
  17.5 1.6 %collective-permute-start.8 = (f32[2,400,128]{2,1,0:T(8,128)S(1)}, f32[2,400,128]{2,1,0:T(8,128)S(1)}, u32[]{:S(2)}, u32[]{:S(2)}) collective-permute-start(f32[2,400,128]{2,1,0:T(8,128)S(1)} %get-tuple-element.78), channel_id=1, source_target_pairs={{0,16},{16,32},{32,48},{48,0},{1,17},{17,33},{33,49},{49,1},{2,18}... | collective-permute-start | bytes 1228808 | tf_op jit(solution)/shard_map/ppermute | solution.py:303
  19.2 2.1 %collective-permute-start.9 = (f32[2,400,128]{2,1,0:T(8,128)S(1)}, f32[2,400,128]{2,1,0:T(8,128)S(1)}, u32[]{:S(2)}, u32[]{:S(2)}) collective-permute-start(f32[2,400,128]{2,1,0:T(8,128)S(1)} %get-tuple-element.79), channel_id=1, source_target_pairs={{0,48},{16,0},{32,16},{48,32},{1,49},{17,1},{33,17},{49,33},{2,50}... | collective-permute-start | bytes 1228808 | tf_op jit(solution)/shard_map/ppermute | solution.py:303
  21.3 1.4 %collective-permute-done.1.up = f32[2,400,128]{2,1,0:T(8,128)S(1)} collective-permute-done((f32[2,400,128]{2,1,0:T(8,128)S(1)}, f32[2,400,128]{2,1,0:T(8,128)S(1)}, u32[]{:S(2)}, u32[]{:S(2)}) %collective-permute-start.1) | collective-permute-done | bytes 409632 | tf_op jit(solution)/shard_map/ppermute | solution.py:303
  22.7 3.8 %collective-permute-done.4.arrived = f32[96,1024]{1,0:T(8,128)S(1)} collective-permute-done((f32[96,1024]{1,0:T(8,128)S(1)}, f32[96,1024]{1,0:T(8,128)S(1)}, u32[]{:S(2)}, u32[]{:S(2)}) %collective-permute-start.4) | collective-permute-done | bytes 393248 | tf_op jit(solution)/shard_map/ppermute | solution.py:463
  26.4 0.7 relay_pack.1
  27.2 1.7 %collective-permute-start.5 = (f32[592,128]{1,0:T(8,128)S(1)}, f32[592,128]{1,0:T(8,128)S(1)}, u32[]{:S(2)}, u32[]{:S(2)}) collective-permute-start(f32[592,128]{1,0:T(8,128)S(1)} %get-tuple-element.72), channel_id=1, source_target_pairs={{0,16},{16,32},{32,48},{48,0},{1,17},{17,33},{33,49},{49,1},{2,18}... | collective-permute-start | bytes 909320 | tf_op jit(solution)/shard_map/ppermute | solution.py:303
  28.9 2.2 %collective-permute-start.6 = (f32[592,128]{1,0:T(8,128)S(1)}, f32[592,128]{1,0:T(8,128)S(1)}, u32[]{:S(2)}, u32[]{:S(2)}) collective-permute-start(f32[592,128]{1,0:T(8,128)S(1)} %get-tuple-element.73), channel_id=1, source_target_pairs={{0,48},{16,0},{32,16},{48,32},{1,49},{17,1},{33,17},{49,33},{2,50}... | collective-permute-start | bytes 909320 | tf_op jit(solution)/shard_map/ppermute | solution.py:303
  31.4 0.5 collective-permute-start.10
  31.9 2.3 %collective-permute-start.11 = (f32[400,128]{1,0:T(8,128)S(1)}, f32[400,128]{1,0:T(8,128)S(1)}, u32[]{:S(2)}, u32[]{:S(2)}) collective-permute-start(f32[400,128]{1,0:T(8,128)S(1)} %get-tuple-element.82), channel_id=1, source_target_pairs={{0,48},{16,0},{32,16},{48,32},{1,49},{17,1},{33,17},{49,33},{2,50}... | collective-permute-start | bytes 614408 | tf_op jit(solution)/shard_map/ppermute | solution.py:303
  34.9 1.0 collective-permute-start.7
  36.0 2.4 %old_state.1 = (f32[16,8,992]{2,1,0:T(8,128)S(1)}, f32[16,8,992]{2,1,0:T(8,128)S(1)}) custom-call(s32[62,2048]{1,0:T(8,128)S(1)} %copy-done.1, s32[62,2048]{1,0:T(8,128)S(1)} %copy-done.2, f32[62]{0:T(128)S(1)} %copy-done.5, f32[62]{0:T(128)S(1)} %copy-done.6, f32[2,128]{1,0:T(2,128)S(1)} %bitcast.16, f32[2,128]{1,0:T(2,128)S(1)} %bitcast.17), custom_call_target="tpu_custom_call" | custom-call | flops 1 | bytes 1024 | tf_op jit(solution)/shard_map/old_state/pallas_call | solution.py:101
  38.4 5.9 %collective-permute-done.7.across = f32[2,96,128]{2,1,0:T(8,128)S(1)} collective-permute-done((f32[2,96,128]{2,1,0:T(8,128)S(1)}, f32[2,96,128]{2,1,0:T(8,128)S(1)}, u32[]{:S(2)}, u32[]{:S(2)}) %collective-permute-start.7) | collective-permute-done | bytes 98336 | tf_op jit(solution)/shard_map/ppermute | solution.py:466
  44.7 25.2 %all_to_all.10.grads = f32[32,8,896]{2,1,0:T(8,128)S(1)} all-to-all(f32[32,8,896]{2,1,0:T(8,128)S(1)} %turn.1), channel_id=1, replica_groups=mesh['yh'=2,'z'=4,'core'=2,'yl'=2,'x'=4] {'yh','core','yl','x'}, dimensions={0} | all-to-all | bytes 1835008 | tf_op jit(solution)/shard_map/all_to_all | solution.py:330
  69.9 0.9 adam.1
  70.9 20.8 %all_to_all.11.rows = f32[32,8,992]{2,1,0:T(8,128)S(1)} all-to-all(f32[32,8,992]{2,1,0:T(8,128)S(1)} %get-tuple-element.94), channel_id=1, replica_groups=mesh['yh'=2,'z'=4,'core'=2,'yl'=2,'x'=4] {'yh','core','yl','x'}, dimensions={0} | all-to-all | bytes 2031616 | tf_op jit(solution)/shard_map/all_to_all | solution.py:330
  92.2 1.6 %collective-permute-start.12 = (f32[2,496,128]{2,1,0:T(8,128)S(1)}, f32[2,496,128]{2,1,0:T(8,128)S(1)}, u32[]{:S(2)}, u32[]{:S(2)}) collective-permute-start(f32[2,496,128]{2,1,0:T(8,128)S(1)} %get-tuple-element.97), channel_id=1, source_target_pairs={{0,16},{8,56},{16,32},{24,8},{32,48},{40,24},{48,0},{56,40},{1,17}... | collective-permute-start | bytes 1523720 | tf_op jit(solution)/shard_map/ppermute | solution.py:486
  93.8 1.4 %new_state.1 = (bf16[62,2048]{1,0:T(8,128)(2,1)}, bf16[62,2048]{1,0:T(8,128)(2,1)}, f32[1,62]{1,0:T(1,128)}, f32[1,62]{1,0:T(1,128)}) custom-call(f32[16,8,992]{2,1,0:T(8,128)S(1)} %get-tuple-element.98.m_in, f32[16,8,992]{2,1,0:T(8,128)S(1)} %get-tuple-element.99.v_in), custom_call_target="tpu_custom_call" | custom-call | flops 1 | bytes 1024 | tf_op jit(solution)/shard_map/new_state/pallas_call | solution.py:130
  95.2 3.3 %hold.1.weight = f32[1984,1024]{1,0:T(8,128)S(1)} custom-call(f32[1984,1024]{1,0:T(8,128)} %bitcast.19), custom_call_target="tpu_custom_call" | custom-call | flops 1 | bytes 1024 | tf_op jit(solution)/shard_map/hold/pallas_call | solution.py:417
  98.6 2.0 %write_weight.5.refs_4_ = f32[1984,1024]{1,0:T(8,128)} custom-call(s32[3]{0:T(128)S(1)} %pad_add_fusion.place, f32[1984,1024]{1,0:T(8,128)S(1)} %hold.1.weight, f32[2,992,128]{2,1,0:T(8,128)S(1)} %get-tuple-element.95.refs_0_, f32[2,992,128]{2,1,0:T(8,128)S(1)} %collective-permute-done.13.refs_1_), custom_call_target="tpu_custom_call" | custom-call | flops 1 | bytes 1024 | tf_op jit(solution)/shard_map/write_weight/pallas_call | solution.py:433
  100.6 2.2 %collective-permute-start.14 = (f32[2,496,128]{2,1,0:T(8,128)S(1)}, f32[2,496,128]{2,1,0:T(8,128)S(1)}, u32[]{:S(2)}, u32[]{:S(2)}) collective-permute-start(f32[2,496,128]{2,1,0:T(8,128)S(1)} %collective-permute-done.12.refs_0_), channel_id=1, source_target_pairs={{0,16},{8,56},{16,32},{24,8},{32,48},{40,24},{48,0},{56,40},{1,17}... | collective-permute-start | bytes 1523720 | tf_op jit(solution)/shard_map/ppermute | solution.py:486
  102.8 3.0 %collective-permute-done.15.refs_1_ = f32[2,496,128]{2,1,0:T(8,128)S(1)} collective-permute-done((f32[2,496,128]{2,1,0:T(8,128)S(1)}, f32[2,496,128]{2,1,0:T(8,128)S(1)}, u32[]{:S(2)}, u32[]{:S(2)}) %collective-permute-start.15) | collective-permute-done | bytes 507936 | tf_op jit(solution)/shard_map/ppermute | solution.py:486
  105.8 2.5 %collective-permute-start.16 = (f32[2,496,128]{2,1,0:T(8,128)S(1)}, f32[2,496,128]{2,1,0:T(8,128)S(1)}, u32[]{:S(2)}, u32[]{:S(2)}) collective-permute-start(f32[2,496,128]{2,1,0:T(8,128)S(1)} %collective-permute-done.15.refs_1_), channel_id=1, source_target_pairs={{0,16},{8,56},{16,32},{24,8},{32,48},{40,24},{48,0},{56,40},{1,17}... | collective-permute-start | bytes 1523720 | tf_op jit(solution)/shard_map/ppermute | solution.py:486
  108.3 0.5 collective-permute-start.19
  108.7 2.5 %collective-permute-done.14.refs_0_ = f32[2,496,128]{2,1,0:T(8,128)S(1)} collective-permute-done((f32[2,496,128]{2,1,0:T(8,128)S(1)}, f32[2,496,128]{2,1,0:T(8,128)S(1)}, u32[]{:S(2)}, u32[]{:S(2)}) %collective-permute-start.14) | collective-permute-done | bytes 507936 | tf_op jit(solution)/shard_map/ppermute | solution.py:486
  111.2 2.5 %collective-permute-start.17 = (f32[2,496,128]{2,1,0:T(8,128)S(1)}, f32[2,496,128]{2,1,0:T(8,128)S(1)}, u32[]{:S(2)}, u32[]{:S(2)}) collective-permute-start(f32[2,496,128]{2,1,0:T(8,128)S(1)} %collective-permute-done.14.refs_0_), channel_id=1, source_target_pairs={{0,16},{8,56},{16,32},{24,8},{32,48},{40,24},{48,0},{56,40},{1,17}... | collective-permute-start | bytes 1523720 | tf_op jit(solution)/shard_map/ppermute | solution.py:486
  113.7 3.0 %collective-permute-done.16.refs_1_ = f32[2,496,128]{2,1,0:T(8,128)S(1)} collective-permute-done((f32[2,496,128]{2,1,0:T(8,128)S(1)}, f32[2,496,128]{2,1,0:T(8,128)S(1)}, u32[]{:S(2)}, u32[]{:S(2)}) %collective-permute-start.16) | collective-permute-done | bytes 507936 | tf_op jit(solution)/shard_map/ppermute | solution.py:486
  116.6 2.5 %collective-permute-start.20 = (f32[2,496,128]{2,1,0:T(8,128)S(1)}, f32[2,496,128]{2,1,0:T(8,128)S(1)}, u32[]{:S(2)}, u32[]{:S(2)}) collective-permute-start(f32[2,496,128]{2,1,0:T(8,128)S(1)} %collective-permute-done.16.refs_1_), channel_id=1, source_target_pairs={{0,16},{8,56},{16,32},{24,8},{32,48},{40,24},{48,0},{56,40},{1,17}... | collective-permute-start | bytes 1523720 | tf_op jit(solution)/shard_map/ppermute | solution.py:486
  119.1 2.0 %write_weight.6.refs_3_ = f32[1984,1024]{1,0:T(8,128)} custom-call(s32[3]{0:T(128)S(1)} %pad_add_fusion.place, f32[1984,1024]{1,0:T(8,128)S(1)} %hold.1.weight, f32[2,496,128]{2,1,0:T(8,128)S(1)} %collective-permute-done.12.refs_0_, f32[2,496,128]{2,1,0:T(8,128)S(1)} %collective-permute-done.15.refs_1_, ...), custom_call_target="tpu_custom_call", output_to_operand_aliasing={{}: (6, {})} | custom-call | flops 1 | bytes 1024 | tf_op jit(solution)/shard_map/write_weight/pallas_call | solution.py:433
  121.1 1.0 collective-permute-done.17.refs_2_
  122.1 1.8 %write_weight.7.refs_2_ = f32[1984,1024]{1,0:T(8,128)} custom-call(s32[3]{0:T(128)S(1)} %pad_add_fusion.place, f32[1984,1024]{1,0:T(8,128)S(1)} %hold.1.weight, f32[2,496,128]{2,1,0:T(8,128)S(1)} %collective-permute-done.14.refs_0_, f32[2,496,128]{2,1,0:T(8,128)S(1)} %collective-permute-done.16.refs_1_, ...), custom_call_target="tpu_custom_call", output_to_operand_aliasing={{}: (5, {})} | custom-call | flops 1 | bytes 1024 | tf_op jit(solution)/shard_map/write_weight/pallas_call | solution.py:433
  123.9 3.7 %collective-permute-done.20.refs_0_ = f32[2,496,128]{2,1,0:T(8,128)S(1)} collective-permute-done((f32[2,496,128]{2,1,0:T(8,128)S(1)}, f32[2,496,128]{2,1,0:T(8,128)S(1)}, u32[]{:S(2)}, u32[]{:S(2)}) %collective-permute-start.20) | collective-permute-done | bytes 507936 | tf_op jit(solution)/shard_map/ppermute | solution.py:486
  127.5 2.5 %collective-permute-start.23 = (f32[2,496,128]{2,1,0:T(8,128)S(1)}, f32[2,496,128]{2,1,0:T(8,128)S(1)}, u32[]{:S(2)}, u32[]{:S(2)}) collective-permute-start(f32[2,496,128]{2,1,0:T(8,128)S(1)} %collective-permute-done.14.refs_0_), channel_id=1, source_target_pairs={{0,8},{8,0},{1,9},{9,1},{2,10},{10,2},{3,11},{11,3},{4,12},{12,4},... | collective-permute-start | bytes 1523720 | tf_op jit(solution)/shard_map/ppermute | solution.py:483
  130.0 0.5 collective-permute-start.21
  130.5 1.0 collective-permute-done.23.refs_0_
  131.5 0.7 collective-permute-done.24.refs_1_
  132.3 1.6 %write_weight.8.refs_3_ = f32[1984,1024]{1,0:T(8,128)} custom-call(s32[3]{0:T(128)S(1)} %pad_add_fusion.place, f32[1984,1024]{1,0:T(8,128)S(1)} %hold.1.weight, f32[2,496,128]{2,1,0:T(8,128)S(1)} %collective-permute-done.23.refs_0_, f32[2,496,128]{2,1,0:T(8,128)S(1)} %collective-permute-done.24.refs_1_, ...), custom_call_target="tpu_custom_call", output_to_operand_aliasing={{}: (4, {})} | custom-call | flops 1 | bytes 1024 | tf_op jit(solution)/shard_map/write_weight/pallas_call | solution.py:433
  133.9 1.8 %write_weight.9 = f32[1984,1024]{1,0:T(8,128)} custom-call(s32[3]{0:T(128)S(1)} %pad_add_fusion.place, f32[1984,1024]{1,0:T(8,128)S(1)} %hold.1.weight, f32[2,496,128]{2,1,0:T(8,128)S(1)} %collective-permute-done.20.refs_0_, f32[2,496,128]{2,1,0:T(8,128)S(1)} %collective-permute-done.21.refs_1_, ...), custom_call_target="tpu_custom_call", output_to_operand_aliasing={{}: (5, {})} | custom-call | flops 1 | bytes 1024 | tf_op jit(solution)/shard_map/write_weight/pallas_call | solution.py:433
  (37 shorter events, 1.5 us)
Async XLA Ops:
  0.6 3.8 %copy-start = (f32[1,1024,1984]{1,2,0:T(8,128)S(1)}, f32[1,1024,1984]{1,2,0:T(8,128)}, u32[]{:S(2)}) copy-start(f32[1,1024,1984]{1,2,0:T(8,128)} %param.10) | copy-start | bytes 24379396
  3.0 4.6 %collective-permute-start = (f32[400,1024]{1,0:T(8,128)S(1)}, f32[400,1024]{1,0:T(8,128)S(1)}, u32[]{:S(2)}, u32[]{:S(2)}) collective-permute-start(f32[400,1024]{1,0:T(8,128)S(1)} %take_part.2), channel_id=1, source_target_pairs={{0,8},{8,0},{1,9},{9,1},{2,10},{10,2},{3,11},{11,3},{4,12},{12,4},... | collective-permute-start | bytes 4915208 | tf_op jit(solution)/shard_map/ppermute | solution.py:457
  8.6 27.4 %copy-start.1 = (s32[62,2048]{1,0:T(8,128)S(1)}, s32[62,2048]{1,0:T(8,128)}, u32[]{:S(2)}) copy-start(s32[62,2048]{1,0:T(8,128)} %m_codes) | copy-start | bytes 1523716
  8.6 27.4 %copy-start.2 = (s32[62,2048]{1,0:T(8,128)S(1)}, s32[62,2048]{1,0:T(8,128)}, u32[]{:S(2)}) copy-start(s32[62,2048]{1,0:T(8,128)} %v_codes.1) | copy-start | bytes 1523716
  8.6 27.4 %copy-start.3 = (f32[256]{0:T(256)S(1)}, f32[256]{0:T(256)}, u32[]{:S(2)}) copy-start(f32[256]{0:T(256)} %param.15) | copy-start | bytes 3076
  8.6 27.4 %copy-start.4 = (f32[256]{0:T(256)S(1)}, f32[256]{0:T(256)}, u32[]{:S(2)}) copy-start(f32[256]{0:T(256)} %param.16) | copy-start | bytes 3076
  8.6 27.4 %copy-start.5 = (f32[62]{0:T(128)S(1)}, f32[62]{0:T(128)}, u32[]{:S(2)}) copy-start(f32[62]{0:T(128)} %m_scale.1) | copy-start | bytes 748
  8.7 27.4 %copy-start.6 = (f32[62]{0:T(128)S(1)}, f32[62]{0:T(128)}, u32[]{:S(2)}) copy-start(f32[62]{0:T(128)} %v_scale.1) | copy-start | bytes 748
  8.7 4.7 %collective-permute-start.3 = (f32[592,1024]{1,0:T(8,128)S(1)}, f32[592,1024]{1,0:T(8,128)S(1)}, u32[]{:S(2)}, u32[]{:S(2)}) collective-permute-start(f32[592,1024]{1,0:T(8,128)S(1)} %take_part.3), channel_id=1, source_target_pairs={{0,8},{8,0},{1,9},{9,1},{2,10},{10,2},{3,11},{11,3},{4,12},{12,4},... | collective-permute-start | bytes 7274504 | tf_op jit(solution)/shard_map/ppermute | solution.py:461
  9.1 13.5 %collective-permute-start.1 = (f32[2,400,128]{2,1,0:T(8,128)S(1)}, f32[2,400,128]{2,1,0:T(8,128)S(1)}, u32[]{:S(2)}, u32[]{:S(2)}) collective-permute-start(f32[2,400,128]{2,1,0:T(8,128)S(1)} %get-tuple-element.65), channel_id=1, source_target_pairs={{0,16},{16,32},{32,48},{48,0},{1,17},{17,33},{33,49},{49,1},{2,18}... | collective-permute-start | bytes 1228808 | tf_op jit(solution)/shard_map/ppermute | solution.py:303
  10.8 11.8 %collective-permute-start.2 = (f32[2,400,128]{2,1,0:T(8,128)S(1)}, f32[2,400,128]{2,1,0:T(8,128)S(1)}, u32[]{:S(2)}, u32[]{:S(2)}) collective-permute-start(f32[2,400,128]{2,1,0:T(8,128)S(1)} %get-tuple-element.66), channel_id=1, source_target_pairs={{0,48},{16,0},{32,16},{48,32},{1,49},{17,1},{33,17},{49,33},{2,50}... | collective-permute-start | bytes 1228808 | tf_op jit(solution)/shard_map/ppermute | solution.py:303
  14.5 12.0 %collective-permute-start.4 = (f32[96,1024]{1,0:T(8,128)S(1)}, f32[96,1024]{1,0:T(8,128)S(1)}, u32[]{:S(2)}, u32[]{:S(2)}) collective-permute-start(f32[96,1024]{1,0:T(8,128)S(1)} %get-tuple-element.70), channel_id=1, source_target_pairs={{0,64},{64,0},{1,65},{65,1},{2,66},{66,2},{3,67},{67,3},{4,68},{68... | collective-permute-start | bytes 1179656 | tf_op jit(solution)/shard_map/ppermute | solution.py:463
  17.5 13.8 %collective-permute-start.8 = (f32[2,400,128]{2,1,0:T(8,128)S(1)}, f32[2,400,128]{2,1,0:T(8,128)S(1)}, u32[]{:S(2)}, u32[]{:S(2)}) collective-permute-start(f32[2,400,128]{2,1,0:T(8,128)S(1)} %get-tuple-element.78), channel_id=1, source_target_pairs={{0,16},{16,32},{32,48},{48,0},{1,17},{17,33},{33,49},{49,1},{2,18}... | collective-permute-start | bytes 1228808 | tf_op jit(solution)/shard_map/ppermute | solution.py:303
  19.2 12.2 %collective-permute-start.9 = (f32[2,400,128]{2,1,0:T(8,128)S(1)}, f32[2,400,128]{2,1,0:T(8,128)S(1)}, u32[]{:S(2)}, u32[]{:S(2)}) collective-permute-start(f32[2,400,128]{2,1,0:T(8,128)S(1)} %get-tuple-element.79), channel_id=1, source_target_pairs={{0,48},{16,0},{32,16},{48,32},{1,49},{17,1},{33,17},{49,33},{2,50}... | collective-permute-start | bytes 1228808 | tf_op jit(solution)/shard_map/ppermute | solution.py:303
  27.2 17.2 %collective-permute-start.5 = (f32[592,128]{1,0:T(8,128)S(1)}, f32[592,128]{1,0:T(8,128)S(1)}, u32[]{:S(2)}, u32[]{:S(2)}) collective-permute-start(f32[592,128]{1,0:T(8,128)S(1)} %get-tuple-element.72), channel_id=1, source_target_pairs={{0,16},{16,32},{32,48},{48,0},{1,17},{17,33},{33,49},{49,1},{2,18}... | collective-permute-start | bytes 909320 | tf_op jit(solution)/shard_map/ppermute | solution.py:303
  28.9 15.5 %collective-permute-start.6 = (f32[592,128]{1,0:T(8,128)S(1)}, f32[592,128]{1,0:T(8,128)S(1)}, u32[]{:S(2)}, u32[]{:S(2)}) collective-permute-start(f32[592,128]{1,0:T(8,128)S(1)} %get-tuple-element.73), channel_id=1, source_target_pairs={{0,48},{16,0},{32,16},{48,32},{1,49},{17,1},{33,17},{49,33},{2,50}... | collective-permute-start | bytes 909320 | tf_op jit(solution)/shard_map/ppermute | solution.py:303
  31.4 13.0 %collective-permute-start.10 = (f32[400,128]{1,0:T(8,128)S(1)}, f32[400,128]{1,0:T(8,128)S(1)}, u32[]{:S(2)}, u32[]{:S(2)}) collective-permute-start(f32[400,128]{1,0:T(8,128)S(1)} %get-tuple-element.81), channel_id=1, source_target_pairs={{0,16},{16,32},{32,48},{48,0},{1,17},{17,33},{33,49},{49,1},{2,18}... | collective-permute-start | bytes 614408 | tf_op jit(solution)/shard_map/ppermute | solution.py:303
  31.9 12.5 %collective-permute-start.11 = (f32[400,128]{1,0:T(8,128)S(1)}, f32[400,128]{1,0:T(8,128)S(1)}, u32[]{:S(2)}, u32[]{:S(2)}) collective-permute-start(f32[400,128]{1,0:T(8,128)S(1)} %get-tuple-element.82), channel_id=1, source_target_pairs={{0,48},{16,0},{32,16},{48,32},{1,49},{17,1},{33,17},{49,33},{2,50}... | collective-permute-start | bytes 614408 | tf_op jit(solution)/shard_map/ppermute | solution.py:303
  34.9 9.5 %collective-permute-start.7 = (f32[2,96,128]{2,1,0:T(8,128)S(1)}, f32[2,96,128]{2,1,0:T(8,128)S(1)}, u32[]{:S(2)}, u32[]{:S(2)}) collective-permute-start(f32[2,96,128]{2,1,0:T(8,128)S(1)} %get-tuple-element.75), channel_id=1, source_target_pairs={{0,32},{16,48},{32,0},{48,16},{1,33},{17,49},{33,1},{49,17},{2,34}... | collective-permute-start | bytes 294920 | tf_op jit(solution)/shard_map/ppermute | solution.py:466
  92.0 6.6 %collective-permute-start.13 = (f32[2,992,128]{2,1,0:T(8,128)S(1)}, f32[2,992,128]{2,1,0:T(8,128)S(1)}, u32[]{:S(2)}, u32[]{:S(2)}) collective-permute-start(f32[2,992,128]{2,1,0:T(8,128)S(1)} %get-tuple-element.95.refs_0_), channel_id=1, source_target_pairs={{0,8},{8,0},{1,9},{9,1},{2,10},{10,2},{3,11},{11,3},{4,12},{12,4},... | collective-permute-start | bytes 3047432 | tf_op jit(solution)/shard_map/ppermute | solution.py:483
  92.2 8.4 %collective-permute-start.12 = (f32[2,496,128]{2,1,0:T(8,128)S(1)}, f32[2,496,128]{2,1,0:T(8,128)S(1)}, u32[]{:S(2)}, u32[]{:S(2)}) collective-permute-start(f32[2,496,128]{2,1,0:T(8,128)S(1)} %get-tuple-element.97), channel_id=1, source_target_pairs={{0,16},{8,56},{16,32},{24,8},{32,48},{40,24},{48,0},{56,40},{1,17}... | collective-permute-start | bytes 1523720 | tf_op jit(solution)/shard_map/ppermute | solution.py:486
  93.7 12.0 %collective-permute-start.15 = (f32[2,496,128]{2,1,0:T(8,128)S(1)}, f32[2,496,128]{2,1,0:T(8,128)S(1)}, u32[]{:S(2)}, u32[]{:S(2)}) collective-permute-start(f32[2,496,128]{2,1,0:T(8,128)S(1)} %get-tuple-element.105), channel_id=1, source_target_pairs={{0,16},{8,56},{16,32},{24,8},{32,48},{40,24},{48,0},{56,40},{1,17}... | collective-permute-start | bytes 1523720 | tf_op jit(solution)/shard_map/ppermute | solution.py:486
  100.6 10.6 %collective-permute-start.14 = (f32[2,496,128]{2,1,0:T(8,128)S(1)}, f32[2,496,128]{2,1,0:T(8,128)S(1)}, u32[]{:S(2)}, u32[]{:S(2)}) collective-permute-start(f32[2,496,128]{2,1,0:T(8,128)S(1)} %collective-permute-done.12.refs_0_), channel_id=1, source_target_pairs={{0,16},{8,56},{16,32},{24,8},{32,48},{40,24},{48,0},{56,40},{1,17}... | collective-permute-start | bytes 1523720 | tf_op jit(solution)/shard_map/ppermute | solution.py:486
  105.8 10.9 %collective-permute-start.16 = (f32[2,496,128]{2,1,0:T(8,128)S(1)}, f32[2,496,128]{2,1,0:T(8,128)S(1)}, u32[]{:S(2)}, u32[]{:S(2)}) collective-permute-start(f32[2,496,128]{2,1,0:T(8,128)S(1)} %collective-permute-done.15.refs_1_), channel_id=1, source_target_pairs={{0,16},{8,56},{16,32},{24,8},{32,48},{40,24},{48,0},{56,40},{1,17}... | collective-permute-start | bytes 1523720 | tf_op jit(solution)/shard_map/ppermute | solution.py:486
  108.2 10.9 %collective-permute-start.18 = (f32[2,496,128]{2,1,0:T(8,128)S(1)}, f32[2,496,128]{2,1,0:T(8,128)S(1)}, u32[]{:S(2)}, u32[]{:S(2)}) collective-permute-start(f32[2,496,128]{2,1,0:T(8,128)S(1)} %collective-permute-done.12.refs_0_), channel_id=1, source_target_pairs={{0,8},{8,0},{1,9},{9,1},{2,10},{10,2},{3,11},{11,3},{4,12},{12,4},... | collective-permute-start | bytes 1523720 | tf_op jit(solution)/shard_map/ppermute | solution.py:483
  108.3 10.9 %collective-permute-start.19 = (f32[2,496,128]{2,1,0:T(8,128)S(1)}, f32[2,496,128]{2,1,0:T(8,128)S(1)}, u32[]{:S(2)}, u32[]{:S(2)}) collective-permute-start(f32[2,496,128]{2,1,0:T(8,128)S(1)} %collective-permute-done.15.refs_1_), channel_id=1, source_target_pairs={{0,8},{8,0},{1,9},{9,1},{2,10},{10,2},{3,11},{11,3},{4,12},{12,4},... | collective-permute-start | bytes 1523720 | tf_op jit(solution)/shard_map/ppermute | solution.py:483
  111.2 10.9 %collective-permute-start.17 = (f32[2,496,128]{2,1,0:T(8,128)S(1)}, f32[2,496,128]{2,1,0:T(8,128)S(1)}, u32[]{:S(2)}, u32[]{:S(2)}) collective-permute-start(f32[2,496,128]{2,1,0:T(8,128)S(1)} %collective-permute-done.14.refs_0_), channel_id=1, source_target_pairs={{0,16},{8,56},{16,32},{24,8},{32,48},{40,24},{48,0},{56,40},{1,17}... | collective-permute-start | bytes 1523720 | tf_op jit(solution)/shard_map/ppermute | solution.py:486
  116.6 10.9 %collective-permute-start.20 = (f32[2,496,128]{2,1,0:T(8,128)S(1)}, f32[2,496,128]{2,1,0:T(8,128)S(1)}, u32[]{:S(2)}, u32[]{:S(2)}) collective-permute-start(f32[2,496,128]{2,1,0:T(8,128)S(1)} %collective-permute-done.16.refs_1_), channel_id=1, source_target_pairs={{0,16},{8,56},{16,32},{24,8},{32,48},{40,24},{48,0},{56,40},{1,17}... | collective-permute-start | bytes 1523720 | tf_op jit(solution)/shard_map/ppermute | solution.py:486
  127.5 4.0 %collective-permute-start.23 = (f32[2,496,128]{2,1,0:T(8,128)S(1)}, f32[2,496,128]{2,1,0:T(8,128)S(1)}, u32[]{:S(2)}, u32[]{:S(2)}) collective-permute-start(f32[2,496,128]{2,1,0:T(8,128)S(1)} %collective-permute-done.14.refs_0_), channel_id=1, source_target_pairs={{0,8},{8,0},{1,9},{9,1},{2,10},{10,2},{3,11},{11,3},{4,12},{12,4},... | collective-permute-start | bytes 1523720 | tf_op jit(solution)/shard_map/ppermute | solution.py:483
  130.0 2.2 %collective-permute-start.24 = (f32[2,496,128]{2,1,0:T(8,128)S(1)}, f32[2,496,128]{2,1,0:T(8,128)S(1)}, u32[]{:S(2)}, u32[]{:S(2)}) collective-permute-start(f32[2,496,128]{2,1,0:T(8,128)S(1)} %collective-permute-done.16.refs_1_), channel_id=1, source_target_pairs={{0,8},{8,0},{1,9},{9,1},{2,10},{10,2},{3,11},{11,3},{4,12},{12,4},... | collective-permute-start | bytes 1523720 | tf_op jit(solution)/shard_map/ppermute | solution.py:483
  130.0 3.8 %collective-permute-start.21 = (f32[2,496,128]{2,1,0:T(8,128)S(1)}, f32[2,496,128]{2,1,0:T(8,128)S(1)}, u32[]{:S(2)}, u32[]{:S(2)}) collective-permute-start(f32[2,496,128]{2,1,0:T(8,128)S(1)} %collective-permute-done.17.refs_2_), channel_id=1, source_target_pairs={{0,8},{8,0},{1,9},{9,1},{2,10},{10,2},{3,11},{11,3},{4,12},{12,4},... | collective-permute-start | bytes 1523720 | tf_op jit(solution)/shard_map/ppermute | solution.py:483
  130.5 3.3 %collective-permute-start.22 = (f32[2,496,128]{2,1,0:T(8,128)S(1)}, f32[2,496,128]{2,1,0:T(8,128)S(1)}, u32[]{:S(2)}, u32[]{:S(2)}) collective-permute-start(f32[2,496,128]{2,1,0:T(8,128)S(1)} %collective-permute-done.20.refs_0_), channel_id=1, source_target_pairs={{0,8},{8,0},{1,9},{9,1},{2,10},{10,2},{3,11},{11,3},{4,12},{12,4},... | collective-permute-start | bytes 1523720 | tf_op jit(solution)/shard_map/ppermute | solution.py:483
